TPU v7x, 32 devices: a whole 2x2x4 slice. The times are simulated.
32 devices in a mesh: shard: 8 (over y, x, core), rep: 4 (over z).
Axes of the slice: x: 2, y: 2, z: 4, core: 2. Of those that a mesh axis runs over, the one named last changes fastest.
Arguments:
- tokens: bfloat16 [64, 128, 2048], P(('shard', 'rep')), may hold values from -6 to 6
- norm1_gain: bfloat16 [2048], P('shard'), may hold values from 0.5 to 1.5
- q_weight: bfloat16 [2048, 2048], P('shard'), may hold values from -0.125 to 0.125
- k_weight: bfloat16 [2048, 256], P('shard'), may hold values from -0.125 to 0.125
- v_weight: bfloat16 [2048, 256], P('shard'), may hold values from -0.125 to 0.125
- o_weight: bfloat16 [2048, 2048], P('shard'), may hold values from -0.5 to 0.5
- norm2_gain: bfloat16 [2048], P('shard'), may hold values from 0.5 to 1.5
- gate_weight: bfloat16 [2048, 5632], P('shard'), may hold values from -0.125 to 0.125
- up_weight: bfloat16 [2048, 5632], P('shard'), may hold values from -0.125 to 0.125
- down_weight: bfloat16 [5632, 2048], P('shard'), may hold values from -0.15625 to 0.15625
- out_grad: bfloat16 [64, 128, 2048], P(('shard', 'rep')), may hold values from -6 to 6
Outputs:
- layer_out: bfloat16 [64, 128, 2048], P(('shard', 'rep'))
- input_grad: float32 [64, 128, 2048], P(('shard', 'rep'))
- norm1_gain_grad: float32 [2048], P('shard')
- q_grad: float32 [2048, 2048], P('shard')
- k_grad: float32 [2048, 256], P('shard')
- v_grad: float32 [2048, 256], P('shard')
- o_grad: float32 [2048, 2048], P('shard')
- norm2_gain_grad: float32 [2048], P('shard')
- gate_grad: float32 [2048, 5632], P('shard')
- up_grad: float32 [2048, 5632], P('shard')
- down_grad: float32 [5632, 2048], P('shard')
All inputs are finite; a program needn't handle non-finite values.
Results may differ from a plain program's by a relative error of at most 0.022.
Values may be sent and summed in bfloat16 or wider, within the bound.
No kernel may reach another device: no remote copies, remote signals or barrier semaphores. Data moves between devices by JAX's collectives and lax.ppermute only.
A program may use at most 384 MiB of HBM per device.

v0:
```python
import math

import jax
import jax.numpy as jnp
from jax import lax
from jax.sharding import PartitionSpec as P

QUERY_HEADS = 32
KEY_VALUE_HEADS = 4
HEAD_SIZE = 64
KV = 256


EPS = 1e-05


def rope_tables(sequence_length, size):
    half = size // 2
    freqs = 1.0 / 10000.0 ** (jnp.arange(half, dtype=jnp.float32) * 2.0 / size)
    angles = jnp.arange(sequence_length, dtype=jnp.float32)[:, None] * freqs[None, :]
    return (jnp.concatenate([jnp.cos(angles)] * 2, -1), jnp.concatenate([jnp.sin(angles)] * 2, -1))


def apply_rotation(value, cosine_table, sine_table):
    half = value.shape[-1] // 2
    turned = jnp.concatenate([-value[..., half:], value[..., :half]], -1)
    return value * cosine_table[None, :, None, :] + turned * sine_table[None, :, None, :]


def rotate_back(grad, cosine_table, sine_table):
    half = grad.shape[-1] // 2
    moved = grad * sine_table[None, :, None, :]
    return grad * cosine_table[None, :, None, :] + jnp.concatenate(
        [moved[..., half:], -moved[..., :half]], -1
    )


def matrix_product(left, right):
    return jnp.dot(left, right, preferred_element_type=jnp.float32)


def across(left, right):
    return lax.dot_general(
        left, right, (((0,), (0,)), ((), ())), preferred_element_type=jnp.float32
    )


def compared_with(left, right):
    return lax.dot_general(
        left, right, (((1,), (1,)), ((), ())), preferred_element_type=jnp.float32
    )


def norm_back(grad_normed, source, inverse, gain):
    scaled = grad_normed * gain.astype(jnp.float32)
    gain_grad = jnp.sum(grad_normed * source * inverse, 0)
    source_grad = inverse * scaled - source * inverse**3 * jnp.mean(
        scaled * source, -1, keepdims=True
    )
    return (gain_grad, source_grad)


def on_device(
    tokens,
    norm1_gain,
    q_weight,
    k_weight,
    v_weight,
    o_weight,
    norm2_gain,
    gate_weight,
    up_weight,
    down_weight,
    out_grad,
):
    local_sequences, sequence_length, width = tokens.shape
    rows = local_sequences * sequence_length
    repeat_heads = QUERY_HEADS // KEY_VALUE_HEADS
    scale = 1.0 / math.sqrt(HEAD_SIZE)
    cosine_table, sine_table = rope_tables(sequence_length, HEAD_SIZE)
    causal = jnp.arange(sequence_length)[:, None] >= jnp.arange(sequence_length)[None, :]
    attn_set = (
        lax.all_gather(norm1_gain, "shard", axis=0, tiled=True),
        lax.all_gather(q_weight, "shard", axis=0, tiled=True),
        lax.all_gather(k_weight, "shard", axis=0, tiled=True),
        lax.all_gather(v_weight, "shard", axis=0, tiled=True),
        lax.all_gather(o_weight, "shard", axis=0, tiled=True),
    )
    gain_one, wq_full, key_weight_whole, value_weight_whole, output_weight_whole = attn_set
    inputs = tokens.reshape(rows, width).astype(jnp.float32)
    inv_one = lax.rsqrt(jnp.mean(inputs * inputs, -1, keepdims=True) + EPS)
    first_normed = (inputs * inv_one * gain_one.astype(jnp.float32)).astype(jnp.bfloat16)
    proj_query = matrix_product(first_normed, wq_full).reshape(
        local_sequences, sequence_length, QUERY_HEADS, HEAD_SIZE
    )
    projected_key = matrix_product(first_normed, key_weight_whole).reshape(
        local_sequences, sequence_length, KEY_VALUE_HEADS, HEAD_SIZE
    )
    value_reduced = (
        matrix_product(first_normed, value_weight_whole)
        .astype(jnp.bfloat16)
        .reshape(local_sequences, sequence_length, KEY_VALUE_HEADS, HEAD_SIZE)
    )
    query_rotated = (
        apply_rotation(proj_query, cosine_table, sine_table)
        .astype(jnp.bfloat16)
        .reshape(local_sequences, sequence_length, KEY_VALUE_HEADS, repeat_heads, HEAD_SIZE)
    )
    key_rot = apply_rotation(projected_key, cosine_table, sine_table).astype(jnp.bfloat16)

    def attend_scores():
        raw = (
            jnp.einsum(
                "stkrh,sukh->skrtu", query_rotated, key_rot, preferred_element_type=jnp.float32
            )
            * scale
        )
        return jnp.where(causal, raw, -1e30)

    scores = attend_scores()
    top_score = jnp.max(scores, -1, keepdims=True)
    total_exp = jnp.sum(jnp.exp(scores - top_score), -1, keepdims=True)
    log_total = top_score + jnp.log(total_exp)
    prob_low = jnp.exp(scores - log_total).astype(jnp.bfloat16)
    context = jnp.einsum(
        "skrtu,sukh->stkrh", prob_low, value_reduced, preferred_element_type=jnp.float32
    )
    context_low = context.reshape(rows, QUERY_HEADS * HEAD_SIZE).astype(jnp.bfloat16)
    hidden_one = inputs + matrix_product(context_low, output_weight_whole)
    mlp_set = (
        lax.all_gather(norm2_gain, "shard", axis=0, tiled=True),
        lax.all_gather(gate_weight, "shard", axis=0, tiled=True),
        lax.all_gather(up_weight, "shard", axis=0, tiled=True),
        lax.all_gather(down_weight, "shard", axis=0, tiled=True),
    )
    gain_two, wg_full, wu_full, wd_full = mlp_set
    inv_two = lax.rsqrt(jnp.mean(hidden_one * hidden_one, -1, keepdims=True) + EPS)
    normed_two = (hidden_one * inv_two * gain_two.astype(jnp.float32)).astype(jnp.bfloat16)
    gate_act = matrix_product(normed_two, wg_full)
    up_act = matrix_product(normed_two, wu_full)
    sigma = jax.nn.sigmoid(gate_act)
    silu_val = gate_act * sigma
    hidden_low = (silu_val * up_act).astype(jnp.bfloat16)
    layer_out = (
        (hidden_one + matrix_product(hidden_low, wd_full))
        .astype(jnp.bfloat16)
        .reshape(local_sequences, sequence_length, width)
    )
    gain_two, wg_full, wu_full, wd_full = (
        lax.all_gather(norm2_gain, "shard", axis=0, tiled=True),
        lax.all_gather(gate_weight, "shard", axis=0, tiled=True),
        lax.all_gather(up_weight, "shard", axis=0, tiled=True),
        lax.all_gather(down_weight, "shard", axis=0, tiled=True),
    )
    upstream = out_grad.reshape(rows, width).astype(jnp.float32)
    upstream_low = upstream.astype(jnp.bfloat16)
    grad_down = across(hidden_low, upstream_low)
    down_owned = lax.psum_scatter(
        grad_down.astype(jnp.bfloat16), "shard", scatter_dimension=0, tiled=True
    ).astype(jnp.float32)
    grad_hidden = compared_with(upstream_low, wd_full)
    grad_gate = (grad_hidden * up_act * (sigma * (1.0 + gate_act * (1.0 - sigma)))).astype(
        jnp.bfloat16
    )
    grad_up = (grad_hidden * silu_val).astype(jnp.bfloat16)
    grad_normed_two = compared_with(grad_gate, wg_full) + compared_with(grad_up, wu_full)
    grad_gain_two, grad_hidden_one = norm_back(grad_normed_two, hidden_one, inv_two, gain_two)
    grad_hidden_one = upstream + grad_hidden_one
    grad_wg = across(normed_two, grad_gate)
    gain_two_owned, gate_owned = (
        lax.psum_scatter(
            grad_gain_two.astype(jnp.bfloat16), "shard", scatter_dimension=0, tiled=True
        ).astype(jnp.float32),
        lax.psum_scatter(
            grad_wg.astype(jnp.bfloat16), "shard", scatter_dimension=0, tiled=True
        ).astype(jnp.float32),
    )
    grad_wu = across(normed_two, grad_up)
    up_owned = lax.psum_scatter(
        grad_wu.astype(jnp.bfloat16), "shard", scatter_dimension=0, tiled=True
    ).astype(jnp.float32)
    mlp_owned = (gain_two_owned, gate_owned, up_owned, down_owned)
    gain_one, wq_full, key_weight_whole, value_weight_whole, output_weight_whole = (
        lax.all_gather(norm1_gain, "shard", axis=0, tiled=True),
        lax.all_gather(q_weight, "shard", axis=0, tiled=True),
        lax.all_gather(k_weight, "shard", axis=0, tiled=True),
        lax.all_gather(v_weight, "shard", axis=0, tiled=True),
        lax.all_gather(o_weight, "shard", axis=0, tiled=True),
    )
    attention_reduced = grad_hidden_one.astype(jnp.bfloat16)
    grad_wo = across(context_low, attention_reduced)
    grad_context = (
        compared_with(attention_reduced, output_weight_whole)
        .astype(jnp.bfloat16)
        .reshape(local_sequences, sequence_length, KEY_VALUE_HEADS, repeat_heads, HEAD_SIZE)
    )
    attn_prob = jnp.exp(attend_scores() - log_total)
    prob_again = attn_prob.astype(jnp.bfloat16)
    grad_prob = jnp.einsum(
        "stkrh,sukh->skrtu", grad_context, value_reduced, preferred_element_type=jnp.float32
    )
    grad_value = jnp.einsum(
        "skrtu,stkrh->sukh", prob_again, grad_context, preferred_element_type=jnp.float32
    )
    grad_value = grad_value.astype(jnp.bfloat16).reshape(rows, KV)
    grad_scores = (
        attn_prob * (grad_prob - jnp.sum(attn_prob * grad_prob, -1, keepdims=True))
    ).astype(jnp.bfloat16)
    grad_query = (
        jnp.einsum("skrtu,sukh->stkrh", grad_scores, key_rot, preferred_element_type=jnp.float32)
        * scale
    )
    grad_query = rotate_back(
        grad_query.reshape(local_sequences, sequence_length, QUERY_HEADS, HEAD_SIZE),
        cosine_table,
        sine_table,
    )
    grad_query = grad_query.astype(jnp.bfloat16).reshape(rows, QUERY_HEADS * HEAD_SIZE)
    grad_key = (
        jnp.einsum(
            "skrtu,stkrh->sukh", grad_scores, query_rotated, preferred_element_type=jnp.float32
        )
        * scale
    )
    grad_key = (
        rotate_back(grad_key, cosine_table, sine_table).astype(jnp.bfloat16).reshape(rows, KV)
    )
    grad_wq = across(first_normed, grad_query)
    grad_wk = across(first_normed, grad_key)
    grad_wv = across(first_normed, grad_value)
    grad_normed_one = (
        compared_with(grad_query, wq_full)
        + compared_with(grad_key, key_weight_whole)
        + compared_with(grad_value, value_weight_whole)
    )
    grad_gain_one, grad_inputs = norm_back(grad_normed_one, inputs, inv_one, gain_one)
    input_grad = (grad_hidden_one + grad_inputs).reshape(local_sequences, sequence_length, width)
    attn_owned = (
        lax.psum_scatter(
            grad_gain_one.astype(jnp.bfloat16), "shard", scatter_dimension=0, tiled=True
        ).astype(jnp.float32),
        lax.psum_scatter(
            grad_wq.astype(jnp.bfloat16), "shard", scatter_dimension=0, tiled=True
        ).astype(jnp.float32),
        lax.psum_scatter(
            grad_wk.astype(jnp.bfloat16), "shard", scatter_dimension=0, tiled=True
        ).astype(jnp.float32),
        lax.psum_scatter(
            grad_wv.astype(jnp.bfloat16), "shard", scatter_dimension=0, tiled=True
        ).astype(jnp.float32),
        lax.psum_scatter(
            grad_wo.astype(jnp.bfloat16), "shard", scatter_dimension=0, tiled=True
        ).astype(jnp.float32),
    )
    summed = (
        lax.psum(attn_owned[0].astype(jnp.bfloat16), "rep").astype(jnp.float32),
        lax.psum(attn_owned[1].astype(jnp.bfloat16), "rep").astype(jnp.float32),
        lax.psum(attn_owned[2].astype(jnp.bfloat16), "rep").astype(jnp.float32),
        lax.psum(attn_owned[3].astype(jnp.bfloat16), "rep").astype(jnp.float32),
        lax.psum(attn_owned[4].astype(jnp.bfloat16), "rep").astype(jnp.float32),
        lax.psum(mlp_owned[0].astype(jnp.bfloat16), "rep").astype(jnp.float32),
        lax.psum(mlp_owned[1].astype(jnp.bfloat16), "rep").astype(jnp.float32),
        lax.psum(mlp_owned[2].astype(jnp.bfloat16), "rep").astype(jnp.float32),
        lax.psum(mlp_owned[3].astype(jnp.bfloat16), "rep").astype(jnp.float32),
    )
    return (
        layer_out,
        input_grad,
        summed[0],
        summed[1],
        summed[2],
        summed[3],
        summed[4],
        summed[5],
        summed[6],
        summed[7],
        summed[8],
    )


def solution(mesh):
    return jax.shard_map(
        on_device,
        mesh=mesh,
        in_specs=(
            P(("shard", "rep"), None, None),
            P("shard"),
            P("shard", None),
            P("shard", None),
            P("shard", None),
            P("shard", None),
            P("shard"),
            P("shard", None),
            P("shard", None),
            P("shard", None),
            P(("shard", "rep"), None, None),
        ),
        out_specs=(
            P(("shard", "rep"), None, None),
            P(("shard", "rep"), None, None),
            P("shard"),
            P("shard", None),
            P("shard", None),
            P("shard", None),
            P("shard", None),
            P("shard"),
            P("shard", None),
            P("shard", None),
            P("shard", None),
        ),
        check_vma=False,
    )
```

profile of v0, /device:TPU:0, one launch (start us, length us, event | category | flops | bytes accessed | tf_op | source)
XLA Modules:
  0.0 1687.2 jit_solution(1169092698932434224)
XLA Ops:
  12.0 10.3 all-gather
  22.4 8.9 all-gather.1
  33.6 2.5 all-gather.10.cloned.1.call-done
  36.1 1.7 convolution_convert_fusion.9
  38.0 23.6 %all-gather.12.cloned.1.call-done = bf16[2048,256]{1,0:T(8,128)(2,1)} async-done(((bf16[256,256]{1,0:T(8,128)(2,1)}), bf16[2048,256]{1,0:T(8,128)(2,1)}) %all-gather.12.cloned.1.call-update) | async-done | bytes 1048592 | tf_op jit(solution)/shard_map/all_gather | solution.py:85
  61.5 1.6 copy.52
  63.7 54.1 %all-gather.14.cloned.1.call-done = bf16[2048,2048]{1,0:T(8,128)(2,1)} async-done(((bf16[256,2048]{1,0:T(8,128)(2,1)}), bf16[2048,2048]{1,0:T(8,128)(2,1)}) %all-gather.14.cloned.1.call-update) | async-done | bytes 8388624 | tf_op jit(solution)/shard_map/all_gather | solution.py:84
  117.8 12.4 copy.53
  130.3 4.9 fusion.30
  136.7 1.2 exponential_reduce_fusion
  138.0 1.2 fusion.21
  139.2 1.1 copy.56
  140.3 33.7 %all-gather.16.cloned.1.call-done = bf16[2048,2048]{1,0:T(8,128)(2,1)} async-done(((bf16[256,2048]{1,0:T(8,128)(2,1)}), bf16[2048,2048]{1,0:T(8,128)(2,1)}) %all-gather.16.cloned.1.call-update) | async-done | bytes 8388624 | tf_op jit(solution)/shard_map/all_gather | solution.py:87
  174.0 5.8 multiply_reduce_fusion.2
  179.9 1.3 copy-done.4
  181.5 110.8 %all-gather.18.cloned.1.call-done = bf16[2048,5632]{1,0:T(8,128)(2,1)} async-done(((bf16[256,5632]{1,0:T(8,128)(2,1)}), bf16[2048,5632]{1,0:T(8,128)(2,1)}) %all-gather.18.cloned.1.call-update) | async-done | bytes 23068688 | tf_op jit(solution)/shard_map/all_gather | solution.py:132
  292.2 13.5 fusion.64
  305.7 104.7 %all-gather.20.cloned.1.call-done = bf16[2048,5632]{1,0:T(8,128)(2,1)} async-done(((bf16[256,5632]{1,0:T(8,128)(2,1)}), bf16[2048,5632]{1,0:T(8,128)(2,1)}) %all-gather.20.cloned.1.call-update) | async-done | bytes 23068688 | tf_op jit(solution)/shard_map/all_gather | solution.py:133
  410.5 13.7 fusion.65
  424.2 104.7 %all-gather.22.cloned.1.call-done = bf16[5632,2048]{1,0:T(8,128)(2,1)} async-done(((bf16[704,2048]{1,0:T(8,128)(2,1)}), bf16[5632,2048]{1,0:T(8,128)(2,1)}) %all-gather.22.cloned.1.call-update) | async-done | bytes 23068688 | tf_op jit(solution)/shard_map/all_gather | solution.py:134
  528.9 25.6 %multiply_convert_fusion = (bf16[256,5632]{1,0:T(8,128)(2,1)}, bf16[256,5632]{1,0:T(8,128)(2,1)}, bf16[256,5632]{1,0:T(8,128)(2,1)}) fusion(f32[256,5632]{1,0:T(8,128)} %fusion.64, f32[256,5632]{1,0:T(8,128)} %fusion.65, bf16[256,2048]{1,0:T(8,128)(2,1)S(1)} %bitcast.216, bf16[5632,2048]{1,0:T(8,128)(2,1)} %all-gather.22.cloned.1.call-done), kind=kOutput, calls=%fused_computation.5 | convolution fusion | flops 5927206912 | bytes 44302336 | tf_op jit(solution)/shard_map/dot_general | solution.py:49
  554.4 12.7 fusion.66
  567.1 14.3 multiply_reduce_fusion
  581.4 2.5 subtract_add_fusion
  583.9 1.3 copy-done.8
  585.2 6.7 convolution_convert_fusion.7
  592.0 3.3 reshape.225
  595.3 2.9 copy.59
  598.2 3.9 fusion.1
  602.2 1.5 fusion.3
  603.8 1.3 copy-done.7
  606.1 1.5 convolution_convert_fusion.6
  607.7 3.3 fusion.23
  611.1 1.5 convolution_convert_fusion.5
  612.8 2.0 convolution_multiply_fusion
  616.6 1.8 add_convert_fusion
  619.5 5.7 convolution_convert_fusion.4
  625.3 1.1 copy-done.11
  626.4 7.2 convolution_convert_fusion.3
  633.7 1.2 copy-done.13
  634.8 12.7 convolution_convert_fusion.2
  647.8 12.9 convolution_convert_fusion.1
  660.8 1.1 copy-done.18
  662.0 12.9 convolution_convert_fusion
  675.2 8.4 reduce-scatter.12.cloned.1.call-done
  683.6 74.6 %reduce-scatter.8.cloned.1.call-done = bf16[256,2048]{1,0:T(8,128)(2,1)} async-done(((bf16[2048,2048]{1,0:T(8,128)(2,1)}), bf16[256,2048]{1,0:T(8,128)(2,1)}) %reduce-scatter.8.cloned.1.call-update) | async-done | bytes 1048592 | tf_op jit(solution)/shard_map/reduce_scatter | solution.py:242
  758.2 75.2 %reduce-scatter.14.cloned.1.call-done = bf16[256,2048]{1,0:T(8,128)(2,1)} async-done(((bf16[2048,2048]{1,0:T(8,128)(2,1)}), bf16[256,2048]{1,0:T(8,128)(2,1)}) %reduce-scatter.14.cloned.1.call-update) | async-done | bytes 1048592 | tf_op jit(solution)/shard_map/reduce_scatter | solution.py:251
  833.4 149.4 %reduce-scatter.16.cloned.1.call-done = bf16[256,5632]{1,0:T(8,128)(2,1)} async-done(((bf16[2048,5632]{1,0:T(8,128)(2,1)}), bf16[256,5632]{1,0:T(8,128)(2,1)}) %reduce-scatter.16.cloned.1.call-update) | async-done | bytes 2883600 | tf_op jit(solution)/shard_map/reduce_scatter | solution.py:174
  982.8 149.5 %reduce-scatter.18.cloned.1.call-done = bf16[256,5632]{1,0:T(8,128)(2,1)} async-done(((bf16[2048,5632]{1,0:T(8,128)(2,1)}), bf16[256,5632]{1,0:T(8,128)(2,1)}) %reduce-scatter.18.cloned.1.call-update) | async-done | bytes 2883600 | tf_op jit(solution)/shard_map/reduce_scatter | solution.py:179
  1132.3 149.4 %reduce-scatter.20.cloned.1.call-done = bf16[704,2048]{1,0:T(8,128)(2,1)} async-done(((bf16[5632,2048]{1,0:T(8,128)(2,1)}), bf16[704,2048]{1,0:T(8,128)(2,1)}) %reduce-scatter.20.cloned.1.call-update) | async-done | bytes 2883600 | tf_op jit(solution)/shard_map/reduce_scatter | solution.py:158
  1283.6 3.3 copy.63
  1286.9 1.7 copy.61
  1289.6 7.0 fusion.24
  1298.1 2.2 fusion.20
  1300.4 13.7 all-reduce.2
  1314.2 12.9 all-reduce.3
  1328.2 3.7 fusion.17
  1332.0 12.1 fusion.5
  1344.1 320.6 %all-reduce.7.cloned.1.call-done = (bf16[256,2048]{1,0:T(8,128)(2,1)}, bf16[256,256]{1,0:T(8,128)(2,1)}, bf16[256,256]{1,0:T(8,128)(2,1)}, bf16[256,2048]{1,0:T(...) async-done(((bf16[256,2048]{1,0:T(8,128)(2,1)}, bf16[256,256]{1,0:T(8,128)(2,1)}, bf16[256,256]{1,0:T(8,128)(2,1)}, ...) | async-done | bytes 11010064 | tf_op jit(solution)/shard_map/psum | solution.py:257
  1664.7 2.9 convert_element_type.213
  1669.1 1.6 convert_element_type.219
  1670.6 3.2 convert_element_type.223
  1673.8 3.2 convert_element_type.225
  1677.0 3.3 convert_element_type.227
  (158 shorter events, 21.0 us)
Async XLA Ops:
  7.2 28.9 %all-gather.10.cloned.1.call-start = ((), (), s32[]{:S(2)}) async-start(), calls=%async_computation.7 | async-start | bytes 1179648 | tf_op jit(solution)/shard_map/all_gather | solution.py:86
  7.9 53.6 %all-gather.12.cloned.1.call-start = ((), (), s32[]{:S(2)}) async-start(), calls=%async_computation.8 | async-start | bytes 1179648 | tf_op jit(solution)/shard_map/all_gather | solution.py:85
  8.7 109.2 %all-gather.14.cloned.1.call-start = ((), (), s32[]{:S(2)}) async-start(), calls=%async_computation.9 | async-start | bytes 9437184 | tf_op jit(solution)/shard_map/all_gather | solution.py:84
  9.4 164.6 %all-gather.16.cloned.1.call-start = ((), (), s32[]{:S(2)}) async-start(), calls=%async_computation.10 | async-start | bytes 9437184 | tf_op jit(solution)/shard_map/all_gather | solution.py:87
  10.0 282.3 %all-gather.18.cloned.1.call-start = ((), (), s32[]{:S(2)}) async-start(), calls=%async_computation.11 | async-start | bytes 25952256 | tf_op jit(solution)/shard_map/all_gather | solution.py:132
  10.6 1.4 copy-start.42
  10.6 11.8 copy-start.43
  10.6 22.1 %copy-start.2 = (bf16[2,128,2048]{2,1,0:T(8,128)(2,1)S(1)}, bf16[2,128,2048]{2,1,0:T(8,128)(2,1)}, u32[]{:S(2)}) copy-start(bf16[2,128,2048]{2,1,0:T(8,128)(2,1)} %param.11) | copy-start | bytes 3145732
  10.6 399.9 %all-gather.20.cloned.1.call-start = ((), (), s32[]{:S(2)}) async-start(), calls=%async_computation.12 | async-start | bytes 25952256 | tf_op jit(solution)/shard_map/all_gather | solution.py:133
  11.2 517.7 %all-gather.22.cloned.1.call-start = ((), (), s32[]{:S(2)}) async-start(), calls=%async_computation.13 | async-start | bytes 25952256 | tf_op jit(solution)/shard_map/all_gather | solution.py:134
  11.9 663.3 %reduce-scatter.10.cloned.1.call-start = ((), (), s32[]{:S(2)}) async-start(), calls=%async_computation.15 | async-start | bytes 1179648 | tf_op jit(solution)/shard_map/reduce_scatter | solution.py:245
  22.4 15.4 copy-start.31
  32.7 102.8 %copy-start.26 = (f32[128,64]{0,1:T(8,128)}, f32[128,64]{0,1:T(8,128)S(1)}, u32[]{:S(2)}) copy-start(f32[128,64]{0,1:T(8,128)S(1)} %get-tuple-element.59) | copy-start | bytes 98308
  32.7 102.8 %copy-start.28 = (f32[128,64]{0,1:T(8,128)}, f32[128,64]{0,1:T(8,128)S(1)}, u32[]{:S(2)}) copy-start(f32[128,64]{0,1:T(8,128)S(1)} %get-tuple-element.42) | copy-start | bytes 98308
  33.0 4.8 copy-start.39
  33.0 4.8 copy-start.37
  136.0 2.0 copy-start.14
  136.7 2.4 copy-start
  138.0 464.2 %copy-start.29 = (f32[2,4,8,128]{3,2,1,0:T(8,128)}, f32[2,4,8,128]{3,2,1,0:T(8,128)S(1)}, u32[]{:S(2)}) copy-start(f32[2,4,8,128]{3,2,1,0:T(8,128)S(1)} %log_add_fusion) | copy-start | bytes 98308
  140.3 39.6 %copy-start.10 = (bf16[2,128,4,8,64]{1,0,4,3,2:T(2,128)(2,1)}, bf16[2,128,4,8,64]{1,0,4,3,2:T(2,128)(2,1)S(1)}, u32[]{:S(2)}) copy-start(bf16[2,128,4,8,64]{1,0,4,3,2:T(2,128)(2,1)S(1)} %copy.56) | copy-start | bytes 3145732
  174.0 7.2 copy-start.36
  179.9 1.3 copy-start.4
  181.4 229.0 %copy-start.12 = (bf16[256,2048]{1,0:T(8,128)(2,1)}, bf16[256,2048]{1,0:T(8,128)(2,1)S(1)}, u32[]{:S(2)}) copy-start(bf16[256,2048]{1,0:T(8,128)(2,1)S(1)} %multiply_convert_fusion.3) | copy-start | bytes 3145732
  305.7 223.1 %copy-start.17 = (bf16[2,128,2048]{2,1,0:T(8,128)(2,1)S(1)}, bf16[2,128,2048]{2,1,0:T(8,128)(2,1)}, u32[]{:S(2)}) copy-start(bf16[2,128,2048]{2,1,0:T(8,128)(2,1)} %param.21) | copy-start | bytes 3145732
  554.4 12.7 copy-start.5
  583.9 1.3 copy-start.8
  598.2 3.9 copy-start.1
  602.2 2.9 copy-start.15
  603.7 1.3 copy-start.7
  603.7 2.2 copy-start.35
  605.9 1.8 copy-start.19
  605.9 1.8 copy-start.30
  607.6 76.0 %reduce-scatter.12.cloned.1.call-start = ((), (), s32[]{:S(2)}) async-start(), calls=%async_computation.16 | async-start | bytes 1179648 | tf_op jit(solution)/shard_map/reduce_scatter | solution.py:248
  612.6 145.6 %reduce-scatter.8.cloned.1.call-start = ((), (), s32[]{:S(2)}) async-start(), calls=%async_computation.14 | async-start | bytes 9437184 | tf_op jit(solution)/shard_map/reduce_scatter | solution.py:242
  615.9 0.8 copy-start.27
  625.2 1.2 copy-start.11
  625.2 208.2 %reduce-scatter.14.cloned.1.call-start = ((), (), s32[]{:S(2)}) async-start(), calls=%async_computation.17 | async-start | bytes 9437184 | tf_op jit(solution)/shard_map/reduce_scatter | solution.py:251
  633.6 1.2 copy-start.13
  633.6 349.1 %reduce-scatter.16.cloned.1.call-start = ((), (), s32[]{:S(2)}) async-start(), calls=%async_computation.18 | async-start | bytes 25952256 | tf_op jit(solution)/shard_map/reduce_scatter | solution.py:174
  647.5 484.8 %reduce-scatter.18.cloned.1.call-start = ((), (), s32[]{:S(2)}) async-start(), calls=%async_computation.19 | async-start | bytes 25952256 | tf_op jit(solution)/shard_map/reduce_scatter | solution.py:179
  660.7 1.2 copy-start.18
  660.8 621.0 %reduce-scatter.20.cloned.1.call-start = ((), (), s32[]{:S(2)}) async-start(), calls=%async_computation.20 | async-start | bytes 25952256 | tf_op jit(solution)/shard_map/reduce_scatter | solution.py:158
  674.9 989.8 %all-reduce.7.cloned.1.call-start = ((), (), s32[]{:S(2)}) async-start(), calls=%async_computation.21 | async-start | bytes 22020096 | tf_op jit(solution)/shard_map/psum | solution.py:257
  1281.7 0.7 copy-start.44
  1281.7 1.9 copy-start.40
  1289.5 7.0 copy-start.21
  1296.6 1.2 copy-start.3
  1296.6 1.5 copy-start.20
  1296.6 1.5 copy-start.32
  1296.6 1.5 copy-start.38
  1298.1 2.2 copy-start.41
  1298.1 30.1 %copy-start.9 = (f32[256,2048]{1,0:T(8,128)S(1)}, f32[256,2048]{1,0:T(8,128)}, u32[]{:S(2)}) copy-start(f32[256,2048]{1,0:T(8,128)} %copy-done.8) | copy-start | bytes 6291460
  1328.2 3.7 copy-start.6
  1328.2 3.7 copy-start.16
  1664.7 2.9 copy-start.34
  1664.7 3.7 copy-start.33
  1664.7 4.4 copy-start.25
  1664.7 6.0 copy-start.24
  1670.6 3.2 copy-start.23
  1673.8 3.2 copy-start.22
Sparse Core Ops, SparseCore 0:
  9.9 26.1 all-gather.9
  38.0 23.4 all-gather.11
  63.4 54.3 all-gather.13
  119.6 54.3 all-gather.15
  175.7 116.4 all-gather.17
  294.0 116.4 all-gather.19
  412.4 116.4 all-gather.21
  607.7 36.0 reduce-scatter.9
  647.6 36.0 reduce-scatter.11
  686.9 71.2 reduce-scatter.7
  762.1 71.2 reduce-scatter.13
  836.8 145.8 reduce-scatter.15
  986.4 145.8 reduce-scatter.17
  1135.8 145.8 reduce-scatter.19
  1285.0 379.6 all-reduce.6
where the time goes:
time: 1690 us
  waiting for transfers between devices  1370 us (81%)
  matrix products  187 us (11%)
  blocking collectives  45.8 us (3%)
  local copies, waits for them, and re-layouts  39.2 us (2%)
  other arithmetic  32.2 us (2%)
    psum x1, waiting for transfers between devices, on_device(): lax.psum(attn_owned[1].astype(jnp.bfloat16), 'rep').astype(jnp.float32)  321 us
    reduce_scatter x1, waiting for transfers between devices, on_device(): lax.psum_scatter(grad_wu.astype(jnp.bfloat16), 'shard', scatter_dimension...  150 us
    reduce_scatter x1, waiting for transfers between devices, on_device(): lax.psum_scatter(grad_wg.astype(jnp.bfloat16), 'shard', scatter_dimension...  149 us
    reduce_scatter x1, waiting for transfers between devices, on_device(): lax.psum_scatter(grad_down.astype(jnp.bfloat16), 'shard', scatter_dimensi...  149 us
    all_gather x1, waiting for transfers between devices, on_device(): lax.all_gather(gate_weight, 'shard', axis=0, tiled=True)  111 us
    all_gather x1, waiting for transfers between devices, on_device(): lax.all_gather(up_weight, 'shard', axis=0, tiled=True)  105 us
    all_gather x1, waiting for transfers between devices, on_device(): lax.all_gather(down_weight, 'shard', axis=0, tiled=True)  105 us
    reduce_scatter x1, waiting for transfers between devices, on_device(): lax.psum_scatter(grad_wo.astype(jnp.bfloat16), 'shard', scatter_dimension...  75.2 us
  transfers between devices with their start and end apart: 15, of which 14 were waited for; matrix products, arithmetic and copies ran while one was open for 9% of the time, Pallas kernels for 0%

commit v1 on v0

v1 whole, which is shorter than its diff:
```python
import functools
import math

import jax
import jax.numpy as jnp
import numpy as np
from jax import lax
from jax.experimental import pallas as pl
from jax.experimental.pallas import tpu as pltpu
from jax.sharding import PartitionSpec as P

HEAD_SIZE = 64
EPS = 1e-05
F32 = jnp.float32
BF16 = jnp.bfloat16
ANY = pl.BlockSpec(memory_space=pl.ANY)
TOKEN = pl.BlockSpec(memory_space=pltpu.HBM)
PER_MIB = 1.4e10


def dot(left, right):
    return jnp.dot(left, right, preferred_element_type=F32)


def dot_nt(left, right):
    return lax.dot_general(left, right, (((1,), (1,)), ((), ())), preferred_element_type=F32)


def dot_tn(left, right):
    return lax.dot_general(left, right, (((0,), (0,)), ((), ())), preferred_element_type=F32)


def shape_of(rows, columns, dtype=BF16):
    return jax.ShapeDtypeStruct((rows, columns), dtype)


def row_blocks(rows, columns):
    return pl.BlockSpec((rows, columns), lambda i: (i, 0))


def row_block_at(rows, columns, at):
    return pl.BlockSpec((rows, columns), lambda i: (at, 0))


def column_blocks(rows, columns):
    return pl.BlockSpec((rows, columns), lambda i: (0, i))


def whole(array):
    zeros = (0,) * array.ndim
    return pl.BlockSpec(array.shape, lambda i: zeros, pipeline_mode=pl.Buffered(1))


def whole_out(array):
    zeros = (0,) * len(array.shape)
    return pl.BlockSpec(array.shape, lambda i: zeros)


class Clock:
    def __init__(self):
        self.token = jnp.zeros((8, 128), F32)

    def call(self, body, args, in_specs, outs, out_specs, steps=1, aliases=None, vmem=60, cost=1):
        n_in, n_out = len(args), len(outs)

        def kernel(*refs):
            body(*refs[:n_in], *refs[n_in + 1 : n_in + 1 + n_out])

        *results, self.token = pl.pallas_call(
            kernel,
            grid=(steps,),
            out_shape=(*outs, pltpu.HBM(self.token.shape, F32)),
            in_specs=[*in_specs, TOKEN],
            out_specs=(*out_specs, TOKEN),
            input_output_aliases={n_in: n_out, **(aliases or {})},
            compiler_params=pltpu.CompilerParams(vmem_limit_bytes=vmem << 20),
            cost_estimate=pl.CostEstimate(flops=cost, bytes_accessed=cost // 1000 + 1, transcendentals=0),
        )(*args, self.token)
        return results

    def pause(self, mib):
        self.call(nothing, [], [], [], [], vmem=1, cost=int(mib * PER_MIB))

    def tie(self, *values):
        outs = [jax.ShapeDtypeStruct(v.shape, v.dtype) for v in values]
        results = self.call(
            nothing, values, [ANY] * len(values), outs, [ANY] * len(values),
            aliases={i: i for i in range(len(values))}, vmem=1,
        )
        return results if len(results) > 1 else results[0]


def nothing(*refs):
    pass


class Line:
    def __init__(self, size, clock):
        self.size = size
        self.clock = clock
        self.me = lax.axis_index("rep")
        self.end = jnp.asarray((self.me == 0) | (self.me == size - 1), jnp.int32).reshape(1)
        self.waiting, self.coming, self.across, self.going = [], None, None, None

    def shift(self, value, pairs):
        return lax.ppermute(value, "rep", pairs)

    def queue(self, value, finish):
        if self.size == 4:
            self.waiting.append((value, finish))
        else:
            finish(lax.psum(value, "rep") if self.size > 1 else value)

    def busy(self):
        return bool(self.waiting or self.coming or self.across or self.going)

    def tick(self, mib=0.1):
        if not self.busy():
            return
        coming, across, going = self.coming, self.across, self.going
        fresh = self.waiting.pop(0) if self.waiting else None
        args, outs, jobs = [], [], []

        def use(*arrays):
            args.extend(arrays)
            return slice(len(args) - len(arrays), len(args))

        def give(array):
            outs.append(shape_of(*array.shape))
            return len(outs) - 1

        inward = [(0, 1), (3, 2)]
        outward = [(1, 0), (2, 3)]
        shared = across and fresh and across["value"].shape == fresh[0].shape
        if across:
            terms = [across["value"], across["arrived"]]
            if shared:
                jobs.append(("fresh", use(fresh[0], *terms), give(fresh[0])))
            else:
                jobs.append(("add", use(*terms), give(across["value"])))
        if coming:
            jobs.append(("add", use(coming["value"], coming["arrived"]), give(coming["value"])))

        if fresh and jobs and not shared:
            jobs.append(("pass", use(fresh[0]), give(fresh[0])))

        def body(end, *refs):
            ins, results = refs[: len(args)], refs[len(args) :]
            outer = end[0] > 0
            for kind, where, out in jobs:
                mine = [ref[...].astype(F32) for ref in ins[where]]
                if kind == "pass":
                    value = mine[0]
                elif kind == "add":
                    value = mine[0] + mine[1]
                else:
                    value = jnp.where(outer, mine[0], mine[1] + mine[2])
                results[out][...] = value.astype(BF16)

        results = []
        if jobs:
            steps = 2 if all(a.shape[0] % 32 == 0 for a in args) else 1
            specs = [row_blocks(a.shape[0] // steps, a.shape[1]) for a in args]
            results = self.clock.call(
                body, [self.end, *args], [pl.BlockSpec(memory_space=pltpu.SMEM), *specs],
                outs, [row_blocks(o.shape[0] // steps, o.shape[1]) for o in outs], steps, vmem=60,
            )
        results = list(results)
        self.going = self.across = self.coming = None
        if across:
            value = results.pop(0)
            arrived = self.shift(value, outward + (inward if shared else []))
            self.going = {"value": value, "arrived": arrived, "finish": across["finish"]}
        if coming:
            value = results.pop(0)
            self.across = {"value": value, "arrived": self.shift(value, [(1, 2), (2, 1)]), "finish": coming["finish"]}
        if fresh:
            value = fresh[0]
            if not shared:
                value = results.pop(0) if results else self.clock.tie(value)
                arrived = self.shift(value, inward)
            self.coming = {"value": value, "arrived": arrived, "finish": fresh[1]}
        self.clock.pause(mib)
        if going:
            going["finish"](self.select(going["arrived"], going["value"]))

    def select(self, ends, others):
        rows, width = others.shape

        def body(end, a, b, out):
            out[...] = jnp.where(end[0] > 0, a[...], b[...])

        spec = column_blocks(rows, width // 2)
        return self.clock.call(
            body, [self.end, ends, others], [pl.BlockSpec(memory_space=pltpu.SMEM), spec, spec],
            [shape_of(rows, width)], [spec], 2,
        )[0]


    def share(self, value):
        up, down = [value], [value]
        top = self.size - 1
        for step in range(top):
            pairs = [(i, i + 1) for i in range(step, top)]
            above = self.shift(up[-1], pairs)
            below = self.shift(down[-1], [(top - a, top - b) for a, b in pairs])
            self.clock.pause(0.1)
            yield
            above, below = self.clock.tie(above, below)
            up.append(above)
            down.append(below)
        self.shared = up, down


class Group:
    def __init__(self, size, clock):
        self.size = size
        self.clock = clock
        self.fast = size == 8
        self.me = jnp.asarray(lax.axis_index("shard"), jnp.int32).reshape(1)

    def swap(self, value, bit):
        return lax.ppermute(value, "shard", [(i, i ^ bit) for i in range(self.size)])

    def gather(self, own):
        half = own.shape[0] // 2
        if not self.fast:
            yield
            yield
            self.gather_all(own)
            return
        by_x, by_y = self.swap(own, 2), self.swap(own, 4)
        self.clock.pause(1)
        yield
        first, second = self.stacked([[[(by_x, 0)]], [[(by_y, 1)]]], half)
        first, second = self.swap(first, 4), self.swap(second, 2)
        self.clock.pause(0.6)
        yield
        self.join(own, [(by_x, 0), (by_x, 1), (by_y, 0), (by_y, 1), (first, 0), (second, 0)])

    def gather_all(self, own):
        every = lax.all_gather(own, "shard", axis=0, tiled=True)
        middle = every.shape[0] // 2
        self.gathered = every[:middle], every[middle:]

    def join(self, own, pieces):
        half, width = own.shape[0] // 2, own.shape[1]
        pieces = [(own, 0), (own, 1), *pieces]

        def body(*refs):
            for at, ref in enumerate(refs[:-1]):
                refs[-1][pl.ds(at * half, half), :] = ref[...]

        def columns(at):
            return pl.BlockSpec((half, width // 4), lambda i: (at, i))

        even = shape_of(half * self.size, width)
        even = self.clock.call(
            body, [array for array, _ in pieces], [columns(at) for _, at in pieces],
            [even], [column_blocks(even.shape[0], width // 4)], 4, vmem=24,
        )[0]
        self.gathered = even, self.swap(even, 1)
        self.clock.pause(4)

    def stacked(self, outs, rows):
        terms = [term for out in outs for block in out for term in block]
        width = terms[0][0].shape[1]

        def body(*refs):
            ins = iter(refs[: len(terms)])
            for out, ref in zip(outs, refs[len(terms) :]):
                for at, block in enumerate(out):
                    values = [next(ins)[...] for _ in block]
                    if len(values) > 1:
                        values = [sum(v.astype(F32) for v in values).astype(BF16)]
                    ref[pl.ds(at * rows, rows), :] = values[0]

        shapes = [shape_of(len(out) * rows, width) for out in outs]
        return self.clock.call(
            body, [array for array, _ in terms], [row_block_at(rows, width, at) for _, at in terms],
            shapes, [whole_out(o) for o in shapes], vmem=40,
        )

    def partner(self, odd):
        if not self.fast:
            return odd
        other = self.swap(odd, 1)
        self.clock.pause(4)
        return other

    def ride(self, own):
        if self.fast:
            self.riding = self.swap(own, 2), self.swap(own, 4)
            self.clock.pause(1)

    def scatter(self, sets, own=None):
        if not self.fast:
            yield
            yield
            both = [jnp.concatenate(pair, 0) for pair in sets]
            totals = [lax.psum_scatter(b, "shard", scatter_dimension=0, tiled=True) for b in both]
            self.terms = [[[(total, 0)], [(total, 1)]] for total in totals]
            if own is not None:
                self.gather_all(own)
            return
        rows = sets[0][0].shape[0] // 8
        rider = self.clock.tie(*self.riding) if own is not None else None

        def both(pair, at):
            return [(pair[0], at), (pair[1], at)]

        to_x = [both(pair, at) for pair in sets for at in (3, 7)]
        to_y = [both(pair, at) for pair in sets for at in (4, 6)]
        to_x, to_y = self.stacked([to_x, to_y], rows)
        by_x, by_y = self.swap(to_x, 2), self.swap(to_y, 4)
        self.clock.pause(len(sets))
        yield
        count = len(sets)
        to_x = [both(pair, 2) + [(by_y, 2 * i + 1)] for i, pair in enumerate(sets)]
        to_y = [both(pair, 5) + [(by_x, 2 * i + 1)] for i, pair in enumerate(sets)]
        if rider:
            to_x.append([(rider[1], 1)])
            to_y.append([(rider[0], 0)])
        to_x, to_y = self.stacked([to_x, to_y], rows)
        last_x, last_y = self.swap(to_x, 2), self.swap(to_y, 4)
        self.clock.pause(0.6 * len(sets) + 0.4 * bool(rider))
        yield
        self.terms = [
            [
                both(pair, 0) + [(by_y, 2 * i), (last_x, i)],
                both(pair, 1) + [(by_x, 2 * i), (last_y, i)],
            ]
            for i, pair in enumerate(sets)
        ]
        if rider:
            first = [(rider[0], 0), (rider[0], 1), (rider[1], 0), (rider[1], 1)]
            self.rider = own, [*first, (last_y, count), (last_x, count)]

    def join_rider(self):
        if self.fast:
            self.join(*self.rider)

    def finish_rows(self, body, terms, args, outs):
        flat = [array for half in terms for array, _ in half]
        rows = args[0].shape[0] // 2
        columns = flat[0].shape[1]
        specs = [row_block_at(rows, columns, at) for half in terms for _, at in half]
        count = len(terms[0])

        def kernel(*refs):
            sums, rest = refs[: len(flat)], refs[len(flat) :]
            for half in (0, 1):
                total = sum(ref[...].astype(F32) for ref in sums[half * count : (half + 1) * count])
                body(pl.ds(half * rows, rows), total, *rest)

        return self.clock.call(
            kernel, [*flat, *args], [*specs, *[whole(a) for a in args]], outs,
            [whole_out(o) for o in outs], vmem=40,
        )

    def exchange(self, load, args, a, b):
        smem = pl.BlockSpec(memory_space=pltpu.SMEM)
        specs = [smem, *[smem if v.ndim == 1 else whole(v) for v in args]]
        if not self.fast:

            def lay(me, *refs):
                for j in range(self.size):
                    refs[-1][j] = load(refs[:-1], j)

            every = jax.ShapeDtypeStruct((self.size, a, b), BF16)
            blocks = self.clock.call(lay, [self.me, *args], specs, [every], [whole_out(every)])[0]
            yield
            yield
            self.exchanged = lax.all_to_all(blocks, "shard", split_axis=0, concat_axis=0)
            return
        four, two = jax.ShapeDtypeStruct((4, a, b), BF16), jax.ShapeDtypeStruct((2, a, b), BF16)

        def pack(me, *refs):
            kept, sent = refs[-2:]
            for j in range(8):
                value = load(refs[:-2], j)
                k = me[0] ^ j

                @pl.when(k & 1 == 0)
                def _(value=value, k=k):
                    kept[k >> 1] = value

                @pl.when(k & 1 == 1)
                def _(value=value, k=k):
                    sent[k >> 1] = value

        kept, sent = self.clock.call(
            pack, [self.me, *args], specs, [four] * 2, [whole_out(four)] * 2, vmem=32
        )
        come = self.swap(sent, 1)
        mib = 8 * a * b / 2**20
        self.clock.pause(mib)
        yield

        def stack(kept, come, *outs):
            for i, out in enumerate(outs):
                out[0] = kept[i + 1]
                out[1] = come[i + 1]

        sends = self.clock.call(
            stack, [kept, come], [whole(kept), whole(come)], [two] * 3, [whole_out(two)] * 3, vmem=24
        )
        arrived = [self.swap(value, 2 * i + 2) for i, value in enumerate(sends)]
        self.clock.pause(mib / 2)
        yield

        def unpack(me, kept, come, *rest):
            out = rest[-1]
            out[me[0]] = kept[0]
            out[me[0] ^ 1] = come[0]
            for i, ref in enumerate(rest[:-1]):
                out[me[0] ^ (2 * i + 2)] = ref[0]
                out[me[0] ^ (2 * i + 3)] = ref[1]

        eight = jax.ShapeDtypeStruct((8, a, b), BF16)
        first = pl.BlockSpec((1, a, b), lambda i: (0, 0, 0))
        self.exchanged = self.clock.call(
            unpack, [self.me, kept, come, *arrived], [smem, first, first, *[whole(v) for v in arrived]],
            [eight], [whole_out(eight)], vmem=24,
        )[0]


def drain(steps):
    for _ in steps:
        pass


class Attention:
    def __init__(self, clock, length, qcols, wqkv, wo):
        self.clock, self.length, self.qcols = clock, length, qcols
        self.wqkv, self.wo = wqkv, wo
        self.heads = qcols // HEAD_SIZE
        self.width = qcols + 2 * HEAD_SIZE
        half = HEAD_SIZE // 2
        freqs = 1.0 / 10000.0 ** (np.arange(half, dtype=np.float32) * 2.0 / HEAD_SIZE)
        angles = np.arange(length, dtype=np.float32)[:, None] * freqs[None, :].astype(np.float32)
        turns = self.heads + 1
        low = np.arange(turns * HEAD_SIZE) % HEAD_SIZE < half
        cosine = np.tile(np.cos(angles), (1, 2 * turns))
        sine = np.tile(np.sin(angles), (1, 2 * turns))
        plain = np.zeros((length, HEAD_SIZE), np.float32)
        self.tables = tuple(
            jnp.asarray(np.concatenate(pair, 1), F32)
            for pair in (
                (cosine, plain + 1.0),
                (np.where(low, -sine, 0.0), plain),
                (np.where(low, 0.0, sine), plain),
            )
        )

    def roll(self, value, by):
        return pltpu.roll(value, by % value.shape[1], 1)

    def stack(self, value):
        head = lax.broadcasted_iota(jnp.int32, value.shape, 1) // HEAD_SIZE
        return jnp.concatenate([jnp.where(head == h, value, 0.0) for h in range(self.heads)], 0).astype(BF16)

    def unstack(self, value):
        head = lax.broadcasted_iota(jnp.int32, (self.length, self.qcols), 1) // HEAD_SIZE
        total = jnp.zeros((self.length, self.qcols), F32)
        for h in range(self.heads):
            total = jnp.where(head == h, value[h * self.length : (h + 1) * self.length], total)
        return total

    def repeated(self, value):
        first = lax.broadcasted_iota(jnp.int32, value.shape, 1) < HEAD_SIZE
        turned = self.roll(value, HEAD_SIZE)
        times = self.qcols // (2 * HEAD_SIZE)
        key = jnp.where(first, value, turned).astype(BF16)
        val = jnp.where(first, turned, value).astype(BF16)
        return jnp.concatenate([key] * times, 1), jnp.concatenate([val] * times, 1)

    def probabilities(self, stacked, keys):
        raw = dot_nt(stacked, keys) * (1.0 / math.sqrt(HEAD_SIZE))
        raw = raw.reshape(self.heads, self.length, self.length)
        at = lax.broadcasted_iota(jnp.int32, raw.shape, 1)
        seen = lax.broadcasted_iota(jnp.int32, raw.shape, 2) <= at
        scores = jnp.where(seen, raw, -1e30)
        e = jnp.exp(scores - jnp.max(scores, -1, keepdims=True))
        prob = e / jnp.sum(e, -1, keepdims=True)
        return prob.reshape(self.heads * self.length, self.length)

    def forward(self, tokens):
        rows, width = tokens.shape
        block, length, qcols = 2 * self.length, self.length, self.qcols

        def body(x, wqkv, wo, c, s1, s2, qkv_out, inv_out, context_t, partial_out):
            source = x[...].astype(F32)
            inv = lax.rsqrt(jnp.mean(source * source, -1, keepdims=True) + EPS)
            inv_out[...] = jnp.broadcast_to(inv, (block, 128))
            lin = dot(x[...], wqkv[...]) * inv
            contexts = []
            for at in range(0, block, length):
                v = lin[at : at + length]
                v = v * c[...] + self.roll(v, -32) * s1[...] + self.roll(v, 32) * s2[...]
                v = v.astype(BF16).astype(F32)
                qkv_out[pl.ds(at, length), :] = v.astype(BF16)
                keys, values = self.repeated(v[:, qcols:])
                prob = self.probabilities(self.stack(v[:, :qcols]), keys)
                context = self.unstack(dot(prob.astype(BF16), values))
                contexts.append(context.astype(BF16))
            context = jnp.concatenate(contexts, 0)
            context_t[...] = context.T
            partial_out[...] = dot(context, wo[...]).astype(BF16)

        args = (tokens, self.wqkv, self.wo, *self.tables)
        return self.clock.call(
            body, args, [row_blocks(block, width), *[whole(a) for a in args[1:]]],
            [shape_of(rows, self.width), shape_of(rows, 128, F32), shape_of(qcols, rows), shape_of(rows, width)],
            [
                row_blocks(block, self.width),
                row_blocks(block, 128),
                column_blocks(qcols, block),
                row_blocks(block, width),
            ],
            rows // block,
        )

    def backward(self, grad, qkv, inv):
        rows, width = grad.shape
        block, length, qcols = 2 * self.length, self.length, self.qcols
        scale = 1.0 / math.sqrt(HEAD_SIZE)

        def fold(value):
            folded = sum(value[:, i : i + 2 * HEAD_SIZE] for i in range(0, qcols, 2 * HEAD_SIZE))
            return folded + self.roll(folded, HEAD_SIZE)

        def body(d, qkv_in, inv_in, wqkv, wo, c, s1, s2, grad_t, partial_out):
            grads = []
            dcontext = dot_nt(d[...], wo[...]).astype(BF16).astype(F32)
            for at in range(0, block, length):
                v = qkv_in[pl.ds(at, length), :].astype(F32)
                keys, values = self.repeated(v[:, qcols:])
                stacked = self.stack(v[:, :qcols])
                prob = self.probabilities(stacked, keys)
                dstacked = self.stack(dcontext[at : at + length])
                dprob = dot_nt(dstacked, values)
                dvalue = fold(dot_tn(prob.astype(BF16), dstacked))
                ds = prob * (dprob - jnp.sum(prob * dprob, -1, keepdims=True))
                ds = ds.astype(BF16)
                dq = self.unstack(dot(ds, keys)) * scale
                dkey = fold(dot_tn(ds, stacked)) * scale
                first = lax.broadcasted_iota(jnp.int32, dkey.shape, 1) < HEAD_SIZE
                g = jnp.concatenate([dq, jnp.where(first, dkey, dvalue)], 1)
                g = g * c[...] - self.roll(g, -32) * s1[...] - self.roll(g, 32) * s2[...]
                grads.append(g)
            g = jnp.concatenate(grads, 0)
            grad_t[...] = (g * inv_in[:, :1]).astype(BF16).T
            partial_out[...] = dot_nt(g.astype(BF16), wqkv[...]).astype(BF16)

        args = (grad, qkv, inv, self.wqkv, self.wo, *self.tables)
        return self.clock.call(
            body, args,
            [
                row_blocks(block, width),
                row_blocks(block, self.width),
                row_blocks(block, 128),
                *[whole(a) for a in args[3:]],
            ],
            [shape_of(self.width, rows), shape_of(rows, width)],
            [column_blocks(self.width, block), row_blocks(block, width)],
            rows // block,
        )


def feed(clock, normed, dy, wg, wu, wd, block=256):
    rows, width = normed.shape
    ff = wd.shape[0]

    def body(x, d, wg, wu, wd, act_out, dgate_out, dup_out, act_t, dgate_t, dup_t):
        gate = dot(x[...], wg[...])
        up = dot(x[...], wu[...])
        dact = dot_nt(d[...], wd[...])
        sigma = jax.nn.sigmoid(gate)
        silu = gate * sigma
        act = (silu * up).astype(BF16)
        dgate = (dact * up * (sigma * (1.0 + gate * (1.0 - sigma)))).astype(BF16)
        dup = (dact * silu).astype(BF16)
        for value, out, turned in ((act, act_out, act_t), (dgate, dgate_out, dgate_t), (dup, dup_out, dup_t)):
            out[...] = value
            turned[...] = value.T

    args = (normed, dy, wg, wu, wd)
    return clock.call(
        body, args, [row_blocks(block, width)] * 2 + [whole(a) for a in args[2:]],
        [shape_of(rows, ff)] * 3 + [shape_of(ff, rows)] * 3,
        [row_blocks(block, ff)] * 3 + [column_blocks(ff, block)] * 3,
        rows // block,
    )


def assemble(clock, me, above, below):
    copies = len(above)
    a, _, b, c = above[0].shape

    def body(me_ref, *refs):
        outs = refs[2 * copies - 1 :]
        for step in range(copies):
            at = lax.rem(me_ref[0] + step, copies)

            def store(ref, at=at):
                for which, out in enumerate(outs):
                    out[0, at] = ref[0, which]

            if step == 0:
                store(refs[0])
                continue

            @pl.when(me_ref[0] + step < copies)
            def _(ref=refs[copies + step - 1], store=store):
                store(ref)

            @pl.when(me_ref[0] + step >= copies)
            def _(ref=refs[copies - step], store=store):
                store(ref)

    args = [*above, *below[1:]]
    out = jax.ShapeDtypeStruct((a, copies, b, c), BF16)
    spec = pl.BlockSpec((1, 2, b, c), lambda i: (i, 0, 0, 0))
    out_spec = pl.BlockSpec((1, copies, b, c), lambda i: (i, 0, 0, 0))
    me = jnp.asarray(me, jnp.int32).reshape(1)
    return clock.call(
        body, [me, *args], [pl.BlockSpec(memory_space=pltpu.SMEM)] + [spec] * len(args),
        [out] * 2, [out_spec] * 2, a, vmem=24,
    )


def feed_weight_grad(clock, exchanged, weight, gain):
    own, columns = weight.shape
    shards, ff, _ = exchanged.shape
    join = 128 // math.gcd(ff, 128)

    def body(ins, w, g, grad_out, sum_out):
        value = ins[...].reshape(join * ff, own).astype(F32).T * g[...]
        grad_out[...] = value

        @pl.when(pl.program_id(0) == 0)
        def _():
            sum_out[...] = jnp.zeros_like(sum_out)

        total = jnp.sum(w[...].astype(F32) * value, -1, keepdims=True)
        sum_out[...] += jnp.broadcast_to(total, sum_out.shape)

    spec = pl.BlockSpec((join, ff, own), lambda i: (i, 0, 0))
    total = shape_of(own, 128, F32)
    return clock.call(
        body, [exchanged, weight, gain], [spec, column_blocks(own, join * ff), whole(gain)],
        [shape_of(own, columns, F32), total], [column_blocks(own, join * ff), whole_out(total)], shards // join,
    )


def qkv_weight_grad(clock, part, wq, wk, wv, gain):
    shards, cols, own = part.shape
    qcols, kv = wq.shape[1] // shards, wk.shape[1]
    sharing = shards * HEAD_SIZE // kv

    def body(ins, wq, wk, wv, g, q_out, k_out, v_out, sum_out):
        total = jnp.zeros((own, 1), F32)
        tails = []
        for j in range(shards):
            value = ins[j].astype(F32).T * g[...]
            at = pl.ds(j * qcols, qcols)
            q_out[:, at] = value[:, :qcols]
            total += jnp.sum(wq[:, at].astype(F32) * value[:, :qcols], -1, keepdims=True)
            tails.append(value[:, qcols:])
        tails = [sum(tails[j : j + sharing]) for j in range(0, shards, sharing)]
        for w, out, at in ((wk, k_out, 0), (wv, v_out, HEAD_SIZE)):
            value = jnp.concatenate([tail[:, at : at + HEAD_SIZE] for tail in tails], 1)
            out[...] = value
            total += jnp.sum(w[...].astype(F32) * value, -1, keepdims=True)
        sum_out[...] = jnp.broadcast_to(total, (own, 128))

    args = [part, wq, wk, wv, gain]
    outs = [shape_of(own, n, F32) for n in (shards * qcols, kv, kv, 128)]
    return clock.call(body, args, [whole(a) for a in args], outs, [whole_out(o) for o in outs])


def widen(clock, *parts):
    rows, width = sum(p.shape[0] for p in parts), parts[0].shape[1]

    def body(*refs):
        refs[-1][...] = jnp.concatenate([ref[...] for ref in refs[:-1]], 0).astype(F32)

    return clock.call(
        body, parts, [column_blocks(p.shape[0], width // 4) for p in parts],
        [shape_of(rows, width, F32)], [column_blocks(rows, width // 4)], 4,
    )[0]


def product(clock, lefts, rights, turned, block=512):
    rows = lefts[0].shape[0]
    width = rights[0].shape[0 if turned else 1]
    count = len(lefts)

    def body(*refs):
        pairs = zip(refs[:count], refs[count : 2 * count])
        multiply = dot_nt if turned else dot
        refs[-1][...] = sum(multiply(a[...], b[...]) for a, b in pairs).astype(BF16)

    return clock.call(
        body, [*lefts, *rights],
        [row_blocks(block, a.shape[1]) for a in lefts] + [whole(b) for b in rights],
        [shape_of(rows, width)], [row_blocks(block, width)], rows // block,
    )[0]


def weight_grad(clock, lefts, rights, parts, block=512):
    rows = lefts[0].shape[0] // parts
    width = rights[0].shape[1]
    count = len(lefts)

    def body(*refs):
        lefts, rights, outs = refs[:count], refs[count : 2 * count], refs[2 * count :]
        total = sum(dot(a[...], b[...]) for a, b in zip(lefts, rights)).astype(BF16)
        for at, out in enumerate(outs):
            out[...] = total[at * rows : (at + 1) * rows]

    return clock.call(
        body, [*lefts, *rights],
        [whole(a) for a in lefts] + [column_blocks(b.shape[0], block) for b in rights],
        [shape_of(rows, width)] * parts, [column_blocks(rows, block)] * parts, width // block,
    )


def on_device(shards, copies, tokens, gain1, wq, wk, wv, wo, gain2, wg, wu, wd, out_grad):
    seqs, length, width = tokens.shape
    rows = seqs * length
    clock = Clock()
    group, line = Group(shards, clock), Line(copies, clock)
    kv_heads = wk.shape[1] // HEAD_SIZE
    sharing = shards // kv_heads
    ff, qcols, own = wd.shape[0], wo.shape[0], wq.shape[0]
    cols = qcols + 2 * HEAD_SIZE
    g1 = gain1.astype(F32)[:, None]
    g2 = gain2.astype(F32)[:, None]
    flat = tokens.reshape(rows, width)
    low = out_grad.reshape(rows, width)

    x_steps = group.gather(flat)
    next(x_steps)

    def load_qkv(refs, j):
        wq, wk, wv, g = refs
        head = j // sharing * HEAD_SIZE
        parts = wq[:, j * qcols : (j + 1) * qcols], wk[:, head : head + HEAD_SIZE], wv[:, head : head + HEAD_SIZE]
        return (jnp.concatenate([p.astype(F32) for p in parts], 1) * g[...]).astype(BF16)

    qkv_steps = group.exchange(load_qkv, [wq, wk, wv, g1], own, cols)
    next(qkv_steps)
    next(x_steps)
    next(qkv_steps)

    share = own // copies

    def load_feed(refs, j):
        copy, wg, wu, g = refs
        at = pl.ds(pl.multiple_of(copy[0] * share, share), share)
        parts = [w[at, j * ff : (j + 1) * ff].astype(F32) * g[at, :] for w in (wg, wu)]
        return jnp.concatenate(parts, 0).astype(BF16)

    copy = jnp.asarray(line.me, jnp.int32).reshape(1)
    feed_steps = group.exchange(load_feed, [copy, wg, wu, g2], 2 * share, ff)
    next(feed_steps)
    drain(x_steps)
    x_all = group.gathered
    drain(qkv_steps)
    wqkv = group.exchanged.reshape(width, cols)
    next(feed_steps)

    attention = Attention(clock, length, qcols, wqkv, wo)
    qkv_o, inv_o, context_ot, part_o = attention.forward(x_all[1])
    other = group.partner(part_o)
    drain(feed_steps)
    share_steps = line.share(group.exchanged.reshape(shards, 2, share, ff))
    next(share_steps, None)
    group.ride(clock.tie(low))
    qkv_e, inv_e, context_et, part_e = attention.forward(x_all[0])
    h1_steps = group.scatter([(part_e, other)], low)
    next(h1_steps)
    next(share_steps, None)
    next(h1_steps)
    next(share_steps, None)
    drain(h1_steps)

    def first_half(at, total, x, h1, inv2, n2):
        value = x[at, :].astype(F32) + total
        inv = lax.rsqrt(jnp.mean(value * value, -1, keepdims=True) + EPS)
        h1[at, :] = value
        inv2[at, :] = jnp.broadcast_to(inv, (inv.shape[0], 128))
        n2[at, :] = (value * inv).astype(BF16)

    h1, inv2, n2 = group.finish_rows(
        first_half, group.terms[0], [flat], [shape_of(rows, width, F32), shape_of(rows, 128, F32), shape_of(rows, width)]
    )
    n2_steps = group.gather(n2)
    next(n2_steps)
    group.join_rider()
    dy = group.gathered
    next(n2_steps)
    drain(share_steps)
    wg_mine, wu_mine = assemble(clock, line.me, *line.shared)
    wg_mine, wu_mine = wg_mine.reshape(width, ff), wu_mine.reshape(width, ff)
    drain(n2_steps)
    n2 = group.gathered
    results = {}

    def sum_copies(name, parts):
        for at, part in enumerate(parts):
            line.queue(part, functools.partial(results.__setitem__, (name, at)))

    def exchange_back(*parts):
        def load(refs, j):
            blocks = [ref[:, j * own : (j + 1) * own] for ref in refs]
            return jnp.concatenate(blocks, 0) if len(blocks) > 1 else blocks[0]

        return group.exchange(load, parts, sum(part.shape[0] for part in parts), own)

    act_e, dgate_e, dup_e, act_et, dgate_et, dup_et = feed(clock, n2[0], dy[0], wg_mine, wu_mine, wd)
    act_o, dgate_o, dup_o, act_ot, dgate_ot, dup_ot = feed(clock, n2[1], dy[1], wg_mine, wu_mine, wd)
    sum_copies("down", weight_grad(clock, (act_et, act_ot), dy, 2))
    line.tick()
    other = group.partner(product(clock, (dgate_o, dup_o), (wg_mine, wu_mine), True))
    part_e = product(clock, (dgate_e, dup_e), (wg_mine, wu_mine), True)
    a2_steps = group.scatter([(part_e, other)])
    next(a2_steps)
    line.tick()
    sum_copies("gate", weight_grad(clock, (dgate_et, dgate_ot), n2, 2))
    sum_copies("up", weight_grad(clock, (dup_et, dup_ot), n2, 2))
    next(a2_steps)
    line.tick()
    drain(a2_steps)

    def second_half(at, total, dy, h1, inv2, dh1, low_out):
        value, inv = h1[at, :], inv2[at, :1]
        middle = jnp.mean(total * value, -1, keepdims=True)
        grad = dy[at, :].astype(F32) + inv * total - value * (inv * inv * inv) * middle
        dh1[at, :] = grad
        low_out[at, :] = grad.astype(BF16)

    dh1, dattn = group.finish_rows(
        second_half, group.terms[0], [low, h1, inv2], [shape_of(rows, width, F32), shape_of(rows, width)]
    )
    dattn_steps = group.gather(dattn)
    next(dattn_steps)
    out_parts = product(clock, (act_e,), (wd,), False), group.partner(product(clock, (act_o,), (wd,), False))
    next(dattn_steps)
    line.tick()
    drain(dattn_steps)
    dattn = group.gathered
    dqkv_et, part_e = attention.backward(dattn[0], qkv_e, inv_e)
    dqkv_ot, part_o = attention.backward(dattn[1], qkv_o, inv_o)
    other = group.partner(part_o)
    line.tick()
    a1_steps = group.scatter([(part_e, other), out_parts])
    next(a1_steps)
    sum_copies("qkv", weight_grad(clock, (dqkv_et, dqkv_ot), x_all, 1))
    sum_copies("o", weight_grad(clock, (context_et, context_ot), dattn, 1))
    line.tick()
    next(a1_steps)
    line.tick()
    drain(a1_steps)

    def output(at, total, h1, out):
        out[at, :] = (h1[at, :] + total).astype(BF16)

    def input_half(at, total, x, dh1, out):
        value = x[at, :].astype(F32)
        inv = lax.rsqrt(jnp.mean(value * value, -1, keepdims=True) + EPS)
        middle = jnp.mean(total * value, -1, keepdims=True)
        out[at, :] = dh1[at, :] + inv * total - value * (inv * inv * inv) * middle

    (input_grad,) = group.finish_rows(
        input_half, group.terms[0], [flat, dh1], [shape_of(rows, width, F32)]
    )
    (layer_out,) = group.finish_rows(output, group.terms[1], [h1], [shape_of(rows, width)])
    def tick_until(name, at):
        while (name, at) not in results:
            line.tick(4)

    tick_until("gate", 1)
    gate_steps = exchange_back(results["gate", 0], results["gate", 1])
    next(gate_steps)
    next(gate_steps)
    line.tick(4)
    down_grad = widen(clock, results["down", 0], results["down", 1])
    drain(gate_steps)
    gate_grad, gate_sums = feed_weight_grad(clock, group.exchanged, wg, g2)
    tick_until("up", 1)
    up_steps = exchange_back(results["up", 0], results["up", 1])
    next(up_steps)
    next(up_steps)
    tick_until("qkv", 0)
    qkv_steps = exchange_back(results["qkv", 0])
    next(qkv_steps)
    drain(up_steps)
    up_back = group.exchanged
    next(qkv_steps)
    up_grad, up_sums = feed_weight_grad(clock, up_back, wu, g2)
    tick_until("o", 0)
    o_grad = widen(clock, results["o", 0])
    drain(qkv_steps)
    q_grad, k_grad, v_grad, qkv_sums = qkv_weight_grad(clock, group.exchanged, wq, wk, wv, g1)

    gain1_grad = qkv_sums[:, 0] / g1[:, 0]
    gain2_grad = (gate_sums[:, 0] + up_sums[:, 0]) / g2[:, 0]
    return (
        layer_out.reshape(seqs, length, width),
        input_grad.reshape(seqs, length, width),
        gain1_grad,
        q_grad,
        k_grad,
        v_grad,
        o_grad,
        gain2_grad,
        gate_grad,
        up_grad,
        down_grad,
    )


def solution(mesh):
    rows = P(("shard", "rep"), None, None)
    vector, matrix = P("shard"), P("shard", None)
    return jax.shard_map(
        functools.partial(on_device, mesh.shape["shard"], mesh.shape["rep"]),
        mesh=mesh,
        in_specs=(rows, vector, matrix, matrix, matrix, matrix, vector, matrix, matrix, matrix, rows),
        out_specs=(rows, rows, vector, matrix, matrix, matrix, matrix, vector, matrix, matrix, matrix),
        check_vma=False,
    )
```

time: 1690 us -> 692 us (0.41)
  waiting for transfers between devices: 1370 us -> 190 us
  Pallas kernels: 0 us -> 324 us
  matrix products: 187 us -> 0 us
  starting transfers between devices: 1.23 us -> 113 us
  blocking collectives: 45.8 us -> 0 us
  other arithmetic: 32.2 us -> 0.69 us
    reduce_scatter x7 -> x0, waiting for transfers between devices: 607 us -> none  [the longest x1 150 us: on_device(): lax.psum_scatter(grad_wu.astype(jnp.bfloat16), 'shard', scatter_dimension...]
    all_gather x7 -> x0, waiting for transfers between devices: 434 us -> none  [the longest x1 111 us: on_device(): lax.all_gather(gate_weight, 'shard', axis=0, tiled=True)]
    pallas_call x0 -> x121, Pallas kernels: none -> 324 us  [call(): pl.pallas_call(kernel, grid=(steps,), out_shape=(*outs, pltpu.HBM(self.to...]
    psum x1 -> x0, waiting for transfers between devices: 321 us -> none  [on_device(): lax.psum(attn_owned[1].astype(jnp.bfloat16), 'rep').astype(jnp.float32)]
    ppermute x0 -> x80, waiting for transfers between devices: none -> 190 us  [the longest x54 107 us: swap(): lax.ppermute(value, 'shard', [(i, i ^ bit) for i in range(self.size)])]
    dot_general x27 -> x0, matrix products: 187 us -> none  [the longest x7 69 us: compared_with(): lax.dot_general(left, right, (((1,), (1,)), ((), ())), preferred_element_...]
    ppermute x0 -> x80, starting transfers between devices: none -> 113 us  [the longest x26 64.2 us: shift(): return lax.ppermute(value, 'rep', pairs)]
    unnamed x95 -> x127, local copies, waits for them, and re-layouts: 10.4 us -> 45.9 us
  transfers between devices with their start and end apart: 15 -> 80, of which waited for: 14 -> 38; matrix products, arithmetic and copies ran while one was open for 9% -> 1% of each run, Pallas kernels for 0% -> 43%
where the time goes in v1:
time: 692 us; the launch traced here: 681 us
  Pallas kernels  324 us (47%)
  waiting for transfers between devices  190 us (27%)
  starting transfers between devices  113 us (16%)
  local copies, waits for them, and re-layouts  51.4 us (7%)
    pallas_call x121, Pallas kernels, call(): pl.pallas_call(kernel, grid=(steps,), out_shape=(*outs, pltpu.HBM(self.to...  324 us
    ppermute x54, waiting for transfers between devices, swap(): lax.ppermute(value, 'shard', [(i, i ^ bit) for i in range(self.size)])  107 us
    ppermute x26, waiting for transfers between devices, shift(): return lax.ppermute(value, 'rep', pairs)  82.9 us
    ppermute x26, starting transfers between devices, shift(): return lax.ppermute(value, 'rep', pairs)  64.2 us
    ppermute x54, starting transfers between devices, swap(): lax.ppermute(value, 'shard', [(i, i ^ bit) for i in range(self.size)])  49.2 us
    unnamed x127, local copies, waits for them, and re-layouts  45.9 us
  transfers between devices with their start and end apart: 80, of which 38 were waited for; matrix products, arithmetic and copies ran while one was open for 1% of the time, Pallas kernels for 43%

profile of v1, /device:TPU:0, one launch (start us, length us, event | category | flops | bytes accessed | tf_op | source)
XLA Modules:
  0.0 681.3 jit_solution(12427376757924317765)
XLA Ops:
  0.6 3.0 collective-permute-start.1
  12.0 15.0 %collective-permute-done.1.refs_1_.refs_4_.refs_5_ = bf16[256,2048]{1,0:T(8,128)(2,1)S(1)} collective-permute-done((bf16[256,2048]{1,0:T(8,128)(2,1)}, bf16[256,2048]{1,0:T(8,128)(2,1)S(1)}, u32[]{:S(2)}, u32[]{:S(2)}) %collective-permute-start.1) | collective-permute-done | bytes 1048608 | tf_op jit(solution)/shard_map/ppermute | solution.py:223
  45.2 4.2 shard_map.230
  49.6 3.9 collective-permute-done.5.refs_3_
  53.5 6.9 %collective-permute-done.7.refs_5_ = bf16[2,256,384]{2,1,0:T(8,128)(2,1)} collective-permute-done((bf16[2,256,384]{2,1,0:T(8,128)(2,1)}, bf16[2,256,384]{2,1,0:T(8,128)(2,1)}, u32[]{:S(2)}, u32[]{:S(2)}) %collective-permute-start.7) | collective-permute-done | bytes 393248 | tf_op jit(solution)/shard_map/ppermute | solution.py:223
  69.0 12.0 %shard_map.235 = (bf16[1024,384]{1,0:T(8,128)(2,1)}, f32[1024,128]{1,0:T(8,128)}, bf16[256,1024]{1,0:T(8,128)(2,1)}, bf16[1024,2048]{1,0:T(8,128)(2,1)}, f32[8,128]{1,0:T(8,128)}) custom-call(bf16[1024,2048]{1,0:T(8,128)(2,1)} %collective-permute-done.12.refs_0_.refs_3_, bf16[2048,384]{1,0:T(8,128)(2,1)} %bitcast.21, ...), custom_call_target="tpu_custom_call", output_to_operand_aliasing={{4}: (6, {})} | custom-call | flops 1 | bytes 1 | tf_op jit(solution)/shard_map/pallas_call | solution.py:69
  81.0 2.8 collective-permute-done.10.refs_4_
  88.1 5.7 collective-permute-start.18
  93.8 12.0 %shard_map.241 = (bf16[1024,384]{1,0:T(8,128)(2,1)}, f32[1024,128]{1,0:T(8,128)}, bf16[256,1024]{1,0:T(8,128)(2,1)}, bf16[1024,2048]{1,0:T(8,128)(2,1)}, f32[8,128]{1,0:T(8,128)}) custom-call(bf16[1024,2048]{1,0:T(8,128)(2,1)} %get-tuple-element.238.refs_0_.refs_2_, bf16[2048,384]{1,0:T(8,128)(2,1)} %bitcast.22, ...), custom_call_target="tpu_custom_call", output_to_operand_aliasing={{4}: (6, {})} | custom-call | flops 1 | bytes 1 | tf_op jit(solution)/shard_map/pallas_call | solution.py:69
  115.5 7.3 %collective-permute-done.19.refs_1_ = bf16[8,2,64,704]{3,2,1,0:T(8,128)(2,1)} collective-permute-done((bf16[8,2,64,704]{3,2,1,0:T(8,128)(2,1)}, bf16[8,2,64,704]{3,2,1,0:T(8,128)(2,1)}, u32[]{:S(2)}, u32[]{:S(2)}) %collective-permute-start.19) | collective-permute-done | bytes 1441824 | tf_op jit(solution)/shard_map/ppermute | solution.py:106
  126.0 8.3 %collective-permute-done.16.refs_2_ = bf16[256,2048]{1,0:T(8,128)(2,1)S(1)} collective-permute-done((bf16[256,2048]{1,0:T(8,128)(2,1)S(1)}, bf16[256,2048]{1,0:T(8,128)(2,1)S(1)}, u32[]{:S(2)}, u32[]{:S(2)}) %collective-permute-start.16) | collective-permute-done | bytes 1048608 | tf_op jit(solution)/shard_map/ppermute | solution.py:223
  140.1 22.8 %collective-permute-done.23.refs_1_ = bf16[8,2,64,704]{3,2,1,0:T(8,128)(2,1)S(1)} collective-permute-done((bf16[8,2,64,704]{3,2,1,0:T(8,128)(2,1)}, bf16[8,2,64,704]{3,2,1,0:T(8,128)(2,1)S(1)}, u32[]{:S(2)}, u32[]{:S(2)}) %collective-permute-start.23) | collective-permute-done | bytes 1441824 | tf_op jit(solution)/shard_map/ppermute | solution.py:106
  175.7 17.7 %collective-permute-done.25.refs_1_.refs_4_.refs_5_ = bf16[256,2048]{1,0:T(8,128)(2,1)S(1)} collective-permute-done((bf16[256,2048]{1,0:T(8,128)(2,1)S(1)}, bf16[256,2048]{1,0:T(8,128)(2,1)S(1)}, u32[]{:S(2)}, u32[]{:S(2)}) %collective-permute-start.25) | collective-permute-done | bytes 1048608 | tf_op jit(solution)/shard_map/ppermute | solution.py:223
  197.4 4.9 shard_map.258
  207.9 17.4 %shard_map.261 = (bf16[1024,704]{1,0:T(8,128)(2,1)}, bf16[1024,704]{1,0:T(8,128)(2,1)}, bf16[1024,704]{1,0:T(8,128)(2,1)}, bf16[704,1024]{1,0:T(8,128)(2,1)}, bf...) custom-call(bf16[1024,2048]{1,0:T(8,128)(2,1)} %get-tuple-element.284, ...), custom_call_target="tpu_custom_call", output_to_operand_aliasing={{6}: (5, {})} | custom-call | flops 1 | bytes 1 | tf_op jit(solution)/shard_map/pallas_call | solution.py:69
  225.3 17.4 %shard_map.262 = (bf16[1024,704]{1,0:T(8,128)(2,1)}, bf16[1024,704]{1,0:T(8,128)(2,1)}, bf16[1024,704]{1,0:T(8,128)(2,1)}, bf16[704,1024]{1,0:T(8,128)(2,1)}, bf...) custom-call(bf16[1024,2048]{1,0:T(8,128)(2,1)} %collective-permute-do, ...), custom_call_target="tpu_custom_call", output_to_operand_aliasing={{6}: (5, {})} | custom-call | flops 1 | bytes 1 | tf_op jit(solution)/shard_map/pallas_call | solution.py:69
  242.7 10.0 %shard_map.263 = (bf16[352,2048]{1,0:T(8,128)(2,1)}, bf16[352,2048]{1,0:T(8,128)(2,1)}, f32[8,128]{1,0:T(8,128)}) custom-call(bf16[704,1024]{1,0:T(8,128)(2,1)} %get-tuple-element.295.refs_0_, bf16[704,1024]{1,0:T(8,128)(2,1)} %get-tuple-element.296.refs_1_, bf16[1024,2048]{1,0:T(8,128)(2,1)} %get-tuple-element.285.refs_1_.refs_2_, ...), custom_call_target="tpu_custom_call", output_to_operand_aliasing={{2}: (4, {})} | custom-call | flops 1 | bytes 1 | tf_op jit(solution)/shard_map/pallas_call | solution.py:69
  255.2 6.1 collective-permute-start.35
  261.3 11.6 %shard_map.266 = (bf16[1024,2048]{1,0:T(8,128)(2,1)}, f32[8,128]{1,0:T(8,128)}) custom-call(bf16[1024,704]{1,0:T(8,128)(2,1)} %get-tuple-element.293.refs_0_, bf16[1024,704]{1,0:T(8,128)(2,1)} %get-tuple-element.294.refs_1_, bf16[2048,704]{1,0:T(8,128)(2,1)} %bitcast.15, bf16[2048,704]{1,0:T(8,128)(2,1)} %bitcast.19, ...), custom_call_target="tpu_custom_call", output_to_operand_aliasing={{1}: (4, {})} | custom-call | flops 1 | bytes 1 | tf_op jit(solution)/shard_map/pallas_call | solution.py:69
  273.1 11.6 %shard_map.268 = (bf16[1024,2048]{1,0:T(8,128)(2,1)}, f32[8,128]{1,0:T(8,128)}) custom-call(bf16[1024,704]{1,0:T(8,128)(2,1)} %get-tuple-element.290.refs_0_, bf16[1024,704]{1,0:T(8,128)(2,1)} %get-tuple-element.291.refs_1_, bf16[2048,704]{1,0:T(8,128)(2,1)} %bitcast.16, bf16[2048,704]{1,0:T(8,128)(2,1)} %bitcast.20, ...), custom_call_target="tpu_custom_call", output_to_operand_aliasing={{1}: (4, {})} | custom-call | flops 1 | bytes 1 | tf_op jit(solution)/shard_map/pallas_call | solution.py:69
  286.9 3.2 shard_map.269
  292.4 3.5 shard_map.271
  297.7 5.2 collective-permute-start.39
  302.9 10.0 %shard_map.273 = (bf16[352,2048]{1,0:T(8,128)(2,1)}, bf16[352,2048]{1,0:T(8,128)(2,1)}, f32[8,128]{1,0:T(8,128)}) custom-call(bf16[704,1024]{1,0:T(8,128)(2,1)} %get-tuple-element.309.refs_0_, bf16[704,1024]{1,0:T(8,128)(2,1)} %get-tuple-element.310.refs_1_, bf16[1024,2048]{1,0:T(8,128)(2,1)} %get-tuple-element.284.refs_0_.refs_2_, ...), custom_call_target="tpu_custom_call", output_to_operand_aliasing={{2}: (4, {})} | custom-call | flops 1 | bytes 1 | tf_op jit(solution)/shard_map/pallas_call | solution.py:69
  312.9 10.1 %shard_map.274 = (bf16[352,2048]{1,0:T(8,128)(2,1)}, bf16[352,2048]{1,0:T(8,128)(2,1)}, f32[8,128]{1,0:T(8,128)}) custom-call(bf16[704,1024]{1,0:T(8,128)(2,1)} %get-tuple-element.307.refs_0_, bf16[704,1024]{1,0:T(8,128)(2,1)} %get-tuple-element.308.refs_1_, bf16[1024,2048]{1,0:T(8,128)(2,1)} %get-tuple-element.284.refs_0_.refs_2_, ...), custom_call_target="tpu_custom_call", output_to_operand_aliasing={{2}: (4, {})} | custom-call | flops 1 | bytes 1 | tf_op jit(solution)/shard_map/pallas_call | solution.py:69
  323.0 2.9 copy-done.1
  332.6 4.7 shard_map.277
  346.3 3.6 shard_map.279
  352.6 7.0 %shard_map.281 = (bf16[1024,2048]{1,0:T(8,128)(2,1)}, f32[8,128]{1,0:T(8,128)}) custom-call(bf16[1024,704]{1,0:T(8,128)(2,1)} %get-tuple-element.289.refs_0_, bf16[704,2048]{1,0:T(8,128)(2,1)} %refs_1_.8, f32[8,128]{1,0:T(8,128)} %shard_map.280.refs_2_), custom_call_target="tpu_custom_call", output_to_operand_aliasing={{1}: (2, {})} | custom-call | flops 1 | bytes 1 | tf_op jit(solution)/shard_map/pallas_call | solution.py:69
  359.6 7.0 %shard_map.282 = (bf16[1024,2048]{1,0:T(8,128)(2,1)}, f32[8,128]{1,0:T(8,128)}) custom-call(bf16[1024,704]{1,0:T(8,128)(2,1)} %get-tuple-element.328.refs_0_, bf16[704,2048]{1,0:T(8,128)(2,1)} %refs_1_.8, f32[8,128]{1,0:T(8,128)} %get-tuple-element.329.refs_2_), custom_call_target="tpu_custom_call", output_to_operand_aliasing={{1}: (2, {})} | custom-call | flops 1 | bytes 1 | tf_op jit(solution)/shard_map/pallas_call | solution.py:69
  366.6 6.8 collective-permute-done.42.refs_1_.refs_4_.refs_5_
  377.0 4.5 shard_map.286
  384.7 2.7 shard_map.288
  387.4 4.2 shard_map.289
  391.6 14.6 %shard_map.291 = (bf16[384,1024]{1,0:T(8,128)(2,1)}, bf16[1024,2048]{1,0:T(8,128)(2,1)}, f32[8,128]{1,0:T(8,128)}) custom-call(bf16[1024,2048]{1,0:T(8,128)(2,1)} %get-tuple-element.341.refs_0_.refs_2_, bf16[1024,384]{1,0:T(8,128)(2,1)} %get-tuple-element.342.refs_1_, f32[1024,128]{1,0:T(8,128)} %get-tuple-element.343.refs_2_, ...), custom_call_target="tpu_custom_call", output_to_operand_aliasing={{2}: (8, {})} | custom-call | flops 1 | bytes 1 | tf_op jit(solution)/shard_map/pallas_call | solution.py:69
  406.2 14.6 %shard_map.292 = (bf16[384,1024]{1,0:T(8,128)(2,1)}, bf16[1024,2048]{1,0:T(8,128)(2,1)}, f32[8,128]{1,0:T(8,128)}) custom-call(bf16[1024,2048]{1,0:T(8,128)(2,1)} %collective-permute-done.47.refs_0_.refs_3_, bf16[1024,384]{1,0:T(8,128)(2,1)} %get-tuple-element.346.refs_1_, f32[1024,128]{1,0:T(8,128)} %get-tuple-element.347.refs_2_, ...), custom_call_target="tpu_custom_call", output_to_operand_aliasing={{2}: (8, {})} | custom-call | flops 1 | bytes 1 | tf_op jit(solution)/shard_map/pallas_call | solution.py:69
  421.4 4.5 shard_map.294
  429.9 2.7 shard_map.296
  434.8 5.5 shard_map.297
  443.5 7.6 %shard_map.299 = (bf16[384,2048]{1,0:T(8,128)(2,1)}, f32[8,128]{1,0:T(8,128)}) custom-call(bf16[384,1024]{1,0:T(8,128)(2,1)} %get-tuple-element.363.refs_0_, bf16[384,1024]{1,0:T(8,128)(2,1)} %get-tuple-element.364.refs_1_, bf16[1024,2048]{1,0:T(8,128)(2,1)} %get-tuple-element.238.refs_0_.refs_2_, ...), custom_call_target="tpu_custom_call", output_to_operand_aliasing={{1}: (4, {})} | custom-call | flops 1 | bytes 1 | tf_op jit(solution)/shard_map/pallas_call | solution.py:69
  451.1 6.6 shard_map.300
  461.0 4.5 shard_map.301
  469.9 2.7 shard_map.303
  472.7 15.1 %collective-permute-done.51.refs_2_.refs_5_ = bf16[512,2048]{1,0:T(8,128)(2,1)S(1)} collective-permute-done((bf16[512,2048]{1,0:T(8,128)(2,1)}, bf16[512,2048]{1,0:T(8,128)(2,1)S(1)}, u32[]{:S(2)}, u32[]{:S(2)}) %collective-permute-start.51) | collective-permute-done | bytes 2097184 | tf_op jit(solution)/shard_map/ppermute | solution.py:223
  491.6 4.0 shard_map.304
  500.4 4.8 shard_map.306
  508.3 7.6 %collective-permute-start.60 = (bf16[384,2048]{1,0:T(8,128)(2,1)}, bf16[384,2048]{1,0:T(8,128)(2,1)}, u32[]{:S(2)}, u32[]{:S(2)}) collective-permute-start(bf16[384,2048]{1,0:T(8,128)(2,1)} %get-tuple-element.383.refs_3_), channel_id=1, source_target_pairs={{0,1},{3,2},{4,5},{7,6},{8,9},{11,10},{12,13},{15,14},{16,17},{19,... | collective-permute-start | bytes 4718600 | tf_op jit(solution)/shard_map/ppermute | solution.py:106
  524.5 4.8 shard_map.309
  529.3 3.4 shard_map.310
  533.3 3.2 collective-permute-done.61.refs_1_.refs_2_
  541.6 5.0 collective-permute-done.60.refs_4_
  546.6 4.6 shard_map.315
  551.2 5.4 collective-permute-start.63
  558.4 2.7 shard_map.317
  561.1 4.8 shard_map.318
  567.2 5.1 collective-permute-done.65.refs_4_
  575.4 6.4 shard_map.320
  581.9 3.8 shard_map.321
  587.4 10.8 %collective-permute-done.70.refs_1_ = bf16[352,2048]{1,0:T(8,128)(2,1)} collective-permute-done((bf16[352,2048]{1,0:T(8,128)(2,1)}, bf16[352,2048]{1,0:T(8,128)(2,1)}, u32[]{:S(2)}, u32[]{:S(2)}) %collective-permute-start.70) | collective-permute-done | bytes 1441824 | tf_op jit(solution)/shard_map/ppermute | solution.py:106
  615.3 27.0 %collective-permute-done.68.refs_1_ = bf16[384,2048]{1,0:T(8,128)(2,1)} collective-permute-done((bf16[384,2048]{1,0:T(8,128)(2,1)}, bf16[384,2048]{1,0:T(8,128)(2,1)}, u32[]{:S(2)}, u32[]{:S(2)}) %collective-permute-start.68) | collective-permute-done | bytes 1572896 | tf_op jit(solution)/shard_map/ppermute | solution.py:106
  642.3 2.8 shard_map.330
  655.1 6.4 shard_map.336
  666.7 3.6 shard_map.339
  674.3 5.0 shard_map.341
  (354 shorter events, 203.6 us)
Async XLA Ops:
  0.6 26.4 %collective-permute-start.1 = (bf16[256,2048]{1,0:T(8,128)(2,1)}, bf16[256,2048]{1,0:T(8,128)(2,1)S(1)}, u32[]{:S(2)}, u32[]{:S(2)}) collective-permute-start(bf16[256,2048]{1,0:T(8,128)(2,1)} %bitcast.25), channel_id=1, source_target_pairs={{0,16},{4,20},{8,24},{12,28},{16,0},{20,4},{24,8},{28,12},{1,17},{... | collective-permute-start | bytes 3145736 | tf_op jit(solution)/shard_map/ppermute | solution.py:223
  3.7 24.8 %collective-permute-start = (bf16[256,2048]{1,0:T(8,128)(2,1)}, bf16[256,2048]{1,0:T(8,128)(2,1)S(1)}, u32[]{:S(2)}, u32[]{:S(2)}) collective-permute-start(bf16[256,2048]{1,0:T(8,128)(2,1)} %bitcast.26), channel_id=1, source_target_pairs={{0,8},{4,12},{8,0},{12,4},{16,24},{20,28},{24,16},{28,20},{1,9},{5... | collective-permute-start | bytes 3145736 | tf_op jit(solution)/shard_map/ppermute | solution.py:223
  10.8 20.7 %collective-permute-start.4 = (bf16[4,256,384]{2,1,0:T(8,128)(2,1)}, bf16[4,256,384]{2,1,0:T(8,128)(2,1)}, u32[]{:S(2)}, u32[]{:S(2)}) collective-permute-start(bf16[4,256,384]{2,1,0:T(8,128)(2,1)} %get-tuple-element.234), channel_id=1, source_target_pairs={{0,4},{4,0},{8,12},{12,8},{16,20},{20,16},{24,28},{28,24},{1,5},{5... | collective-permute-start | bytes 2359304 | tf_op jit(solution)/shard_map/ppermute | solution.py:223
  34.9 18.6 %collective-permute-start.5 = (bf16[2,256,384]{2,1,0:T(8,128)(2,1)}, bf16[2,256,384]{2,1,0:T(8,128)(2,1)}, u32[]{:S(2)}, u32[]{:S(2)}) collective-permute-start(bf16[2,256,384]{2,1,0:T(8,128)(2,1)} %get-tuple-element.239), channel_id=1, source_target_pairs={{0,8},{4,12},{8,0},{12,4},{16,24},{20,28},{24,16},{28,20},{1,9},{5... | collective-permute-start | bytes 1179656 | tf_op jit(solution)/shard_map/ppermute | solution.py:223
  35.3 18.2 %collective-permute-start.6 = (bf16[2,256,384]{2,1,0:T(8,128)(2,1)}, bf16[2,256,384]{2,1,0:T(8,128)(2,1)}, u32[]{:S(2)}, u32[]{:S(2)}) collective-permute-start(bf16[2,256,384]{2,1,0:T(8,128)(2,1)} %get-tuple-element.240), channel_id=1, source_target_pairs={{0,16},{4,20},{8,24},{12,28},{16,0},{20,4},{24,8},{28,12},{1,17},{... | collective-permute-start | bytes 1179656 | tf_op jit(solution)/shard_map/ppermute | solution.py:223
  36.9 23.4 %collective-permute-start.7 = (bf16[2,256,384]{2,1,0:T(8,128)(2,1)}, bf16[2,256,384]{2,1,0:T(8,128)(2,1)}, u32[]{:S(2)}, u32[]{:S(2)}) collective-permute-start(bf16[2,256,384]{2,1,0:T(8,128)(2,1)} %get-tuple-element.241), channel_id=1, source_target_pairs={{0,24},{4,28},{8,16},{12,20},{16,8},{20,12},{24,0},{28,4},{1,25},{... | collective-permute-start | bytes 1179656 | tf_op jit(solution)/shard_map/ppermute | solution.py:223
  44.8 18.2 %collective-permute-start.8 = (bf16[4,128,704]{1,2,0:T(8,128)(2,1)S(1)}, bf16[4,128,704]{1,2,0:T(8,128)(2,1)}, u32[]{:S(2)}, u32[]{:S(2)}) collective-permute-start(bf16[4,128,704]{1,2,0:T(8,128)(2,1)S(1)} %copy-done.56), channel_id=1, source_target_pairs={{0,4},{4,0},{8,12},{12,8},{16,20},{20,16},{24,28},{28,24},{1,5},{5... | collective-permute-start | bytes 2162696 | tf_op jit(solution)/shard_map/ppermute | solution.py:223
  49.4 19.6 %collective-permute-start.12 = (bf16[1024,2048]{1,0:T(8,128)(2,1)}, bf16[1024,2048]{1,0:T(8,128)(2,1)}, u32[]{:S(2)}, u32[]{:S(2)}) collective-permute-start(bf16[1024,2048]{1,0:T(8,128)(2,1)} %get-tuple-element.238.refs_0_.refs_2_), channel_id=1, source_target_pairs={{0,4},{4,0},{8,12},{12,8},{16,20},{20,16},{24,28},{28,24},{1,5},{5... | collective-permute-start | bytes 12582920 | tf_op jit(solution)/shard_map/ppermute | solution.py:223
  67.0 16.8 %collective-permute-start.10 = (bf16[2,128,704]{2,1,0:T(8,128)(2,1)}, bf16[2,128,704]{2,1,0:T(8,128)(2,1)S(1)}, u32[]{:S(2)}, u32[]{:S(2)}) collective-permute-start(bf16[2,128,704]{2,1,0:T(8,128)(2,1)} %get-tuple-element.248), channel_id=1, source_target_pairs={{0,16},{4,20},{8,24},{12,28},{16,0},{20,4},{24,8},{28,12},{1,17},{... | collective-permute-start | bytes 1081352 | tf_op jit(solution)/shard_map/ppermute | solution.py:223
  67.6 16.2 %collective-permute-start.11 = (bf16[2,128,704]{2,1,0:T(8,128)(2,1)}, bf16[2,128,704]{2,1,0:T(8,128)(2,1)S(1)}, u32[]{:S(2)}, u32[]{:S(2)}) collective-permute-start(bf16[2,128,704]{2,1,0:T(8,128)(2,1)} %get-tuple-element.249), channel_id=1, source_target_pairs={{0,24},{4,28},{8,16},{12,20},{16,8},{20,12},{24,0},{28,4},{1,25},{... | collective-permute-start | bytes 1081352 | tf_op jit(solution)/shard_map/ppermute | solution.py:223
  81.0 27.5 %collective-permute-start.13 = (bf16[1024,2048]{1,0:T(8,128)(2,1)}, bf16[1024,2048]{1,0:T(8,128)(2,1)}, u32[]{:S(2)}, u32[]{:S(2)}) collective-permute-start(bf16[1024,2048]{1,0:T(8,128)(2,1)} %get-tuple-element.255), channel_id=1, source_target_pairs={{0,4},{4,0},{8,12},{12,8},{16,20},{20,16},{24,28},{28,24},{1,5},{5... | collective-permute-start | bytes 12582920 | tf_op jit(solution)/shard_map/ppermute | solution.py:223
  85.0 23.0 %collective-permute-start.15 = (bf16[256,2048]{1,0:T(8,128)(2,1)}, bf16[256,2048]{1,0:T(8,128)(2,1)S(1)}, u32[]{:S(2)}, u32[]{:S(2)}) collective-permute-start(bf16[256,2048]{1,0:T(8,128)(2,1)} %get-tuple-element.256), channel_id=1, source_target_pairs={{0,16},{4,20},{8,24},{12,28},{16,0},{20,4},{24,8},{28,12},{1,17},{... | collective-permute-start | bytes 3145736 | tf_op jit(solution)/shard_map/ppermute | solution.py:223
  85.7 22.7 %collective-permute-start.14 = (bf16[256,2048]{1,0:T(8,128)(2,1)}, bf16[256,2048]{1,0:T(8,128)(2,1)S(1)}, u32[]{:S(2)}, u32[]{:S(2)}) collective-permute-start(bf16[256,2048]{1,0:T(8,128)(2,1)} %get-tuple-element.256), channel_id=1, source_target_pairs={{0,8},{4,12},{8,0},{12,4},{16,24},{20,28},{24,16},{28,20},{1,9},{5... | collective-permute-start | bytes 3145736 | tf_op jit(solution)/shard_map/ppermute | solution.py:223
  86.8 36.0 %collective-permute-start.19 = (bf16[8,2,64,704]{3,2,1,0:T(8,128)(2,1)}, bf16[8,2,64,704]{3,2,1,0:T(8,128)(2,1)}, u32[]{:S(2)}, u32[]{:S(2)}) collective-permute-start(bf16[8,2,64,704]{3,2,1,0:T(8,128)(2,1)} %bitcast.35), channel_id=1, source_target_pairs={{3,2},{2,1},{1,0},{7,6},{6,5},{5,4},{11,10},{10,9},{9,8},{15,14},{... | collective-permute-start | bytes 4325384 | tf_op jit(solution)/shard_map/ppermute | solution.py:106
  88.1 35.9 %collective-permute-start.18 = (bf16[8,2,64,704]{3,2,1,0:T(8,128)(2,1)}, bf16[8,2,64,704]{3,2,1,0:T(8,128)(2,1)}, u32[]{:S(2)}, u32[]{:S(2)}) collective-permute-start(bf16[8,2,64,704]{3,2,1,0:T(8,128)(2,1)} %bitcast.36), channel_id=1, source_target_pairs={{0,1},{1,2},{2,3},{4,5},{5,6},{6,7},{8,9},{9,10},{10,11},{12,13},{... | collective-permute-start | bytes 4325384 | tf_op jit(solution)/shard_map/ppermute | solution.py:106
  112.6 21.7 %collective-permute-start.16 = (bf16[256,2048]{1,0:T(8,128)(2,1)S(1)}, bf16[256,2048]{1,0:T(8,128)(2,1)S(1)}, u32[]{:S(2)}, u32[]{:S(2)}) collective-permute-start(bf16[256,2048]{1,0:T(8,128)(2,1)S(1)} %get-tuple-element.259), channel_id=1, source_target_pairs={{0,16},{4,20},{8,24},{12,28},{16,0},{20,4},{24,8},{28,12},{1,17},{... | collective-permute-start | bytes 3145736 | tf_op jit(solution)/shard_map/ppermute | solution.py:223
  114.0 22.1 %collective-permute-start.17 = (bf16[256,2048]{1,0:T(8,128)(2,1)S(1)}, bf16[256,2048]{1,0:T(8,128)(2,1)S(1)}, u32[]{:S(2)}, u32[]{:S(2)}) collective-permute-start(bf16[256,2048]{1,0:T(8,128)(2,1)S(1)} %get-tuple-element.261), channel_id=1, source_target_pairs={{0,8},{4,12},{8,0},{12,4},{16,24},{20,28},{24,16},{28,20},{1,9},{5... | collective-permute-start | bytes 3145736 | tf_op jit(solution)/shard_map/ppermute | solution.py:223
  124.7 38.2 %collective-permute-start.23 = (bf16[8,2,64,704]{3,2,1,0:T(8,128)(2,1)}, bf16[8,2,64,704]{3,2,1,0:T(8,128)(2,1)S(1)}, u32[]{:S(2)}, u32[]{:S(2)}) collective-permute-start(bf16[8,2,64,704]{3,2,1,0:T(8,128)(2,1)} %get-tuple-element.269.refs_5_), channel_id=1, source_target_pairs={{2,1},{1,0},{6,5},{5,4},{10,9},{9,8},{14,13},{13,12},{18,17},{17,1... | collective-permute-start | bytes 4325384 | tf_op jit(solution)/shard_map/ppermute | solution.py:106
  137.8 27.5 %collective-permute-start.20 = (bf16[256,2048]{1,0:T(8,128)(2,1)S(1)}, bf16[256,2048]{1,0:T(8,128)(2,1)S(1)}, u32[]{:S(2)}, u32[]{:S(2)}) collective-permute-start(bf16[256,2048]{1,0:T(8,128)(2,1)S(1)} %get-tuple-element.266), channel_id=1, source_target_pairs={{0,8},{4,12},{8,0},{12,4},{16,24},{20,28},{24,16},{28,20},{1,9},{5... | collective-permute-start | bytes 3145736 | tf_op jit(solution)/shard_map/ppermute | solution.py:223
  139.6 25.7 %collective-permute-start.21 = (bf16[256,2048]{1,0:T(8,128)(2,1)S(1)}, bf16[256,2048]{1,0:T(8,128)(2,1)S(1)}, u32[]{:S(2)}, u32[]{:S(2)}) collective-permute-start(bf16[256,2048]{1,0:T(8,128)(2,1)S(1)} %get-tuple-element.267), channel_id=1, source_target_pairs={{0,16},{4,20},{8,24},{12,28},{16,0},{20,4},{24,8},{28,12},{1,17},{... | collective-permute-start | bytes 3145736 | tf_op jit(solution)/shard_map/ppermute | solution.py:223
  163.0 33.0 %collective-permute-start.28 = (bf16[8,2,64,704]{3,2,1,0:T(8,128)(2,1)S(1)}, bf16[8,2,64,704]{3,2,1,0:T(8,128)(2,1)S(1)}, u32[]{:S(2)}, u32[]{:S(2)}) collective-permute-start(bf16[8,2,64,704]{3,2,1,0:T(8,128)(2,1)S(1)} %get-tuple-element.277.refs_3_), channel_id=1, source_target_pairs={{2,3},{6,7},{10,11},{14,15},{18,19},{22,23},{26,27},{30,31}} | collective-permute-start | bytes 4325384 | tf_op jit(solution)/shard_map/ppermute | solution.py:106
  163.7 33.6 %collective-permute-start.29 = (bf16[8,2,64,704]{3,2,1,0:T(8,128)(2,1)S(1)}, bf16[8,2,64,704]{3,2,1,0:T(8,128)(2,1)S(1)}, u32[]{:S(2)}, u32[]{:S(2)}) collective-permute-start(bf16[8,2,64,704]{3,2,1,0:T(8,128)(2,1)S(1)} %get-tuple-element.278.refs_6_), channel_id=1, source_target_pairs={{1,0},{5,4},{9,8},{13,12},{17,16},{21,20},{25,24},{29,28}} | collective-permute-start | bytes 4325384 | tf_op jit(solution)/shard_map/ppermute | solution.py:106
  171.0 22.4 %collective-permute-start.25 = (bf16[256,2048]{1,0:T(8,128)(2,1)S(1)}, bf16[256,2048]{1,0:T(8,128)(2,1)S(1)}, u32[]{:S(2)}, u32[]{:S(2)}) collective-permute-start(bf16[256,2048]{1,0:T(8,128)(2,1)S(1)} %get-tuple-element.272.refs_0_.refs_1_), channel_id=1, source_target_pairs={{0,16},{4,20},{8,24},{12,28},{16,0},{20,4},{24,8},{28,12},{1,17},{... | collective-permute-start | bytes 3145736 | tf_op jit(solution)/shard_map/ppermute | solution.py:223
  173.0 22.6 %collective-permute-start.24 = (bf16[256,2048]{1,0:T(8,128)(2,1)S(1)}, bf16[256,2048]{1,0:T(8,128)(2,1)S(1)}, u32[]{:S(2)}, u32[]{:S(2)}) collective-permute-start(bf16[256,2048]{1,0:T(8,128)(2,1)S(1)} %get-tuple-element.272.refs_0_.refs_1_), channel_id=1, source_target_pairs={{0,8},{4,12},{8,0},{12,4},{16,24},{20,28},{24,16},{28,20},{1,9},{5... | collective-permute-start | bytes 3145736 | tf_op jit(solution)/shard_map/ppermute | solution.py:223
  175.7 49.6 %collective-permute-start.31 = (bf16[1024,2048]{1,0:T(8,128)(2,1)}, bf16[1024,2048]{1,0:T(8,128)(2,1)}, u32[]{:S(2)}, u32[]{:S(2)}) collective-permute-start(bf16[1024,2048]{1,0:T(8,128)(2,1)} %get-tuple-element.285.refs_1_.refs_2_), channel_id=1, source_target_pairs={{0,4},{4,0},{8,12},{12,8},{16,20},{20,16},{24,28},{28,24},{1,5},{5... | collective-permute-start | bytes 12582920 | tf_op jit(solution)/shard_map/ppermute | solution.py:223
  207.9 17.4 %collective-permute-start.30 = (bf16[1024,2048]{1,0:T(8,128)(2,1)}, bf16[1024,2048]{1,0:T(8,128)(2,1)}, u32[]{:S(2)}, u32[]{:S(2)}) collective-permute-start(bf16[1024,2048]{1,0:T(8,128)(2,1)} %get-tuple-element.284.refs_0_.refs_2_), channel_id=1, source_target_pairs={{0,4},{4,0},{8,12},{12,8},{16,20},{20,16},{24,28},{28,24},{1,5},{5... | collective-permute-start | bytes 12582920 | tf_op jit(solution)/shard_map/ppermute | solution.py:223
  255.2 37.3 %collective-permute-start.35 = (bf16[352,2048]{1,0:T(8,128)(2,1)}, bf16[352,2048]{1,0:T(8,128)(2,1)}, u32[]{:S(2)}, u32[]{:S(2)}) collective-permute-start(bf16[352,2048]{1,0:T(8,128)(2,1)} %copy-done.22), channel_id=1, source_target_pairs={{0,1},{3,2},{4,5},{7,6},{8,9},{11,10},{12,13},{15,14},{16,17},{19,... | collective-permute-start | bytes 4325384 | tf_op jit(solution)/shard_map/ppermute | solution.py:106
  290.1 32.9 %collective-permute-start.33 = (bf16[256,2048]{1,0:T(8,128)(2,1)}, bf16[256,2048]{1,0:T(8,128)(2,1)S(1)}, u32[]{:S(2)}, u32[]{:S(2)}) collective-permute-start(bf16[256,2048]{1,0:T(8,128)(2,1)} %get-tuple-element.305), channel_id=1, source_target_pairs={{0,16},{4,20},{8,24},{12,28},{16,0},{20,4},{24,8},{28,12},{1,17},{... | collective-permute-start | bytes 3145736 | tf_op jit(solution)/shard_map/ppermute | solution.py:223
  291.8 31.2 %collective-permute-start.34 = (bf16[256,2048]{1,0:T(8,128)(2,1)}, bf16[256,2048]{1,0:T(8,128)(2,1)S(1)}, u32[]{:S(2)}, u32[]{:S(2)}) collective-permute-start(bf16[256,2048]{1,0:T(8,128)(2,1)} %get-tuple-element.306), channel_id=1, source_target_pairs={{0,8},{4,12},{8,0},{12,4},{16,24},{20,28},{24,16},{28,20},{1,9},{5... | collective-permute-start | bytes 3145736 | tf_op jit(solution)/shard_map/ppermute | solution.py:223
  295.9 35.2 %collective-permute-start.38 = (bf16[352,2048]{1,0:T(8,128)(2,1)}, bf16[352,2048]{1,0:T(8,128)(2,1)}, u32[]{:S(2)}, u32[]{:S(2)}) collective-permute-start(bf16[352,2048]{1,0:T(8,128)(2,1)} %get-tuple-element.322.refs_2_), channel_id=1, source_target_pairs={{1,2},{2,1},{5,6},{6,5},{9,10},{10,9},{13,14},{14,13},{17,18},{18,... | collective-permute-start | bytes 4325384 | tf_op jit(solution)/shard_map/ppermute | solution.py:106
  297.7 34.9 %collective-permute-start.39 = (bf16[352,2048]{1,0:T(8,128)(2,1)}, bf16[352,2048]{1,0:T(8,128)(2,1)}, u32[]{:S(2)}, u32[]{:S(2)}) collective-permute-start(bf16[352,2048]{1,0:T(8,128)(2,1)} %get-tuple-element.323.refs_4_), channel_id=1, source_target_pairs={{0,1},{3,2},{4,5},{7,6},{8,9},{11,10},{12,13},{15,14},{16,17},{19,... | collective-permute-start | bytes 4325384 | tf_op jit(solution)/shard_map/ppermute | solution.py:106
  337.2 39.7 %collective-permute-start.45 = (bf16[352,2048]{1,0:T(8,128)(2,1)}, bf16[352,2048]{1,0:T(8,128)(2,1)}, u32[]{:S(2)}, u32[]{:S(2)}) collective-permute-start(bf16[352,2048]{1,0:T(8,128)(2,1)} %get-tuple-element.335.refs_2_), channel_id=1, source_target_pairs={{1,0},{2,3},{0,1},{3,2},{5,4},{6,7},{4,5},{7,6},{9,8},{10,11},{8,9... | collective-permute-start | bytes 4325384 | tf_op jit(solution)/shard_map/ppermute | solution.py:106
  339.7 37.2 %collective-permute-start.46 = (bf16[352,2048]{1,0:T(8,128)(2,1)}, bf16[352,2048]{1,0:T(8,128)(2,1)}, u32[]{:S(2)}, u32[]{:S(2)}) collective-permute-start(bf16[352,2048]{1,0:T(8,128)(2,1)} %get-tuple-element.337.refs_2_), channel_id=1, source_target_pairs={{1,2},{2,1},{5,6},{6,5},{9,10},{10,9},{13,14},{14,13},{17,18},{18,... | collective-permute-start | bytes 4325384 | tf_op jit(solution)/shard_map/ppermute | solution.py:106
  349.9 23.5 %collective-permute-start.42 = (bf16[256,2048]{1,0:T(8,128)(2,1)}, bf16[256,2048]{1,0:T(8,128)(2,1)S(1)}, u32[]{:S(2)}, u32[]{:S(2)}) collective-permute-start(bf16[256,2048]{1,0:T(8,128)(2,1)} %get-tuple-element.331.refs_0_.refs_1_), channel_id=1, source_target_pairs={{0,16},{4,20},{8,24},{12,28},{16,0},{20,4},{24,8},{28,12},{1,17},{... | collective-permute-start | bytes 3145736 | tf_op jit(solution)/shard_map/ppermute | solution.py:223
  351.7 23.2 %collective-permute-start.41 = (bf16[256,2048]{1,0:T(8,128)(2,1)}, bf16[256,2048]{1,0:T(8,128)(2,1)S(1)}, u32[]{:S(2)}, u32[]{:S(2)}) collective-permute-start(bf16[256,2048]{1,0:T(8,128)(2,1)} %get-tuple-element.331.refs_0_.refs_1_), channel_id=1, source_target_pairs={{0,8},{4,12},{8,0},{12,4},{16,24},{20,28},{24,16},{28,20},{1,9},{5... | collective-permute-start | bytes 3145736 | tf_op jit(solution)/shard_map/ppermute | solution.py:223
  366.6 66.0 %collective-permute-start.40 = (bf16[1024,2048]{1,0:T(8,128)(2,1)}, bf16[1024,2048]{1,0:T(8,128)(2,1)}, u32[]{:S(2)}, u32[]{:S(2)}) collective-permute-start(bf16[1024,2048]{1,0:T(8,128)(2,1)} %get-tuple-element.330), channel_id=1, source_target_pairs={{0,4},{4,0},{8,12},{12,8},{16,20},{20,16},{24,28},{28,24},{1,5},{5... | collective-permute-start | bytes 12582920 | tf_op jit(solution)/shard_map/ppermute | solution.py:223
  381.5 39.9 %collective-permute-start.49 = (bf16[352,2048]{1,0:T(8,128)(2,1)}, bf16[352,2048]{1,0:T(8,128)(2,1)}, u32[]{:S(2)}, u32[]{:S(2)}) collective-permute-start(bf16[352,2048]{1,0:T(8,128)(2,1)} %get-tuple-element.350.refs_2_), channel_id=1, source_target_pairs={{1,0},{2,3},{0,1},{3,2},{5,4},{6,7},{4,5},{7,6},{9,8},{10,11},{8,9... | collective-permute-start | bytes 4325384 | tf_op jit(solution)/shard_map/ppermute | solution.py:106
  382.9 38.5 %collective-permute-start.50 = (bf16[352,2048]{1,0:T(8,128)(2,1)}, bf16[352,2048]{1,0:T(8,128)(2,1)}, u32[]{:S(2)}, u32[]{:S(2)}) collective-permute-start(bf16[352,2048]{1,0:T(8,128)(2,1)} %get-tuple-element.352.refs_2_), channel_id=1, source_target_pairs={{1,2},{2,1},{5,6},{6,5},{9,10},{10,9},{13,14},{14,13},{17,18},{18,... | collective-permute-start | bytes 4325384 | tf_op jit(solution)/shard_map/ppermute | solution.py:106
  425.9 34.0 %collective-permute-start.53 = (bf16[352,2048]{1,0:T(8,128)(2,1)}, bf16[352,2048]{1,0:T(8,128)(2,1)S(1)}, u32[]{:S(2)}, u32[]{:S(2)}) collective-permute-start(bf16[352,2048]{1,0:T(8,128)(2,1)} %get-tuple-element.358.refs_2_), channel_id=1, source_target_pairs={{1,0},{2,3},{0,1},{3,2},{5,4},{6,7},{4,5},{7,6},{9,8},{10,11},{8,9... | collective-permute-start | bytes 4325384 | tf_op jit(solution)/shard_map/ppermute | solution.py:106
  427.9 32.0 %collective-permute-start.54 = (bf16[352,2048]{1,0:T(8,128)(2,1)}, bf16[352,2048]{1,0:T(8,128)(2,1)}, u32[]{:S(2)}, u32[]{:S(2)}) collective-permute-start(bf16[352,2048]{1,0:T(8,128)(2,1)} %get-tuple-element.360.refs_2_), channel_id=1, source_target_pairs={{1,2},{2,1},{5,6},{6,5},{9,10},{10,9},{13,14},{14,13},{17,18},{18,... | collective-permute-start | bytes 4325384 | tf_op jit(solution)/shard_map/ppermute | solution.py:106
  440.3 47.5 %collective-permute-start.51 = (bf16[512,2048]{1,0:T(8,128)(2,1)}, bf16[512,2048]{1,0:T(8,128)(2,1)S(1)}, u32[]{:S(2)}, u32[]{:S(2)}) collective-permute-start(bf16[512,2048]{1,0:T(8,128)(2,1)} %get-tuple-element.356), channel_id=1, source_target_pairs={{0,16},{4,20},{8,24},{12,28},{16,0},{20,4},{24,8},{28,12},{1,17},{... | collective-permute-start | bytes 6291464 | tf_op jit(solution)/shard_map/ppermute | solution.py:223
  442.0 47.3 %collective-permute-start.52 = (bf16[512,2048]{1,0:T(8,128)(2,1)}, bf16[512,2048]{1,0:T(8,128)(2,1)}, u32[]{:S(2)}, u32[]{:S(2)}) collective-permute-start(bf16[512,2048]{1,0:T(8,128)(2,1)} %get-tuple-element.357), channel_id=1, source_target_pairs={{0,8},{4,12},{8,0},{12,4},{16,24},{20,28},{24,16},{28,20},{1,9},{5... | collective-permute-start | bytes 6291464 | tf_op jit(solution)/shard_map/ppermute | solution.py:223
  465.5 33.8 %collective-permute-start.57 = (bf16[352,2048]{1,0:T(8,128)(2,1)}, bf16[352,2048]{1,0:T(8,128)(2,1)S(1)}, u32[]{:S(2)}, u32[]{:S(2)}) collective-permute-start(bf16[352,2048]{1,0:T(8,128)(2,1)} %get-tuple-element.373.refs_2_), channel_id=1, source_target_pairs={{1,0},{2,3},{0,1},{3,2},{5,4},{6,7},{4,5},{7,6},{9,8},{10,11},{8,9... | collective-permute-start | bytes 4325384 | tf_op jit(solution)/shard_map/ppermute | solution.py:106
  468.2 31.2 %collective-permute-start.58 = (bf16[352,2048]{1,0:T(8,128)(2,1)}, bf16[352,2048]{1,0:T(8,128)(2,1)}, u32[]{:S(2)}, u32[]{:S(2)}) collective-permute-start(bf16[352,2048]{1,0:T(8,128)(2,1)} %get-tuple-element.374.refs_1_), channel_id=1, source_target_pairs={{1,2},{2,1},{5,6},{6,5},{9,10},{10,9},{13,14},{14,13},{17,18},{18,... | collective-permute-start | bytes 4325384 | tf_op jit(solution)/shard_map/ppermute | solution.py:106
  495.6 23.9 %collective-permute-start.55 = (bf16[256,2048]{1,0:T(8,128)(2,1)}, bf16[256,2048]{1,0:T(8,128)(2,1)}, u32[]{:S(2)}, u32[]{:S(2)}) collective-permute-start(bf16[256,2048]{1,0:T(8,128)(2,1)} %get-tuple-element.370), channel_id=1, source_target_pairs={{0,8},{4,12},{8,0},{12,4},{16,24},{20,28},{24,16},{28,20},{1,9},{5... | collective-permute-start | bytes 3145736 | tf_op jit(solution)/shard_map/ppermute | solution.py:223
  497.0 23.7 %collective-permute-start.56 = (bf16[256,2048]{1,0:T(8,128)(2,1)}, bf16[256,2048]{1,0:T(8,128)(2,1)}, u32[]{:S(2)}, u32[]{:S(2)}) collective-permute-start(bf16[256,2048]{1,0:T(8,128)(2,1)} %get-tuple-element.371), channel_id=1, source_target_pairs={{0,16},{4,20},{8,24},{12,28},{16,0},{20,4},{24,8},{28,12},{1,17},{... | collective-permute-start | bytes 3145736 | tf_op jit(solution)/shard_map/ppermute | solution.py:223
  505.2 34.1 %collective-permute-start.59 = (bf16[352,2048]{1,0:T(8,128)(2,1)}, bf16[352,2048]{1,0:T(8,128)(2,1)}, u32[]{:S(2)}, u32[]{:S(2)}) collective-permute-start(bf16[352,2048]{1,0:T(8,128)(2,1)} %get-tuple-element.382.refs_1_), channel_id=1, source_target_pairs={{1,2},{2,1},{5,6},{6,5},{9,10},{10,9},{13,14},{14,13},{17,18},{18,... | collective-permute-start | bytes 4325384 | tf_op jit(solution)/shard_map/ppermute | solution.py:106
  507.0 49.6 %collective-permute-start.67 = (bf16[352,2048]{1,0:T(8,128)(2,1)}, bf16[352,2048]{1,0:T(8,128)(2,1)}, u32[]{:S(2)}, u32[]{:S(2)}) collective-permute-start(bf16[352,2048]{1,0:T(8,128)(2,1)} %get-tuple-element.399.refs_2_), channel_id=1, source_target_pairs={{1,0},{2,3},{5,4},{6,7},{9,8},{10,11},{13,12},{14,15},{17,16},{18,... | collective-permute-start | bytes 4325384 | tf_op jit(solution)/shard_map/ppermute | solution.py:106
  508.3 38.3 %collective-permute-start.60 = (bf16[384,2048]{1,0:T(8,128)(2,1)}, bf16[384,2048]{1,0:T(8,128)(2,1)}, u32[]{:S(2)}, u32[]{:S(2)}) collective-permute-start(bf16[384,2048]{1,0:T(8,128)(2,1)} %get-tuple-element.383.refs_3_), channel_id=1, source_target_pairs={{0,1},{3,2},{4,5},{7,6},{8,9},{11,10},{12,13},{15,14},{16,17},{19,... | collective-permute-start | bytes 4718600 | tf_op jit(solution)/shard_map/ppermute | solution.py:106
  538.1 27.8 %collective-permute-start.64 = (bf16[2,704,256]{2,1,0:T(8,128)(2,1)}, bf16[2,704,256]{2,1,0:T(8,128)(2,1)S(1)}, u32[]{:S(2)}, u32[]{:S(2)}) collective-permute-start(bf16[2,704,256]{2,1,0:T(8,128)(2,1)} %get-tuple-element.394), channel_id=1, source_target_pairs={{0,8},{4,12},{8,0},{12,4},{16,24},{20,28},{24,16},{28,20},{1,9},{5... | collective-permute-start | bytes 2162696 | tf_op jit(solution)/shard_map/ppermute | solution.py:223
  538.7 33.7 %collective-permute-start.65 = (bf16[2,704,256]{2,1,0:T(8,128)(2,1)}, bf16[2,704,256]{2,1,0:T(8,128)(2,1)}, u32[]{:S(2)}, u32[]{:S(2)}) collective-permute-start(bf16[2,704,256]{2,1,0:T(8,128)(2,1)} %get-tuple-element.395), channel_id=1, source_target_pairs={{0,16},{4,20},{8,24},{12,28},{16,0},{20,4},{24,8},{28,12},{1,17},{... | collective-permute-start | bytes 2162696 | tf_op jit(solution)/shard_map/ppermute | solution.py:223
  539.3 33.1 %collective-permute-start.66 = (bf16[2,704,256]{2,1,0:T(8,128)(2,1)}, bf16[2,704,256]{2,1,0:T(8,128)(2,1)}, u32[]{:S(2)}, u32[]{:S(2)}) collective-permute-start(bf16[2,704,256]{2,1,0:T(8,128)(2,1)} %get-tuple-element.396), channel_id=1, source_target_pairs={{0,24},{4,28},{8,16},{12,20},{16,8},{20,12},{24,0},{28,4},{1,25},{... | collective-permute-start | bytes 2162696 | tf_op jit(solution)/shard_map/ppermute | solution.py:223
  551.2 30.6 %collective-permute-start.63 = (bf16[256,2048]{1,0:T(8,128)(2,1)}, bf16[256,2048]{1,0:T(8,128)(2,1)}, u32[]{:S(2)}, u32[]{:S(2)}) collective-permute-start(bf16[256,2048]{1,0:T(8,128)(2,1)} %get-tuple-element.393.refs_3_), channel_id=1, source_target_pairs={{0,1},{3,2},{4,5},{7,6},{8,9},{11,10},{12,13},{15,14},{16,17},{19,... | collective-permute-start | bytes 3145736 | tf_op jit(solution)/shard_map/ppermute | solution.py:106
  556.6 25.2 %collective-permute-start.62 = (bf16[384,2048]{1,0:T(8,128)(2,1)}, bf16[384,2048]{1,0:T(8,128)(2,1)}, u32[]{:S(2)}, u32[]{:S(2)}) collective-permute-start(bf16[384,2048]{1,0:T(8,128)(2,1)} %get-tuple-element.392.refs_1_), channel_id=1, source_target_pairs={{1,2},{2,1},{5,6},{6,5},{9,10},{10,9},{13,14},{14,13},{17,18},{18,... | collective-permute-start | bytes 4718600 | tf_op jit(solution)/shard_map/ppermute | solution.py:106
  565.9 32.3 %collective-permute-start.70 = (bf16[352,2048]{1,0:T(8,128)(2,1)}, bf16[352,2048]{1,0:T(8,128)(2,1)}, u32[]{:S(2)}, u32[]{:S(2)}) collective-permute-start(bf16[352,2048]{1,0:T(8,128)(2,1)} %get-tuple-element.409.refs_2_), channel_id=1, source_target_pairs={{1,0},{2,3},{5,4},{6,7},{9,8},{10,11},{13,12},{14,15},{17,16},{18,... | collective-permute-start | bytes 4325384 | tf_op jit(solution)/shard_map/ppermute | solution.py:106
  585.6 22.0 %collective-permute-start.69 = (bf16[256,2048]{1,0:T(8,128)(2,1)}, bf16[256,2048]{1,0:T(8,128)(2,1)}, u32[]{:S(2)}, u32[]{:S(2)}) collective-permute-start(bf16[256,2048]{1,0:T(8,128)(2,1)} %get-tuple-element.407.refs_1_), channel_id=1, source_target_pairs={{1,2},{2,1},{5,6},{6,5},{9,10},{10,9},{13,14},{14,13},{17,18},{18,... | collective-permute-start | bytes 3145736 | tf_op jit(solution)/shard_map/ppermute | solution.py:106
  602.9 39.4 %collective-permute-start.68 = (bf16[384,2048]{1,0:T(8,128)(2,1)}, bf16[384,2048]{1,0:T(8,128)(2,1)}, u32[]{:S(2)}, u32[]{:S(2)}) collective-permute-start(bf16[384,2048]{1,0:T(8,128)(2,1)} %get-tuple-element.406.refs_2_), channel_id=1, source_target_pairs={{1,0},{2,3},{5,4},{6,7},{9,8},{10,11},{13,12},{14,15},{17,16},{18,... | collective-permute-start | bytes 4718600 | tf_op jit(solution)/shard_map/ppermute | solution.py:106
  610.1 36.8 %collective-permute-start.73 = (bf16[2,704,256]{2,1,0:T(8,128)(2,1)}, bf16[2,704,256]{2,1,0:T(8,128)(2,1)}, u32[]{:S(2)}, u32[]{:S(2)}) collective-permute-start(bf16[2,704,256]{2,1,0:T(8,128)(2,1)} %get-tuple-element.422), channel_id=1, source_target_pairs={{0,8},{4,12},{8,0},{12,4},{16,24},{20,28},{24,16},{28,20},{1,9},{5... | collective-permute-start | bytes 2162696 | tf_op jit(solution)/shard_map/ppermute | solution.py:223
  611.8 35.1 %collective-permute-start.74 = (bf16[2,704,256]{2,1,0:T(8,128)(2,1)}, bf16[2,704,256]{2,1,0:T(8,128)(2,1)}, u32[]{:S(2)}, u32[]{:S(2)}) collective-permute-start(bf16[2,704,256]{2,1,0:T(8,128)(2,1)} %get-tuple-element.423), channel_id=1, source_target_pairs={{0,16},{4,20},{8,24},{12,28},{16,0},{20,4},{24,8},{28,12},{1,17},{... | collective-permute-start | bytes 2162696 | tf_op jit(solution)/shard_map/ppermute | solution.py:223
  613.6 33.3 %collective-permute-start.75 = (bf16[2,704,256]{2,1,0:T(8,128)(2,1)}, bf16[2,704,256]{2,1,0:T(8,128)(2,1)}, u32[]{:S(2)}, u32[]{:S(2)}) collective-permute-start(bf16[2,704,256]{2,1,0:T(8,128)(2,1)} %get-tuple-element.424), channel_id=1, source_target_pairs={{0,24},{4,28},{8,16},{12,20},{16,8},{20,12},{24,0},{28,4},{1,25},{... | collective-permute-start | bytes 2162696 | tf_op jit(solution)/shard_map/ppermute | solution.py:223
  614.0 50.4 %collective-permute-start.79 = (bf16[256,2048]{1,0:T(8,128)(2,1)}, bf16[256,2048]{1,0:T(8,128)(2,1)}, u32[]{:S(2)}, u32[]{:S(2)}) collective-permute-start(bf16[256,2048]{1,0:T(8,128)(2,1)} %get-tuple-element.430.refs_2_), channel_id=1, source_target_pairs={{1,0},{2,3},{5,4},{6,7},{9,8},{10,11},{13,12},{14,15},{17,16},{18,... | collective-permute-start | bytes 3145736 | tf_op jit(solution)/shard_map/ppermute | solution.py:106
  651.2 19.1 %collective-permute-start.76 = (bf16[2,384,256]{2,1,0:T(8,128)(2,1)S(1)}, bf16[2,384,256]{2,1,0:T(8,128)(2,1)S(1)}, u32[]{:S(2)}, u32[]{:S(2)}) collective-permute-start(bf16[2,384,256]{2,1,0:T(8,128)(2,1)S(1)} %get-tuple-element.427), channel_id=1, source_target_pairs={{0,8},{4,12},{8,0},{12,4},{16,24},{20,28},{24,16},{28,20},{1,9},{5... | collective-permute-start | bytes 1179656 | tf_op jit(solution)/shard_map/ppermute | solution.py:223
  653.0 18.9 %collective-permute-start.77 = (bf16[2,384,256]{2,1,0:T(8,128)(2,1)S(1)}, bf16[2,384,256]{2,1,0:T(8,128)(2,1)S(1)}, u32[]{:S(2)}, u32[]{:S(2)}) collective-permute-start(bf16[2,384,256]{2,1,0:T(8,128)(2,1)S(1)} %get-tuple-element.428), channel_id=1, source_target_pairs={{0,16},{4,20},{8,24},{12,28},{16,0},{20,4},{24,8},{28,12},{1,17},{... | collective-permute-start | bytes 1179656 | tf_op jit(solution)/shard_map/ppermute | solution.py:223
  654.7 18.3 %collective-permute-start.78 = (bf16[2,384,256]{2,1,0:T(8,128)(2,1)S(1)}, bf16[2,384,256]{2,1,0:T(8,128)(2,1)S(1)}, u32[]{:S(2)}, u32[]{:S(2)}) collective-permute-start(bf16[2,384,256]{2,1,0:T(8,128)(2,1)S(1)} %get-tuple-element.429), channel_id=1, source_target_pairs={{0,24},{4,28},{8,16},{12,20},{16,8},{20,12},{24,0},{28,4},{1,25},{... | collective-permute-start | bytes 1179656 | tf_op jit(solution)/shard_map/ppermute | solution.py:223
  (79 other events, 441.9 us)

commit v2 on v1

--- a/solution.py
+++ b/solution.py
@@ -159,11 +159,11 @@
 
         results = []
         if jobs:
-            steps = 2 if all(a.shape[0] % 32 == 0 for a in args) else 1
-            specs = [row_blocks(a.shape[0] // steps, a.shape[1]) for a in args]
+            steps = 4
+            specs = [column_blocks(a.shape[0], a.shape[1] // steps) for a in args]
             results = self.clock.call(
                 body, [self.end, *args], [pl.BlockSpec(memory_space=pltpu.SMEM), *specs],
-                outs, [row_blocks(o.shape[0] // steps, o.shape[1]) for o in outs], steps, vmem=60,
+                outs, [column_blocks(o.shape[0], o.shape[1] // steps) for o in outs], steps, vmem=60,
             )
         results = list(results)
         self.going = self.across = self.coming = None
@@ -358,7 +358,7 @@
             [whole_out(o) for o in outs], vmem=40,
         )
 
-    def exchange(self, load, args, a, b):
+    def exchange(self, load, args, a, b, apart=False):
         smem = pl.BlockSpec(memory_space=pltpu.SMEM)
         specs = [smem, *[smem if v.ndim == 1 else whole(v) for v in args]]
         if not self.fast:
@@ -405,9 +405,13 @@
         sends = self.clock.call(
             stack, [kept, come], [whole(kept), whole(come)], [two] * 3, [whole_out(two)] * 3, vmem=24
         )
-        arrived = [self.swap(value, 2 * i + 2) for i, value in enumerate(sends)]
+        arrived = [self.swap(value, 2 * i + 2) for i, value in enumerate(sends[: 2 if apart else 3])]
         self.clock.pause(mib / 2)
         yield
+        if apart:
+            arrived.append(self.swap(self.clock.tie(sends[2]), 6))
+            self.clock.pause(mib / 2)
+            yield
 
         def unpack(me, kept, come, *rest):
             out = rest[-1]
@@ -709,20 +713,26 @@
     )[0]
 
 
-def weight_grad(clock, lefts, rights, parts, block=512):
+def weight_grad(clock, lefts, rights, parts, block=512, part=None):
     rows = lefts[0].shape[0] // parts
+    if part is not None:
+        parts = 1
+    at = part or 0
     width = rights[0].shape[1]
     count = len(lefts)
 
     def body(*refs):
         lefts, rights, outs = refs[:count], refs[count : 2 * count], refs[2 * count :]
         total = sum(dot(a[...], b[...]) for a, b in zip(lefts, rights)).astype(BF16)
-        for at, out in enumerate(outs):
-            out[...] = total[at * rows : (at + 1) * rows]
+        for i, out in enumerate(outs):
+            out[...] = total[i * rows : (i + 1) * rows]
+
+    def left(array):
+        return pl.BlockSpec((rows * parts, array.shape[1]), lambda i: (at, 0), pipeline_mode=pl.Buffered(1))
 
     return clock.call(
         body, [*lefts, *rights],
-        [whole(a) for a in lefts] + [column_blocks(b.shape[0], block) for b in rights],
+        [left(a) for a in lefts] + [column_blocks(b.shape[0], block) for b in rights],
         [shape_of(rows, width)] * parts, [column_blocks(rows, block)] * parts, width // block,
     )
 
@@ -813,17 +823,20 @@
         for at, part in enumerate(parts):
             line.queue(part, functools.partial(results.__setitem__, (name, at)))
 
-    def exchange_back(*parts):
+    def exchange_back(*parts, apart=False):
         def load(refs, j):
             blocks = [ref[:, j * own : (j + 1) * own] for ref in refs]
             return jnp.concatenate(blocks, 0) if len(blocks) > 1 else blocks[0]
 
-        return group.exchange(load, parts, sum(part.shape[0] for part in parts), own)
+        return group.exchange(load, parts, sum(part.shape[0] for part in parts), own, apart)
 
     act_e, dgate_e, dup_e, act_et, dgate_et, dup_et = feed(clock, n2[0], dy[0], wg_mine, wu_mine, wd)
     act_o, dgate_o, dup_o, act_ot, dgate_ot, dup_ot = feed(clock, n2[1], dy[1], wg_mine, wu_mine, wd)
-    sum_copies("down", weight_grad(clock, (act_et, act_ot), dy, 2))
+    first = weight_grad(clock, (act_et, act_ot), dy, 2, part=0)
+    line.queue(first[0], functools.partial(results.__setitem__, ("down", 0)))
     line.tick()
+    second = weight_grad(clock, (act_et, act_ot), dy, 2, part=1)
+    line.queue(second[0], functools.partial(results.__setitem__, ("down", 1)))
     other = group.partner(product(clock, (dgate_o, dup_o), (wg_mine, wu_mine), True))
     part_e = product(clock, (dgate_e, dup_e), (wg_mine, wu_mine), True)
     a2_steps = group.scatter([(part_e, other)])
@@ -880,19 +893,20 @@
     (layer_out,) = group.finish_rows(output, group.terms[1], [h1], [shape_of(rows, width)])
     def tick_until(name, at):
         while (name, at) not in results:
-            line.tick(4)
+            line.tick(0.1)
 
     tick_until("gate", 1)
-    gate_steps = exchange_back(results["gate", 0], results["gate", 1])
-    next(gate_steps)
+    gate_steps = exchange_back(results["gate", 0], results["gate", 1], apart=True)
     next(gate_steps)
     line.tick(4)
+    next(gate_steps)
     down_grad = widen(clock, results["down", 0], results["down", 1])
+    tick_until("up", 1)
+    next(gate_steps, None)
+    up_steps = exchange_back(results["up", 0], results["up", 1])
+    next(up_steps)
     drain(gate_steps)
     gate_grad, gate_sums = feed_weight_grad(clock, group.exchanged, wg, g2)
-    tick_until("up", 1)
-    up_steps = exchange_back(results["up", 0], results["up", 1])
-    next(up_steps)
     next(up_steps)
     tick_until("qkv", 0)
     qkv_steps = exchange_back(results["qkv", 0])

time: 692 us -> 710 us (1.026)
  Pallas kernels: 324 us -> 339 us
    pallas_call x121 -> x124, Pallas kernels: 324 us -> 339 us  [call(): pl.pallas_call(kernel, grid=(steps,), out_shape=(*outs, pltpu.HBM(self.to...]
    ppermute x26, waiting for transfers between devices: 82.9 us -> 96 us  [shift(): return lax.ppermute(value, 'rep', pairs)]
    ppermute x54, waiting for transfers between devices: 107 us -> 99.4 us  [swap(): lax.ppermute(value, 'shard', [(i, i ^ bit) for i in range(self.size)])]
    unnamed x127 -> x131, local copies, waits for them, and re-layouts: 45.9 us -> 46.8 us
  transfers between devices with their start and end apart: 80 -> 80, of which waited for: 38 -> 35; matrix products, arithmetic and copies ran while one was open for 1% -> 1% of each run, Pallas kernels for 43% -> 44%
where the time goes in v2:
time: 710 us; the launch traced here: 696 us
  Pallas kernels  339 us (48%)
  waiting for transfers between devices  195 us (27%)
  starting transfers between devices  106 us (15%)
  local copies, waits for them, and re-layouts  52.3 us (7%)
    pallas_call x124, Pallas kernels, call(): pl.pallas_call(kernel, grid=(steps,), out_shape=(*outs, pltpu.HBM(self.to...  339 us
    ppermute x54, waiting for transfers between devices, swap(): lax.ppermute(value, 'shard', [(i, i ^ bit) for i in range(self.size)])  99.4 us
    ppermute x26, waiting for transfers between devices, shift(): return lax.ppermute(value, 'rep', pairs)  96 us
    ppermute x26, starting transfers between devices, shift(): return lax.ppermute(value, 'rep', pairs)  61.3 us
    unnamed x131, local copies, waits for them, and re-layouts  46.8 us
    ppermute x54, starting transfers between devices, swap(): lax.ppermute(value, 'shard', [(i, i ^ bit) for i in range(self.size)])  44.3 us
  transfers between devices with their start and end apart: 80, of which 35 were waited for; matrix products, arithmetic and copies ran while one was open for 1% of the time, Pallas kernels for 44%

profile of v2, /device:TPU:0, one launch (start us, length us, event | category | flops | bytes accessed | tf_op | source)
XLA Modules:
  0.0 696.0 jit_solution(1413767968511035509)
XLA Ops:
  0.6 3.0 collective-permute-start.1
  12.0 15.0 %collective-permute-done.1.refs_1_.refs_4_.refs_5_ = bf16[256,2048]{1,0:T(8,128)(2,1)S(1)} collective-permute-done((bf16[256,2048]{1,0:T(8,128)(2,1)}, bf16[256,2048]{1,0:T(8,128)(2,1)S(1)}, u32[]{:S(2)}, u32[]{:S(2)}) %collective-permute-start.1) | collective-permute-done | bytes 1048608 | tf_op jit(solution)/shard_map/ppermute | solution.py:223
  45.2 4.2 shard_map.230
  49.6 3.9 collective-permute-done.5.refs_3_
  53.5 6.9 collective-permute-done.7.refs_5_
  69.0 12.0 %shard_map.235 = (bf16[1024,384]{1,0:T(8,128)(2,1)}, f32[1024,128]{1,0:T(8,128)}, bf16[256,1024]{1,0:T(8,128)(2,1)}, bf16[1024,2048]{1,0:T(8,128)(2,1)}, f32[8,128]{1,0:T(8,128)}) custom-call(bf16[1024,2048]{1,0:T(8,128)(2,1)} %collective-permute-done.12.refs_0_.refs_3_, bf16[2048,384]{1,0:T(8,128)(2,1)} %bitcast.21, ...), custom_call_target="tpu_custom_call", output_to_operand_aliasing={{4}: (6, {})} | custom-call | flops 1 | bytes 1 | tf_op jit(solution)/shard_map/pallas_call | solution.py:69
  88.1 5.7 collective-permute-start.18
  93.8 12.0 %shard_map.241 = (bf16[1024,384]{1,0:T(8,128)(2,1)}, f32[1024,128]{1,0:T(8,128)}, bf16[256,1024]{1,0:T(8,128)(2,1)}, bf16[1024,2048]{1,0:T(8,128)(2,1)}, f32[8,128]{1,0:T(8,128)}) custom-call(bf16[1024,2048]{1,0:T(8,128)(2,1)} %get-tuple-element.241.refs_0_.refs_2_, bf16[2048,384]{1,0:T(8,128)(2,1)} %bitcast.22, ...), custom_call_target="tpu_custom_call", output_to_operand_aliasing={{4}: (6, {})} | custom-call | flops 1 | bytes 1 | tf_op jit(solution)/shard_map/pallas_call | solution.py:69
  115.5 7.3 %collective-permute-done.19.refs_1_ = bf16[8,2,64,704]{3,2,1,0:T(8,128)(2,1)} collective-permute-done((bf16[8,2,64,704]{3,2,1,0:T(8,128)(2,1)}, bf16[8,2,64,704]{3,2,1,0:T(8,128)(2,1)}, u32[]{:S(2)}, u32[]{:S(2)}) %collective-permute-start.19) | collective-permute-done | bytes 1441824 | tf_op jit(solution)/shard_map/ppermute | solution.py:106
  126.0 8.3 %collective-permute-done.16.refs_2_ = bf16[256,2048]{1,0:T(8,128)(2,1)S(1)} collective-permute-done((bf16[256,2048]{1,0:T(8,128)(2,1)S(1)}, bf16[256,2048]{1,0:T(8,128)(2,1)S(1)}, u32[]{:S(2)}, u32[]{:S(2)}) %collective-permute-start.16) | collective-permute-done | bytes 1048608 | tf_op jit(solution)/shard_map/ppermute | solution.py:223
  140.1 22.9 %collective-permute-done.23.refs_1_ = bf16[8,2,64,704]{3,2,1,0:T(8,128)(2,1)S(1)} collective-permute-done((bf16[8,2,64,704]{3,2,1,0:T(8,128)(2,1)}, bf16[8,2,64,704]{3,2,1,0:T(8,128)(2,1)S(1)}, u32[]{:S(2)}, u32[]{:S(2)}) %collective-permute-start.23) | collective-permute-done | bytes 1441824 | tf_op jit(solution)/shard_map/ppermute | solution.py:106
  175.7 17.7 %collective-permute-done.25.refs_1_.refs_4_.refs_5_ = bf16[256,2048]{1,0:T(8,128)(2,1)S(1)} collective-permute-done((bf16[256,2048]{1,0:T(8,128)(2,1)S(1)}, bf16[256,2048]{1,0:T(8,128)(2,1)S(1)}, u32[]{:S(2)}, u32[]{:S(2)}) %collective-permute-start.25) | collective-permute-done | bytes 1048608 | tf_op jit(solution)/shard_map/ppermute | solution.py:223
  197.4 4.9 shard_map.258
  207.9 17.3 %shard_map.261 = (bf16[1024,704]{1,0:T(8,128)(2,1)}, bf16[1024,704]{1,0:T(8,128)(2,1)}, bf16[1024,704]{1,0:T(8,128)(2,1)}, bf16[704,1024]{1,0:T(8,128)(2,1)}, bf...) custom-call(bf16[1024,2048]{1,0:T(8,128)(2,1)} %get-tuple-element.287, ...), custom_call_target="tpu_custom_call", output_to_operand_aliasing={{6}: (5, {})} | custom-call | flops 1 | bytes 1 | tf_op jit(solution)/shard_map/pallas_call | solution.py:69
  225.3 17.4 %shard_map.262 = (bf16[1024,704]{1,0:T(8,128)(2,1)}, bf16[1024,704]{1,0:T(8,128)(2,1)}, bf16[1024,704]{1,0:T(8,128)(2,1)}, bf16[704,1024]{1,0:T(8,128)(2,1)}, bf...) custom-call(bf16[1024,2048]{1,0:T(8,128)(2,1)} %collective-permute-do, ...), custom_call_target="tpu_custom_call", output_to_operand_aliasing={{6}: (5, {})} | custom-call | flops 1 | bytes 1 | tf_op jit(solution)/shard_map/pallas_call | solution.py:69
  242.7 7.4 %shard_map.263 = (bf16[352,2048]{1,0:T(8,128)(2,1)}, f32[8,128]{1,0:T(8,128)}) custom-call(bf16[704,1024]{1,0:T(8,128)(2,1)} %get-tuple-element.298.refs_0_, bf16[704,1024]{1,0:T(8,128)(2,1)} %get-tuple-element.299.refs_1_, bf16[1024,2048]{1,0:T(8,128)(2,1)} %get-tuple-element.288.refs_1_.refs_2_, ...), custom_call_target="tpu_custom_call", output_to_operand_aliasing={{1}: (4, {})} | custom-call | flops 1 | bytes 1 | tf_op jit(solution)/shard_map/pallas_call | solution.py:69
  252.5 6.2 collective-permute-start.35
  258.7 7.4 %shard_map.266 = (bf16[352,2048]{1,0:T(8,128)(2,1)}, f32[8,128]{1,0:T(8,128)}) custom-call(bf16[704,1024]{1,0:T(8,128)(2,1)} %get-tuple-element.298.refs_0_, bf16[704,1024]{1,0:T(8,128)(2,1)} %get-tuple-element.299.refs_1_, bf16[1024,2048]{1,0:T(8,128)(2,1)} %get-tuple-element.288.refs_1_.refs_2_, ...), custom_call_target="tpu_custom_call", output_to_operand_aliasing={{1}: (4, {})} | custom-call | flops 1 | bytes 1 | tf_op jit(solution)/shard_map/pallas_call | solution.py:69
  266.1 11.6 %shard_map.267 = (bf16[1024,2048]{1,0:T(8,128)(2,1)}, f32[8,128]{1,0:T(8,128)}) custom-call(bf16[1024,704]{1,0:T(8,128)(2,1)} %get-tuple-element.296.refs_0_, bf16[1024,704]{1,0:T(8,128)(2,1)} %get-tuple-element.297.refs_1_, bf16[2048,704]{1,0:T(8,128)(2,1)} %bitcast.15, bf16[2048,704]{1,0:T(8,128)(2,1)} %bitcast.19, ...), custom_call_target="tpu_custom_call", output_to_operand_aliasing={{1}: (4, {})} | custom-call | flops 1 | bytes 1 | tf_op jit(solution)/shard_map/pallas_call | solution.py:69
  277.9 11.6 %shard_map.269 = (bf16[1024,2048]{1,0:T(8,128)(2,1)}, f32[8,128]{1,0:T(8,128)}) custom-call(bf16[1024,704]{1,0:T(8,128)(2,1)} %get-tuple-element.293.refs_0_, bf16[1024,704]{1,0:T(8,128)(2,1)} %get-tuple-element.294.refs_1_, bf16[2048,704]{1,0:T(8,128)(2,1)} %bitcast.16, bf16[2048,704]{1,0:T(8,128)(2,1)} %bitcast.20, ...), custom_call_target="tpu_custom_call", output_to_operand_aliasing={{1}: (4, {})} | custom-call | flops 1 | bytes 1 | tf_op jit(solution)/shard_map/pallas_call | solution.py:69
  291.7 3.1 shard_map.270
  297.2 4.3 shard_map.272
  305.8 10.0 %shard_map.274 = (bf16[352,2048]{1,0:T(8,128)(2,1)}, bf16[352,2048]{1,0:T(8,128)(2,1)}, f32[8,128]{1,0:T(8,128)}) custom-call(bf16[704,1024]{1,0:T(8,128)(2,1)} %get-tuple-element.313.refs_0_, bf16[704,1024]{1,0:T(8,128)(2,1)} %get-tuple-element.314.refs_1_, bf16[1024,2048]{1,0:T(8,128)(2,1)} %get-tuple-element.287.refs_0_.refs_2_, ...), custom_call_target="tpu_custom_call", output_to_operand_aliasing={{2}: (4, {})} | custom-call | flops 1 | bytes 1 | tf_op jit(solution)/shard_map/pallas_call | solution.py:69
  315.8 10.0 %shard_map.275 = (bf16[352,2048]{1,0:T(8,128)(2,1)}, bf16[352,2048]{1,0:T(8,128)(2,1)}, f32[8,128]{1,0:T(8,128)}) custom-call(bf16[704,1024]{1,0:T(8,128)(2,1)} %get-tuple-element.311.refs_0_, bf16[704,1024]{1,0:T(8,128)(2,1)} %get-tuple-element.312.refs_1_, bf16[1024,2048]{1,0:T(8,128)(2,1)} %get-tuple-element.287.refs_0_.refs_2_, ...), custom_call_target="tpu_custom_call", output_to_operand_aliasing={{2}: (4, {})} | custom-call | flops 1 | bytes 1 | tf_op jit(solution)/shard_map/pallas_call | solution.py:69
  325.9 2.9 copy-done.1
  332.8 3.1 collective-permute-done.39.refs_5_
  335.9 5.4 shard_map.278
  350.4 3.6 shard_map.280
  355.7 7.0 %shard_map.282 = (bf16[1024,2048]{1,0:T(8,128)(2,1)}, f32[8,128]{1,0:T(8,128)}) custom-call(bf16[1024,704]{1,0:T(8,128)(2,1)} %get-tuple-element.292.refs_0_, bf16[704,2048]{1,0:T(8,128)(2,1)} %refs_1_.8, f32[8,128]{1,0:T(8,128)} %shard_map.281.refs_2_), custom_call_target="tpu_custom_call", output_to_operand_aliasing={{1}: (2, {})} | custom-call | flops 1 | bytes 1 | tf_op jit(solution)/shard_map/pallas_call | solution.py:69
  362.7 7.0 %shard_map.283 = (bf16[1024,2048]{1,0:T(8,128)(2,1)}, f32[8,128]{1,0:T(8,128)}) custom-call(bf16[1024,704]{1,0:T(8,128)(2,1)} %get-tuple-element.332.refs_0_, bf16[704,2048]{1,0:T(8,128)(2,1)} %refs_1_.8, f32[8,128]{1,0:T(8,128)} %get-tuple-element.333.refs_2_), custom_call_target="tpu_custom_call", output_to_operand_aliasing={{1}: (2, {})} | custom-call | flops 1 | bytes 1 | tf_op jit(solution)/shard_map/pallas_call | solution.py:69
  369.7 8.4 %collective-permute-done.42.refs_1_.refs_4_.refs_5_ = bf16[256,2048]{1,0:T(8,128)(2,1)S(1)} collective-permute-done((bf16[256,2048]{1,0:T(8,128)(2,1)}, bf16[256,2048]{1,0:T(8,128)(2,1)S(1)}, u32[]{:S(2)}, u32[]{:S(2)}) %collective-permute-start.42) | collective-permute-done | bytes 1048608 | tf_op jit(solution)/shard_map/ppermute | solution.py:223
  382.2 5.2 shard_map.287
  392.4 4.2 shard_map.290
  396.6 14.7 %shard_map.292 = (bf16[384,1024]{1,0:T(8,128)(2,1)}, bf16[1024,2048]{1,0:T(8,128)(2,1)}, f32[8,128]{1,0:T(8,128)}) custom-call(bf16[1024,2048]{1,0:T(8,128)(2,1)} %get-tuple-element.345.refs_0_.refs_2_, bf16[1024,384]{1,0:T(8,128)(2,1)} %get-tuple-element.346.refs_1_, f32[1024,128]{1,0:T(8,128)} %get-tuple-element.347.refs_2_, ...), custom_call_target="tpu_custom_call", output_to_operand_aliasing={{2}: (8, {})} | custom-call | flops 1 | bytes 1 | tf_op jit(solution)/shard_map/pallas_call | solution.py:69
  411.2 14.7 %shard_map.293 = (bf16[384,1024]{1,0:T(8,128)(2,1)}, bf16[1024,2048]{1,0:T(8,128)(2,1)}, f32[8,128]{1,0:T(8,128)}) custom-call(bf16[1024,2048]{1,0:T(8,128)(2,1)} %collective-permute-done.47.refs_0_.refs_3_, bf16[1024,384]{1,0:T(8,128)(2,1)} %get-tuple-element.350.refs_1_, f32[1024,128]{1,0:T(8,128)} %get-tuple-element.351.refs_2_, ...), custom_call_target="tpu_custom_call", output_to_operand_aliasing={{2}: (8, {})} | custom-call | flops 1 | bytes 1 | tf_op jit(solution)/shard_map/pallas_call | solution.py:69
  426.4 5.2 shard_map.295
  440.5 5.5 shard_map.298
  446.9 7.6 %shard_map.300 = (bf16[384,2048]{1,0:T(8,128)(2,1)}, f32[8,128]{1,0:T(8,128)}) custom-call(bf16[384,1024]{1,0:T(8,128)(2,1)} %get-tuple-element.367.refs_0_, bf16[384,1024]{1,0:T(8,128)(2,1)} %get-tuple-element.368.refs_1_, bf16[1024,2048]{1,0:T(8,128)(2,1)} %get-tuple-element.241.refs_0_.refs_2_, ...), custom_call_target="tpu_custom_call", output_to_operand_aliasing={{1}: (4, {})} | custom-call | flops 1 | bytes 1 | tf_op jit(solution)/shard_map/pallas_call | solution.py:69
  454.5 6.5 shard_map.301
  461.0 4.5 collective-permute-done.53.refs_5_.refs_1_
  466.6 5.3 shard_map.302
  471.9 2.8 collective-permute-start.57
  479.2 14.2 %collective-permute-done.51.refs_2_.refs_5_ = bf16[512,2048]{1,0:T(8,128)(2,1)S(1)} collective-permute-done((bf16[512,2048]{1,0:T(8,128)(2,1)}, bf16[512,2048]{1,0:T(8,128)(2,1)S(1)}, u32[]{:S(2)}, u32[]{:S(2)}) %collective-permute-start.51) | collective-permute-done | bytes 2097184 | tf_op jit(solution)/shard_map/ppermute | solution.py:223
  495.8 4.0 shard_map.305
  502.1 3.7 collective-permute-done.57.refs_4_.refs_1_
  507.0 5.6 shard_map.307
  515.6 8.7 %collective-permute-start.60 = (bf16[384,2048]{1,0:T(8,128)(2,1)}, bf16[384,2048]{1,0:T(8,128)(2,1)}, u32[]{:S(2)}, u32[]{:S(2)}) collective-permute-start(bf16[384,2048]{1,0:T(8,128)(2,1)} %get-tuple-element.387.refs_3_), channel_id=1, source_target_pairs={{0,1},{3,2},{4,5},{7,6},{8,9},{11,10},{12,13},{15,14},{16,17},{19,... | collective-permute-start | bytes 4718600 | tf_op jit(solution)/shard_map/ppermute | solution.py:106
  530.9 4.8 shard_map.310
  535.7 3.4 shard_map.311
  540.7 14.6 %collective-permute-done.60.refs_4_ = bf16[384,2048]{1,0:T(8,128)(2,1)} collective-permute-done((bf16[384,2048]{1,0:T(8,128)(2,1)}, bf16[384,2048]{1,0:T(8,128)(2,1)}, u32[]{:S(2)}, u32[]{:S(2)}) %collective-permute-start.60) | collective-permute-done | bytes 1572896 | tf_op jit(solution)/shard_map/ppermute | solution.py:106
  555.3 5.4 shard_map.314
  560.8 5.3 collective-permute-start.62
  574.2 4.8 shard_map.319
  578.9 6.1 collective-permute-done.62.refs_4_
  585.1 4.6 shard_map.320
  589.7 8.9 %collective-permute-done.67.refs_1_ = bf16[352,2048]{1,0:T(8,128)(2,1)} collective-permute-done((bf16[352,2048]{1,0:T(8,128)(2,1)}, bf16[352,2048]{1,0:T(8,128)(2,1)}, u32[]{:S(2)}, u32[]{:S(2)}) %collective-permute-start.67) | collective-permute-done | bytes 1441824 | tf_op jit(solution)/shard_map/ppermute | solution.py:106
  610.0 8.3 %collective-permute-done.71.refs_5_ = bf16[2,704,256]{2,1,0:T(8,128)(2,1)S(1)} collective-permute-done((bf16[2,704,256]{2,1,0:T(8,128)(2,1)}, bf16[2,704,256]{2,1,0:T(8,128)(2,1)S(1)}, u32[]{:S(2)}, u32[]{:S(2)}) %collective-permute-start.71) | collective-permute-done | bytes 720928 | tf_op jit(solution)/shard_map/ppermute | solution.py:223
  621.2 6.5 shard_map.328
  634.0 3.7 shard_map.331
  638.9 19.4 %collective-permute-done.65.refs_1_ = bf16[384,2048]{1,0:T(8,128)(2,1)} collective-permute-done((bf16[384,2048]{1,0:T(8,128)(2,1)}, bf16[384,2048]{1,0:T(8,128)(2,1)}, u32[]{:S(2)}, u32[]{:S(2)}) %collective-permute-start.65) | collective-permute-done | bytes 1572896 | tf_op jit(solution)/shard_map/ppermute | solution.py:106
  670.1 6.4 shard_map.339
  677.5 3.1 collective-permute-done.79.refs_1_
  683.0 3.6 shard_map.342
  689.0 5.0 shard_map.344
  (361 shorter events, 200.2 us)
Async XLA Ops:
  0.6 26.4 %collective-permute-start.1 = (bf16[256,2048]{1,0:T(8,128)(2,1)}, bf16[256,2048]{1,0:T(8,128)(2,1)S(1)}, u32[]{:S(2)}, u32[]{:S(2)}) collective-permute-start(bf16[256,2048]{1,0:T(8,128)(2,1)} %bitcast.25), channel_id=1, source_target_pairs={{0,16},{4,20},{8,24},{12,28},{16,0},{20,4},{24,8},{28,12},{1,17},{... | collective-permute-start | bytes 3145736 | tf_op jit(solution)/shard_map/ppermute | solution.py:223
  3.7 24.8 %collective-permute-start = (bf16[256,2048]{1,0:T(8,128)(2,1)}, bf16[256,2048]{1,0:T(8,128)(2,1)S(1)}, u32[]{:S(2)}, u32[]{:S(2)}) collective-permute-start(bf16[256,2048]{1,0:T(8,128)(2,1)} %bitcast.26), channel_id=1, source_target_pairs={{0,8},{4,12},{8,0},{12,4},{16,24},{20,28},{24,16},{28,20},{1,9},{5... | collective-permute-start | bytes 3145736 | tf_op jit(solution)/shard_map/ppermute | solution.py:223
  10.8 20.7 %collective-permute-start.4 = (bf16[4,256,384]{2,1,0:T(8,128)(2,1)}, bf16[4,256,384]{2,1,0:T(8,128)(2,1)}, u32[]{:S(2)}, u32[]{:S(2)}) collective-permute-start(bf16[4,256,384]{2,1,0:T(8,128)(2,1)} %get-tuple-element.237), channel_id=1, source_target_pairs={{0,4},{4,0},{8,12},{12,8},{16,20},{20,16},{24,28},{28,24},{1,5},{5... | collective-permute-start | bytes 2359304 | tf_op jit(solution)/shard_map/ppermute | solution.py:223
  34.9 18.6 %collective-permute-start.5 = (bf16[2,256,384]{2,1,0:T(8,128)(2,1)}, bf16[2,256,384]{2,1,0:T(8,128)(2,1)}, u32[]{:S(2)}, u32[]{:S(2)}) collective-permute-start(bf16[2,256,384]{2,1,0:T(8,128)(2,1)} %get-tuple-element.242), channel_id=1, source_target_pairs={{0,8},{4,12},{8,0},{12,4},{16,24},{20,28},{24,16},{28,20},{1,9},{5... | collective-permute-start | bytes 1179656 | tf_op jit(solution)/shard_map/ppermute | solution.py:223
  35.3 18.2 %collective-permute-start.6 = (bf16[2,256,384]{2,1,0:T(8,128)(2,1)}, bf16[2,256,384]{2,1,0:T(8,128)(2,1)}, u32[]{:S(2)}, u32[]{:S(2)}) collective-permute-start(bf16[2,256,384]{2,1,0:T(8,128)(2,1)} %get-tuple-element.243), channel_id=1, source_target_pairs={{0,16},{4,20},{8,24},{12,28},{16,0},{20,4},{24,8},{28,12},{1,17},{... | collective-permute-start | bytes 1179656 | tf_op jit(solution)/shard_map/ppermute | solution.py:223
  37.0 23.4 %collective-permute-start.7 = (bf16[2,256,384]{2,1,0:T(8,128)(2,1)}, bf16[2,256,384]{2,1,0:T(8,128)(2,1)}, u32[]{:S(2)}, u32[]{:S(2)}) collective-permute-start(bf16[2,256,384]{2,1,0:T(8,128)(2,1)} %get-tuple-element.244), channel_id=1, source_target_pairs={{0,24},{4,28},{8,16},{12,20},{16,8},{20,12},{24,0},{28,4},{1,25},{... | collective-permute-start | bytes 1179656 | tf_op jit(solution)/shard_map/ppermute | solution.py:223
  44.9 18.1 %collective-permute-start.8 = (bf16[4,128,704]{1,2,0:T(8,128)(2,1)S(1)}, bf16[4,128,704]{1,2,0:T(8,128)(2,1)}, u32[]{:S(2)}, u32[]{:S(2)}) collective-permute-start(bf16[4,128,704]{1,2,0:T(8,128)(2,1)S(1)} %copy-done.59), channel_id=1, source_target_pairs={{0,4},{4,0},{8,12},{12,8},{16,20},{20,16},{24,28},{28,24},{1,5},{5... | collective-permute-start | bytes 2162696 | tf_op jit(solution)/shard_map/ppermute | solution.py:223
  49.4 19.6 %collective-permute-start.12 = (bf16[1024,2048]{1,0:T(8,128)(2,1)}, bf16[1024,2048]{1,0:T(8,128)(2,1)}, u32[]{:S(2)}, u32[]{:S(2)}) collective-permute-start(bf16[1024,2048]{1,0:T(8,128)(2,1)} %get-tuple-element.241.refs_0_.refs_2_), channel_id=1, source_target_pairs={{0,4},{4,0},{8,12},{12,8},{16,20},{20,16},{24,28},{28,24},{1,5},{5... | collective-permute-start | bytes 12582920 | tf_op jit(solution)/shard_map/ppermute | solution.py:223
  67.0 16.8 %collective-permute-start.10 = (bf16[2,128,704]{2,1,0:T(8,128)(2,1)}, bf16[2,128,704]{2,1,0:T(8,128)(2,1)S(1)}, u32[]{:S(2)}, u32[]{:S(2)}) collective-permute-start(bf16[2,128,704]{2,1,0:T(8,128)(2,1)} %get-tuple-element.251), channel_id=1, source_target_pairs={{0,16},{4,20},{8,24},{12,28},{16,0},{20,4},{24,8},{28,12},{1,17},{... | collective-permute-start | bytes 1081352 | tf_op jit(solution)/shard_map/ppermute | solution.py:223
  81.0 27.5 %collective-permute-start.13 = (bf16[1024,2048]{1,0:T(8,128)(2,1)}, bf16[1024,2048]{1,0:T(8,128)(2,1)}, u32[]{:S(2)}, u32[]{:S(2)}) collective-permute-start(bf16[1024,2048]{1,0:T(8,128)(2,1)} %get-tuple-element.258), channel_id=1, source_target_pairs={{0,4},{4,0},{8,12},{12,8},{16,20},{20,16},{24,28},{28,24},{1,5},{5... | collective-permute-start | bytes 12582920 | tf_op jit(solution)/shard_map/ppermute | solution.py:223
  85.0 23.0 %collective-permute-start.15 = (bf16[256,2048]{1,0:T(8,128)(2,1)}, bf16[256,2048]{1,0:T(8,128)(2,1)S(1)}, u32[]{:S(2)}, u32[]{:S(2)}) collective-permute-start(bf16[256,2048]{1,0:T(8,128)(2,1)} %get-tuple-element.259), channel_id=1, source_target_pairs={{0,16},{4,20},{8,24},{12,28},{16,0},{20,4},{24,8},{28,12},{1,17},{... | collective-permute-start | bytes 3145736 | tf_op jit(solution)/shard_map/ppermute | solution.py:223
  85.7 22.7 %collective-permute-start.14 = (bf16[256,2048]{1,0:T(8,128)(2,1)}, bf16[256,2048]{1,0:T(8,128)(2,1)S(1)}, u32[]{:S(2)}, u32[]{:S(2)}) collective-permute-start(bf16[256,2048]{1,0:T(8,128)(2,1)} %get-tuple-element.259), channel_id=1, source_target_pairs={{0,8},{4,12},{8,0},{12,4},{16,24},{20,28},{24,16},{28,20},{1,9},{5... | collective-permute-start | bytes 3145736 | tf_op jit(solution)/shard_map/ppermute | solution.py:223
  86.8 36.0 %collective-permute-start.19 = (bf16[8,2,64,704]{3,2,1,0:T(8,128)(2,1)}, bf16[8,2,64,704]{3,2,1,0:T(8,128)(2,1)}, u32[]{:S(2)}, u32[]{:S(2)}) collective-permute-start(bf16[8,2,64,704]{3,2,1,0:T(8,128)(2,1)} %bitcast.35), channel_id=1, source_target_pairs={{3,2},{2,1},{1,0},{7,6},{6,5},{5,4},{11,10},{10,9},{9,8},{15,14},{... | collective-permute-start | bytes 4325384 | tf_op jit(solution)/shard_map/ppermute | solution.py:106
  88.1 35.9 %collective-permute-start.18 = (bf16[8,2,64,704]{3,2,1,0:T(8,128)(2,1)}, bf16[8,2,64,704]{3,2,1,0:T(8,128)(2,1)}, u32[]{:S(2)}, u32[]{:S(2)}) collective-permute-start(bf16[8,2,64,704]{3,2,1,0:T(8,128)(2,1)} %bitcast.36), channel_id=1, source_target_pairs={{0,1},{1,2},{2,3},{4,5},{5,6},{6,7},{8,9},{9,10},{10,11},{12,13},{... | collective-permute-start | bytes 4325384 | tf_op jit(solution)/shard_map/ppermute | solution.py:106
  112.6 21.7 %collective-permute-start.16 = (bf16[256,2048]{1,0:T(8,128)(2,1)S(1)}, bf16[256,2048]{1,0:T(8,128)(2,1)S(1)}, u32[]{:S(2)}, u32[]{:S(2)}) collective-permute-start(bf16[256,2048]{1,0:T(8,128)(2,1)S(1)} %get-tuple-element.262), channel_id=1, source_target_pairs={{0,16},{4,20},{8,24},{12,28},{16,0},{20,4},{24,8},{28,12},{1,17},{... | collective-permute-start | bytes 3145736 | tf_op jit(solution)/shard_map/ppermute | solution.py:223
  114.0 22.1 %collective-permute-start.17 = (bf16[256,2048]{1,0:T(8,128)(2,1)S(1)}, bf16[256,2048]{1,0:T(8,128)(2,1)S(1)}, u32[]{:S(2)}, u32[]{:S(2)}) collective-permute-start(bf16[256,2048]{1,0:T(8,128)(2,1)S(1)} %get-tuple-element.264), channel_id=1, source_target_pairs={{0,8},{4,12},{8,0},{12,4},{16,24},{20,28},{24,16},{28,20},{1,9},{5... | collective-permute-start | bytes 3145736 | tf_op jit(solution)/shard_map/ppermute | solution.py:223
  124.7 38.3 %collective-permute-start.23 = (bf16[8,2,64,704]{3,2,1,0:T(8,128)(2,1)}, bf16[8,2,64,704]{3,2,1,0:T(8,128)(2,1)S(1)}, u32[]{:S(2)}, u32[]{:S(2)}) collective-permute-start(bf16[8,2,64,704]{3,2,1,0:T(8,128)(2,1)} %get-tuple-element.272.refs_5_), channel_id=1, source_target_pairs={{2,1},{1,0},{6,5},{5,4},{10,9},{9,8},{14,13},{13,12},{18,17},{17,1... | collective-permute-start | bytes 4325384 | tf_op jit(solution)/shard_map/ppermute | solution.py:106
  137.8 27.5 %collective-permute-start.20 = (bf16[256,2048]{1,0:T(8,128)(2,1)S(1)}, bf16[256,2048]{1,0:T(8,128)(2,1)S(1)}, u32[]{:S(2)}, u32[]{:S(2)}) collective-permute-start(bf16[256,2048]{1,0:T(8,128)(2,1)S(1)} %get-tuple-element.269), channel_id=1, source_target_pairs={{0,8},{4,12},{8,0},{12,4},{16,24},{20,28},{24,16},{28,20},{1,9},{5... | collective-permute-start | bytes 3145736 | tf_op jit(solution)/shard_map/ppermute | solution.py:223
  139.6 25.7 %collective-permute-start.21 = (bf16[256,2048]{1,0:T(8,128)(2,1)S(1)}, bf16[256,2048]{1,0:T(8,128)(2,1)S(1)}, u32[]{:S(2)}, u32[]{:S(2)}) collective-permute-start(bf16[256,2048]{1,0:T(8,128)(2,1)S(1)} %get-tuple-element.270), channel_id=1, source_target_pairs={{0,16},{4,20},{8,24},{12,28},{16,0},{20,4},{24,8},{28,12},{1,17},{... | collective-permute-start | bytes 3145736 | tf_op jit(solution)/shard_map/ppermute | solution.py:223
  163.0 33.0 %collective-permute-start.28 = (bf16[8,2,64,704]{3,2,1,0:T(8,128)(2,1)S(1)}, bf16[8,2,64,704]{3,2,1,0:T(8,128)(2,1)S(1)}, u32[]{:S(2)}, u32[]{:S(2)}) collective-permute-start(bf16[8,2,64,704]{3,2,1,0:T(8,128)(2,1)S(1)} %get-tuple-element.280.refs_3_), channel_id=1, source_target_pairs={{2,3},{6,7},{10,11},{14,15},{18,19},{22,23},{26,27},{30,31}} | collective-permute-start | bytes 4325384 | tf_op jit(solution)/shard_map/ppermute | solution.py:106
  163.8 33.6 %collective-permute-start.29 = (bf16[8,2,64,704]{3,2,1,0:T(8,128)(2,1)S(1)}, bf16[8,2,64,704]{3,2,1,0:T(8,128)(2,1)S(1)}, u32[]{:S(2)}, u32[]{:S(2)}) collective-permute-start(bf16[8,2,64,704]{3,2,1,0:T(8,128)(2,1)S(1)} %get-tuple-element.281.refs_6_), channel_id=1, source_target_pairs={{1,0},{5,4},{9,8},{13,12},{17,16},{21,20},{25,24},{29,28}} | collective-permute-start | bytes 4325384 | tf_op jit(solution)/shard_map/ppermute | solution.py:106
  171.0 22.4 %collective-permute-start.25 = (bf16[256,2048]{1,0:T(8,128)(2,1)S(1)}, bf16[256,2048]{1,0:T(8,128)(2,1)S(1)}, u32[]{:S(2)}, u32[]{:S(2)}) collective-permute-start(bf16[256,2048]{1,0:T(8,128)(2,1)S(1)} %get-tuple-element.275.refs_0_.refs_1_), channel_id=1, source_target_pairs={{0,16},{4,20},{8,24},{12,28},{16,0},{20,4},{24,8},{28,12},{1,17},{... | collective-permute-start | bytes 3145736 | tf_op jit(solution)/shard_map/ppermute | solution.py:223
  173.0 22.6 %collective-permute-start.24 = (bf16[256,2048]{1,0:T(8,128)(2,1)S(1)}, bf16[256,2048]{1,0:T(8,128)(2,1)S(1)}, u32[]{:S(2)}, u32[]{:S(2)}) collective-permute-start(bf16[256,2048]{1,0:T(8,128)(2,1)S(1)} %get-tuple-element.275.refs_0_.refs_1_), channel_id=1, source_target_pairs={{0,8},{4,12},{8,0},{12,4},{16,24},{20,28},{24,16},{28,20},{1,9},{5... | collective-permute-start | bytes 3145736 | tf_op jit(solution)/shard_map/ppermute | solution.py:223
  175.7 49.5 %collective-permute-start.31 = (bf16[1024,2048]{1,0:T(8,128)(2,1)}, bf16[1024,2048]{1,0:T(8,128)(2,1)}, u32[]{:S(2)}, u32[]{:S(2)}) collective-permute-start(bf16[1024,2048]{1,0:T(8,128)(2,1)} %get-tuple-element.288.refs_1_.refs_2_), channel_id=1, source_target_pairs={{0,4},{4,0},{8,12},{12,8},{16,20},{20,16},{24,28},{28,24},{1,5},{5... | collective-permute-start | bytes 12582920 | tf_op jit(solution)/shard_map/ppermute | solution.py:223
  207.9 17.4 %collective-permute-start.30 = (bf16[1024,2048]{1,0:T(8,128)(2,1)}, bf16[1024,2048]{1,0:T(8,128)(2,1)}, u32[]{:S(2)}, u32[]{:S(2)}) collective-permute-start(bf16[1024,2048]{1,0:T(8,128)(2,1)} %get-tuple-element.287.refs_0_.refs_2_), channel_id=1, source_target_pairs={{0,4},{4,0},{8,12},{12,8},{16,20},{20,16},{24,28},{28,24},{1,5},{5... | collective-permute-start | bytes 12582920 | tf_op jit(solution)/shard_map/ppermute | solution.py:223
  252.5 44.7 %collective-permute-start.35 = (bf16[352,2048]{1,0:T(8,128)(2,1)}, bf16[352,2048]{1,0:T(8,128)(2,1)}, u32[]{:S(2)}, u32[]{:S(2)}) collective-permute-start(bf16[352,2048]{1,0:T(8,128)(2,1)} %copy-done.24), channel_id=1, source_target_pairs={{0,1},{3,2},{4,5},{7,6},{8,9},{11,10},{12,13},{15,14},{16,17},{19,... | collective-permute-start | bytes 4325384 | tf_op jit(solution)/shard_map/ppermute | solution.py:106
  294.8 31.0 %collective-permute-start.33 = (bf16[256,2048]{1,0:T(8,128)(2,1)}, bf16[256,2048]{1,0:T(8,128)(2,1)S(1)}, u32[]{:S(2)}, u32[]{:S(2)}) collective-permute-start(bf16[256,2048]{1,0:T(8,128)(2,1)} %get-tuple-element.309), channel_id=1, source_target_pairs={{0,16},{4,20},{8,24},{12,28},{16,0},{20,4},{24,8},{28,12},{1,17},{... | collective-permute-start | bytes 3145736 | tf_op jit(solution)/shard_map/ppermute | solution.py:223
  296.6 29.3 %collective-permute-start.34 = (bf16[256,2048]{1,0:T(8,128)(2,1)}, bf16[256,2048]{1,0:T(8,128)(2,1)S(1)}, u32[]{:S(2)}, u32[]{:S(2)}) collective-permute-start(bf16[256,2048]{1,0:T(8,128)(2,1)} %get-tuple-element.310), channel_id=1, source_target_pairs={{0,8},{4,12},{8,0},{12,4},{16,24},{20,28},{24,16},{28,20},{1,9},{5... | collective-permute-start | bytes 3145736 | tf_op jit(solution)/shard_map/ppermute | solution.py:223
  301.5 31.3 %collective-permute-start.38 = (bf16[352,2048]{1,0:T(8,128)(2,1)}, bf16[352,2048]{1,0:T(8,128)(2,1)}, u32[]{:S(2)}, u32[]{:S(2)}) collective-permute-start(bf16[352,2048]{1,0:T(8,128)(2,1)} %get-tuple-element.326.refs_2_), channel_id=1, source_target_pairs={{1,2},{2,1},{5,6},{6,5},{9,10},{10,9},{13,14},{14,13},{17,18},{18,... | collective-permute-start | bytes 4325384 | tf_op jit(solution)/shard_map/ppermute | solution.py:106
  303.3 32.6 %collective-permute-start.39 = (bf16[352,2048]{1,0:T(8,128)(2,1)}, bf16[352,2048]{1,0:T(8,128)(2,1)}, u32[]{:S(2)}, u32[]{:S(2)}) collective-permute-start(bf16[352,2048]{1,0:T(8,128)(2,1)} %get-tuple-element.327.refs_4_), channel_id=1, source_target_pairs={{0,1},{3,2},{4,5},{7,6},{8,9},{11,10},{12,13},{15,14},{16,17},{19,... | collective-permute-start | bytes 4325384 | tf_op jit(solution)/shard_map/ppermute | solution.py:106
  341.3 40.9 %collective-permute-start.45 = (bf16[352,2048]{1,0:T(8,128)(2,1)}, bf16[352,2048]{1,0:T(8,128)(2,1)}, u32[]{:S(2)}, u32[]{:S(2)}) collective-permute-start(bf16[352,2048]{1,0:T(8,128)(2,1)} %get-tuple-element.339.refs_2_), channel_id=1, source_target_pairs={{1,0},{2,3},{0,1},{3,2},{5,4},{6,7},{4,5},{7,6},{9,8},{10,11},{8,9... | collective-permute-start | bytes 4325384 | tf_op jit(solution)/shard_map/ppermute | solution.py:106
  343.8 38.4 %collective-permute-start.46 = (bf16[352,2048]{1,0:T(8,128)(2,1)}, bf16[352,2048]{1,0:T(8,128)(2,1)}, u32[]{:S(2)}, u32[]{:S(2)}) collective-permute-start(bf16[352,2048]{1,0:T(8,128)(2,1)} %get-tuple-element.341.refs_2_), channel_id=1, source_target_pairs={{1,2},{2,1},{5,6},{6,5},{9,10},{10,9},{13,14},{14,13},{17,18},{18,... | collective-permute-start | bytes 4325384 | tf_op jit(solution)/shard_map/ppermute | solution.py:106
  354.0 24.1 %collective-permute-start.42 = (bf16[256,2048]{1,0:T(8,128)(2,1)}, bf16[256,2048]{1,0:T(8,128)(2,1)S(1)}, u32[]{:S(2)}, u32[]{:S(2)}) collective-permute-start(bf16[256,2048]{1,0:T(8,128)(2,1)} %get-tuple-element.335.refs_0_.refs_1_), channel_id=1, source_target_pairs={{0,16},{4,20},{8,24},{12,28},{16,0},{20,4},{24,8},{28,12},{1,17},{... | collective-permute-start | bytes 3145736 | tf_op jit(solution)/shard_map/ppermute | solution.py:223
  354.3 23.9 %collective-permute-start.41 = (bf16[256,2048]{1,0:T(8,128)(2,1)}, bf16[256,2048]{1,0:T(8,128)(2,1)S(1)}, u32[]{:S(2)}, u32[]{:S(2)}) collective-permute-start(bf16[256,2048]{1,0:T(8,128)(2,1)} %get-tuple-element.335.refs_0_.refs_1_), channel_id=1, source_target_pairs={{0,8},{4,12},{8,0},{12,4},{16,24},{20,28},{24,16},{28,20},{1,9},{5... | collective-permute-start | bytes 3145736 | tf_op jit(solution)/shard_map/ppermute | solution.py:223
  369.7 68.6 %collective-permute-start.40 = (bf16[1024,2048]{1,0:T(8,128)(2,1)}, bf16[1024,2048]{1,0:T(8,128)(2,1)}, u32[]{:S(2)}, u32[]{:S(2)}) collective-permute-start(bf16[1024,2048]{1,0:T(8,128)(2,1)} %get-tuple-element.334), channel_id=1, source_target_pairs={{0,4},{4,0},{8,12},{12,8},{16,20},{20,16},{24,28},{28,24},{1,5},{5... | collective-permute-start | bytes 12582920 | tf_op jit(solution)/shard_map/ppermute | solution.py:223
  387.4 39.0 %collective-permute-start.49 = (bf16[352,2048]{1,0:T(8,128)(2,1)}, bf16[352,2048]{1,0:T(8,128)(2,1)}, u32[]{:S(2)}, u32[]{:S(2)}) collective-permute-start(bf16[352,2048]{1,0:T(8,128)(2,1)} %get-tuple-element.354.refs_2_), channel_id=1, source_target_pairs={{1,0},{2,3},{0,1},{3,2},{5,4},{6,7},{4,5},{7,6},{9,8},{10,11},{8,9... | collective-permute-start | bytes 4325384 | tf_op jit(solution)/shard_map/ppermute | solution.py:106
  387.9 38.5 %collective-permute-start.50 = (bf16[352,2048]{1,0:T(8,128)(2,1)}, bf16[352,2048]{1,0:T(8,128)(2,1)}, u32[]{:S(2)}, u32[]{:S(2)}) collective-permute-start(bf16[352,2048]{1,0:T(8,128)(2,1)} %get-tuple-element.356.refs_2_), channel_id=1, source_target_pairs={{1,2},{2,1},{5,6},{6,5},{9,10},{10,9},{13,14},{14,13},{17,18},{18,... | collective-permute-start | bytes 4325384 | tf_op jit(solution)/shard_map/ppermute | solution.py:106
  431.6 33.9 %collective-permute-start.53 = (bf16[352,2048]{1,0:T(8,128)(2,1)}, bf16[352,2048]{1,0:T(8,128)(2,1)S(1)}, u32[]{:S(2)}, u32[]{:S(2)}) collective-permute-start(bf16[352,2048]{1,0:T(8,128)(2,1)} %get-tuple-element.362.refs_2_), channel_id=1, source_target_pairs={{1,0},{2,3},{0,1},{3,2},{5,4},{6,7},{4,5},{7,6},{9,8},{10,11},{8,9... | collective-permute-start | bytes 4325384 | tf_op jit(solution)/shard_map/ppermute | solution.py:106
  433.5 32.0 %collective-permute-start.54 = (bf16[352,2048]{1,0:T(8,128)(2,1)}, bf16[352,2048]{1,0:T(8,128)(2,1)}, u32[]{:S(2)}, u32[]{:S(2)}) collective-permute-start(bf16[352,2048]{1,0:T(8,128)(2,1)} %get-tuple-element.364.refs_2_), channel_id=1, source_target_pairs={{1,2},{2,1},{5,6},{6,5},{9,10},{10,9},{13,14},{14,13},{17,18},{18,... | collective-permute-start | bytes 4325384 | tf_op jit(solution)/shard_map/ppermute | solution.py:106
  446.0 47.5 %collective-permute-start.51 = (bf16[512,2048]{1,0:T(8,128)(2,1)}, bf16[512,2048]{1,0:T(8,128)(2,1)S(1)}, u32[]{:S(2)}, u32[]{:S(2)}) collective-permute-start(bf16[512,2048]{1,0:T(8,128)(2,1)} %get-tuple-element.360), channel_id=1, source_target_pairs={{0,16},{4,20},{8,24},{12,28},{16,0},{20,4},{24,8},{28,12},{1,17},{... | collective-permute-start | bytes 6291464 | tf_op jit(solution)/shard_map/ppermute | solution.py:223
  446.2 47.3 %collective-permute-start.52 = (bf16[512,2048]{1,0:T(8,128)(2,1)}, bf16[512,2048]{1,0:T(8,128)(2,1)}, u32[]{:S(2)}, u32[]{:S(2)}) collective-permute-start(bf16[512,2048]{1,0:T(8,128)(2,1)} %get-tuple-element.361), channel_id=1, source_target_pairs={{0,8},{4,12},{8,0},{12,4},{16,24},{20,28},{24,16},{28,20},{1,9},{5... | collective-permute-start | bytes 6291464 | tf_op jit(solution)/shard_map/ppermute | solution.py:223
  471.9 34.0 %collective-permute-start.57 = (bf16[352,2048]{1,0:T(8,128)(2,1)}, bf16[352,2048]{1,0:T(8,128)(2,1)S(1)}, u32[]{:S(2)}, u32[]{:S(2)}) collective-permute-start(bf16[352,2048]{1,0:T(8,128)(2,1)} %get-tuple-element.377.refs_2_), channel_id=1, source_target_pairs={{1,0},{2,3},{0,1},{3,2},{5,4},{6,7},{4,5},{7,6},{9,8},{10,11},{8,9... | collective-permute-start | bytes 4325384 | tf_op jit(solution)/shard_map/ppermute | solution.py:106
  474.7 31.2 %collective-permute-start.58 = (bf16[352,2048]{1,0:T(8,128)(2,1)}, bf16[352,2048]{1,0:T(8,128)(2,1)}, u32[]{:S(2)}, u32[]{:S(2)}) collective-permute-start(bf16[352,2048]{1,0:T(8,128)(2,1)} %get-tuple-element.378.refs_1_), channel_id=1, source_target_pairs={{1,2},{2,1},{5,6},{6,5},{9,10},{10,9},{13,14},{14,13},{17,18},{18,... | collective-permute-start | bytes 4325384 | tf_op jit(solution)/shard_map/ppermute | solution.py:106
  499.8 27.3 %collective-permute-start.55 = (bf16[256,2048]{1,0:T(8,128)(2,1)}, bf16[256,2048]{1,0:T(8,128)(2,1)}, u32[]{:S(2)}, u32[]{:S(2)}) collective-permute-start(bf16[256,2048]{1,0:T(8,128)(2,1)} %get-tuple-element.374), channel_id=1, source_target_pairs={{0,8},{4,12},{8,0},{12,4},{16,24},{20,28},{24,16},{28,20},{1,9},{5... | collective-permute-start | bytes 3145736 | tf_op jit(solution)/shard_map/ppermute | solution.py:223
  500.4 26.7 %collective-permute-start.56 = (bf16[256,2048]{1,0:T(8,128)(2,1)}, bf16[256,2048]{1,0:T(8,128)(2,1)}, u32[]{:S(2)}, u32[]{:S(2)}) collective-permute-start(bf16[256,2048]{1,0:T(8,128)(2,1)} %get-tuple-element.375), channel_id=1, source_target_pairs={{0,16},{4,20},{8,24},{12,28},{16,0},{20,4},{24,8},{28,12},{1,17},{... | collective-permute-start | bytes 3145736 | tf_op jit(solution)/shard_map/ppermute | solution.py:223
  512.5 28.2 %collective-permute-start.59 = (bf16[352,2048]{1,0:T(8,128)(2,1)}, bf16[352,2048]{1,0:T(8,128)(2,1)}, u32[]{:S(2)}, u32[]{:S(2)}) collective-permute-start(bf16[352,2048]{1,0:T(8,128)(2,1)} %get-tuple-element.386.refs_1_), channel_id=1, source_target_pairs={{1,2},{2,1},{5,6},{6,5},{9,10},{10,9},{13,14},{14,13},{17,18},{18,... | collective-permute-start | bytes 4325384 | tf_op jit(solution)/shard_map/ppermute | solution.py:106
  514.3 54.9 %collective-permute-start.64 = (bf16[352,2048]{1,0:T(8,128)(2,1)}, bf16[352,2048]{1,0:T(8,128)(2,1)}, u32[]{:S(2)}, u32[]{:S(2)}) collective-permute-start(bf16[352,2048]{1,0:T(8,128)(2,1)} %get-tuple-element.399.refs_2_), channel_id=1, source_target_pairs={{1,0},{2,3},{5,4},{6,7},{9,8},{10,11},{13,12},{14,15},{17,16},{18,... | collective-permute-start | bytes 4325384 | tf_op jit(solution)/shard_map/ppermute | solution.py:106
  515.6 39.7 %collective-permute-start.60 = (bf16[384,2048]{1,0:T(8,128)(2,1)}, bf16[384,2048]{1,0:T(8,128)(2,1)}, u32[]{:S(2)}, u32[]{:S(2)}) collective-permute-start(bf16[384,2048]{1,0:T(8,128)(2,1)} %get-tuple-element.387.refs_3_), channel_id=1, source_target_pairs={{0,1},{3,2},{4,5},{7,6},{8,9},{11,10},{12,13},{15,14},{16,17},{19,... | collective-permute-start | bytes 4718600 | tf_op jit(solution)/shard_map/ppermute | solution.py:106
  540.7 31.3 %collective-permute-start.63 = (bf16[4,704,256]{2,1,0:T(8,128)(2,1)}, bf16[4,704,256]{2,1,0:T(8,128)(2,1)S(1)}, u32[]{:S(2)}, u32[]{:S(2)}) collective-permute-start(bf16[4,704,256]{2,1,0:T(8,128)(2,1)} %get-tuple-element.398), channel_id=1, source_target_pairs={{0,4},{4,0},{8,12},{12,8},{16,20},{20,16},{24,28},{28,24},{1,5},{5... | collective-permute-start | bytes 4325384 | tf_op jit(solution)/shard_map/ppermute | solution.py:223
  560.8 24.3 %collective-permute-start.62 = (bf16[256,2048]{1,0:T(8,128)(2,1)}, bf16[256,2048]{1,0:T(8,128)(2,1)}, u32[]{:S(2)}, u32[]{:S(2)}) collective-permute-start(bf16[256,2048]{1,0:T(8,128)(2,1)} %get-tuple-element.394.refs_3_), channel_id=1, source_target_pairs={{0,1},{3,2},{4,5},{7,6},{8,9},{11,10},{12,13},{15,14},{16,17},{19,... | collective-permute-start | bytes 3145736 | tf_op jit(solution)/shard_map/ppermute | solution.py:106
  566.1 32.5 %collective-permute-start.67 = (bf16[352,2048]{1,0:T(8,128)(2,1)}, bf16[352,2048]{1,0:T(8,128)(2,1)}, u32[]{:S(2)}, u32[]{:S(2)}) collective-permute-start(bf16[352,2048]{1,0:T(8,128)(2,1)} %get-tuple-element.407.refs_2_), channel_id=1, source_target_pairs={{1,0},{2,3},{5,4},{6,7},{9,8},{10,11},{13,12},{14,15},{17,16},{18,... | collective-permute-start | bytes 4325384 | tf_op jit(solution)/shard_map/ppermute | solution.py:106
  567.4 17.7 %collective-permute-start.61 = (bf16[384,2048]{1,0:T(8,128)(2,1)}, bf16[384,2048]{1,0:T(8,128)(2,1)}, u32[]{:S(2)}, u32[]{:S(2)}) collective-permute-start(bf16[384,2048]{1,0:T(8,128)(2,1)} %get-tuple-element.393.refs_1_), channel_id=1, source_target_pairs={{1,2},{2,1},{5,6},{6,5},{9,10},{10,9},{13,14},{14,13},{17,18},{18,... | collective-permute-start | bytes 4718600 | tf_op jit(solution)/shard_map/ppermute | solution.py:106
  573.2 35.5 %collective-permute-start.69 = (bf16[2,704,256]{2,1,0:T(8,128)(2,1)}, bf16[2,704,256]{2,1,0:T(8,128)(2,1)S(1)}, u32[]{:S(2)}, u32[]{:S(2)}) collective-permute-start(bf16[2,704,256]{2,1,0:T(8,128)(2,1)} %get-tuple-element.415), channel_id=1, source_target_pairs={{0,8},{4,12},{8,0},{12,4},{16,24},{20,28},{24,16},{28,20},{1,9},{5... | collective-permute-start | bytes 2162696 | tf_op jit(solution)/shard_map/ppermute | solution.py:223
  573.8 36.2 %collective-permute-start.70 = (bf16[2,704,256]{2,1,0:T(8,128)(2,1)}, bf16[2,704,256]{2,1,0:T(8,128)(2,1)}, u32[]{:S(2)}, u32[]{:S(2)}) collective-permute-start(bf16[2,704,256]{2,1,0:T(8,128)(2,1)} %get-tuple-element.416), channel_id=1, source_target_pairs={{0,16},{4,20},{8,24},{12,28},{16,0},{20,4},{24,8},{28,12},{1,17},{... | collective-permute-start | bytes 2162696 | tf_op jit(solution)/shard_map/ppermute | solution.py:223
  603.6 30.3 %collective-permute-start.66 = (bf16[256,2048]{1,0:T(8,128)(2,1)}, bf16[256,2048]{1,0:T(8,128)(2,1)}, u32[]{:S(2)}, u32[]{:S(2)}) collective-permute-start(bf16[256,2048]{1,0:T(8,128)(2,1)} %get-tuple-element.405.refs_1_), channel_id=1, source_target_pairs={{1,2},{2,1},{5,6},{6,5},{9,10},{10,9},{13,14},{14,13},{17,18},{18,... | collective-permute-start | bytes 3145736 | tf_op jit(solution)/shard_map/ppermute | solution.py:106
  608.7 19.0 %collective-permute-start.68 = (bf16[4,704,256]{2,1,0:T(8,128)(2,1)}, bf16[4,704,256]{2,1,0:T(8,128)(2,1)}, u32[]{:S(2)}, u32[]{:S(2)}) collective-permute-start(bf16[4,704,256]{2,1,0:T(8,128)(2,1)} %get-tuple-element.414), channel_id=1, source_target_pairs={{0,4},{4,0},{8,12},{12,8},{16,20},{20,16},{24,28},{28,24},{1,5},{5... | collective-permute-start | bytes 4325384 | tf_op jit(solution)/shard_map/ppermute | solution.py:223
  608.7 49.6 %collective-permute-start.65 = (bf16[384,2048]{1,0:T(8,128)(2,1)}, bf16[384,2048]{1,0:T(8,128)(2,1)}, u32[]{:S(2)}, u32[]{:S(2)}) collective-permute-start(bf16[384,2048]{1,0:T(8,128)(2,1)} %get-tuple-element.404.refs_2_), channel_id=1, source_target_pairs={{1,0},{2,3},{5,4},{6,7},{9,8},{10,11},{13,12},{14,15},{17,16},{18,... | collective-permute-start | bytes 4718600 | tf_op jit(solution)/shard_map/ppermute | solution.py:106
  630.5 32.7 %collective-permute-start.73 = (bf16[2,704,256]{2,1,0:T(8,128)(2,1)}, bf16[2,704,256]{2,1,0:T(8,128)(2,1)S(1)}, u32[]{:S(2)}, u32[]{:S(2)}) collective-permute-start(bf16[2,704,256]{2,1,0:T(8,128)(2,1)} %get-tuple-element.428), channel_id=1, source_target_pairs={{0,8},{4,12},{8,0},{12,4},{16,24},{20,28},{24,16},{28,20},{1,9},{5... | collective-permute-start | bytes 2162696 | tf_op jit(solution)/shard_map/ppermute | solution.py:223
  631.1 32.1 %collective-permute-start.74 = (bf16[2,704,256]{2,1,0:T(8,128)(2,1)}, bf16[2,704,256]{2,1,0:T(8,128)(2,1)}, u32[]{:S(2)}, u32[]{:S(2)}) collective-permute-start(bf16[2,704,256]{2,1,0:T(8,128)(2,1)} %get-tuple-element.429), channel_id=1, source_target_pairs={{0,16},{4,20},{8,24},{12,28},{16,0},{20,4},{24,8},{28,12},{1,17},{... | collective-permute-start | bytes 2162696 | tf_op jit(solution)/shard_map/ppermute | solution.py:223
  631.4 31.8 %collective-permute-start.75 = (bf16[2,704,256]{2,1,0:T(8,128)(2,1)}, bf16[2,704,256]{2,1,0:T(8,128)(2,1)}, u32[]{:S(2)}, u32[]{:S(2)}) collective-permute-start(bf16[2,704,256]{2,1,0:T(8,128)(2,1)} %get-tuple-element.430), channel_id=1, source_target_pairs={{0,24},{4,28},{8,16},{12,20},{16,8},{20,12},{24,0},{28,4},{1,25},{... | collective-permute-start | bytes 2162696 | tf_op jit(solution)/shard_map/ppermute | solution.py:223
  637.6 43.0 %collective-permute-start.79 = (bf16[256,2048]{1,0:T(8,128)(2,1)}, bf16[256,2048]{1,0:T(8,128)(2,1)}, u32[]{:S(2)}, u32[]{:S(2)}) collective-permute-start(bf16[256,2048]{1,0:T(8,128)(2,1)} %get-tuple-element.436.refs_2_), channel_id=1, source_target_pairs={{1,0},{2,3},{5,4},{6,7},{9,8},{10,11},{13,12},{14,15},{17,16},{18,... | collective-permute-start | bytes 3145736 | tf_op jit(solution)/shard_map/ppermute | solution.py:106
  666.5 20.0 %collective-permute-start.76 = (bf16[2,384,256]{2,1,0:T(8,128)(2,1)S(1)}, bf16[2,384,256]{2,1,0:T(8,128)(2,1)S(1)}, u32[]{:S(2)}, u32[]{:S(2)}) collective-permute-start(bf16[2,384,256]{2,1,0:T(8,128)(2,1)S(1)} %get-tuple-element.433), channel_id=1, source_target_pairs={{0,8},{4,12},{8,0},{12,4},{16,24},{20,28},{24,16},{28,20},{1,9},{5... | collective-permute-start | bytes 1179656 | tf_op jit(solution)/shard_map/ppermute | solution.py:223
  668.0 18.9 %collective-permute-start.77 = (bf16[2,384,256]{2,1,0:T(8,128)(2,1)S(1)}, bf16[2,384,256]{2,1,0:T(8,128)(2,1)S(1)}, u32[]{:S(2)}, u32[]{:S(2)}) collective-permute-start(bf16[2,384,256]{2,1,0:T(8,128)(2,1)S(1)} %get-tuple-element.434), channel_id=1, source_target_pairs={{0,16},{4,20},{8,24},{12,28},{16,0},{20,4},{24,8},{28,12},{1,17},{... | collective-permute-start | bytes 1179656 | tf_op jit(solution)/shard_map/ppermute | solution.py:223
  669.8 17.9 %collective-permute-start.78 = (bf16[2,384,256]{2,1,0:T(8,128)(2,1)S(1)}, bf16[2,384,256]{2,1,0:T(8,128)(2,1)S(1)}, u32[]{:S(2)}, u32[]{:S(2)}) collective-permute-start(bf16[2,384,256]{2,1,0:T(8,128)(2,1)S(1)} %get-tuple-element.435), channel_id=1, source_target_pairs={{0,24},{4,28},{8,16},{12,20},{16,8},{20,12},{24,0},{28,4},{1,25},{... | collective-permute-start | bytes 1179656 | tf_op jit(solution)/shard_map/ppermute | solution.py:223
  (81 other events, 459.7 us)

commit v3 on v1

--- a/solution.py
+++ b/solution.py
@@ -358,7 +358,7 @@
             [whole_out(o) for o in outs], vmem=40,
         )
 
-    def exchange(self, load, args, a, b):
+    def exchange(self, load, args, a, b, apart=False):
         smem = pl.BlockSpec(memory_space=pltpu.SMEM)
         specs = [smem, *[smem if v.ndim == 1 else whole(v) for v in args]]
         if not self.fast:
@@ -405,9 +405,13 @@
         sends = self.clock.call(
             stack, [kept, come], [whole(kept), whole(come)], [two] * 3, [whole_out(two)] * 3, vmem=24
         )
-        arrived = [self.swap(value, 2 * i + 2) for i, value in enumerate(sends)]
+        arrived = [self.swap(value, 2 * i + 2) for i, value in enumerate(sends[: 2 if apart else 3])]
         self.clock.pause(mib / 2)
         yield
+        if apart:
+            arrived.append(self.swap(self.clock.tie(sends[2]), 6))
+            self.clock.pause(mib / 2)
+            yield
 
         def unpack(me, kept, come, *rest):
             out = rest[-1]
@@ -630,13 +634,16 @@
     )
 
 
-def feed_weight_grad(clock, exchanged, weight, gain):
+def feed_weight_grad(clock, parts, weight, gain):
     own, columns = weight.shape
-    shards, ff, _ = exchanged.shape
+    shards = parts[0].shape[0]
+    ff = sum(part.shape[1] for part in parts)
     join = 128 // math.gcd(ff, 128)
 
-    def body(ins, w, g, grad_out, sum_out):
-        value = ins[...].reshape(join * ff, own).astype(F32).T * g[...]
+    def body(*refs):
+        (w, g, grad_out, sum_out), ins = refs[len(parts) :], refs[: len(parts)]
+        value = jnp.concatenate([ref[...] for ref in ins], 1) if len(ins) > 1 else ins[0][...]
+        value = value.reshape(join * ff, own).astype(F32).T * g[...]
         grad_out[...] = value
 
         @pl.when(pl.program_id(0) == 0)
@@ -646,10 +653,10 @@
         total = jnp.sum(w[...].astype(F32) * value, -1, keepdims=True)
         sum_out[...] += jnp.broadcast_to(total, sum_out.shape)
 
-    spec = pl.BlockSpec((join, ff, own), lambda i: (i, 0, 0))
+    specs = [pl.BlockSpec((join, part.shape[1], own), lambda i: (i, 0, 0)) for part in parts]
     total = shape_of(own, 128, F32)
     return clock.call(
-        body, [exchanged, weight, gain], [spec, column_blocks(own, join * ff), whole(gain)],
+        body, [*parts, weight, gain], [*specs, column_blocks(own, join * ff), whole(gain)],
         [shape_of(own, columns, F32), total], [column_blocks(own, join * ff), whole_out(total)], shards // join,
     )
 
@@ -680,15 +687,17 @@
     return clock.call(body, args, [whole(a) for a in args], outs, [whole_out(o) for o in outs])
 
 
-def widen(clock, *parts):
-    rows, width = sum(p.shape[0] for p in parts), parts[0].shape[1]
-
-    def body(*refs):
-        refs[-1][...] = jnp.concatenate([ref[...] for ref in refs[:-1]], 0).astype(F32)
+def widen(clock, value, start, rows, at=0, pieces=1, into=None):
+    width = value.shape[1]
+
+    def body(ref, *rest):
+        rest[-1][...] = ref[start : start + rows, :].astype(F32)
 
     return clock.call(
-        body, parts, [column_blocks(p.shape[0], width // 4) for p in parts],
-        [shape_of(rows, width, F32)], [column_blocks(rows, width // 4)], 4,
+        body, [value] + ([into] if into is not None else []),
+        [column_blocks(value.shape[0], width // 4)] + ([TOKEN] if into is not None else []),
+        [shape_of(pieces * rows, width, F32)], [pl.BlockSpec((rows, width // 4), lambda i: (at, i))], 4,
+        aliases={1: 0} if into is not None else None,
     )[0]
 
 
@@ -709,21 +718,34 @@
     )[0]
 
 
-def weight_grad(clock, lefts, rights, parts, block=512):
-    rows = lefts[0].shape[0] // parts
+def weight_grad(clock, lefts, rights, cuts, at=0, above=None, padding=0, block=512):
+    rows = sum(cuts)
     width = rights[0].shape[1]
     count = len(lefts)
+    extra = [above] if above is not None else []
+    heights = list(cuts)
+    heights[-1] += padding + sum(v.shape[0] for v in extra)
 
     def body(*refs):
-        lefts, rights, outs = refs[:count], refs[count : 2 * count], refs[2 * count :]
+        lefts, rights, outs = refs[:count], refs[count : 2 * count], refs[2 * count + len(extra) :]
         total = sum(dot(a[...], b[...]) for a, b in zip(lefts, rights)).astype(BF16)
-        for at, out in enumerate(outs):
-            out[...] = total[at * rows : (at + 1) * rows]
+        parts = [ref[...] for ref in refs[2 * count : 2 * count + len(extra)]] + [total]
+        if padding:
+            parts.append(jnp.zeros((padding, block), BF16))
+        total = jnp.concatenate(parts, 0) if len(parts) > 1 else total
+        start = 0
+        for height, out in zip(heights, outs):
+            out[...] = total[start : start + height]
+            start += height
+
+    def left(array):
+        return pl.BlockSpec((rows, array.shape[1]), lambda i: (at, 0), pipeline_mode=pl.Buffered(1))
 
     return clock.call(
-        body, [*lefts, *rights],
-        [whole(a) for a in lefts] + [column_blocks(b.shape[0], block) for b in rights],
-        [shape_of(rows, width)] * parts, [column_blocks(rows, block)] * parts, width // block,
+        body, [*lefts, *rights, *extra],
+        [left(a) for a in lefts] + [column_blocks(b.shape[0], block) for b in [*rights, *extra]],
+        [shape_of(height, width) for height in heights],
+        [column_blocks(height, block) for height in heights], width // block,
     )
 
 
@@ -809,28 +831,36 @@
     n2 = group.gathered
     results = {}
 
-    def sum_copies(name, parts):
-        for at, part in enumerate(parts):
+    def sum_copies(name, parts, first=0):
+        for at, part in enumerate(parts, first):
             line.queue(part, functools.partial(results.__setitem__, (name, at)))
 
     def exchange_back(*parts):
         def load(refs, j):
-            blocks = [ref[:, j * own : (j + 1) * own] for ref in refs]
+            blocks = [ref[:rows, j * own : (j + 1) * own] for ref, (_, rows) in zip(refs, parts)]
             return jnp.concatenate(blocks, 0) if len(blocks) > 1 else blocks[0]
 
-        return group.exchange(load, parts, sum(part.shape[0] for part in parts), own)
+        return group.exchange(load, [value for value, _ in parts], sum(rows for _, rows in parts), own)
+
+    piece = ff // 2
+    rest = cols - piece
+    padding = piece - rest - qcols
+    if line.size != 4 or rest < 0 or padding < 0:
+        rest = padding = 0
 
     act_e, dgate_e, dup_e, act_et, dgate_et, dup_et = feed(clock, n2[0], dy[0], wg_mine, wu_mine, wd)
     act_o, dgate_o, dup_o, act_ot, dgate_ot, dup_ot = feed(clock, n2[1], dy[1], wg_mine, wu_mine, wd)
-    sum_copies("down", weight_grad(clock, (act_et, act_ot), dy, 2))
+    down_parts = weight_grad(clock, (act_et, act_ot), dy, [piece, piece])
+    sum_copies("down", down_parts[:1])
     line.tick()
+    sum_copies("gate", weight_grad(clock, (dgate_et, dgate_ot), n2, [piece]))
     other = group.partner(product(clock, (dgate_o, dup_o), (wg_mine, wu_mine), True))
     part_e = product(clock, (dgate_e, dup_e), (wg_mine, wu_mine), True)
     a2_steps = group.scatter([(part_e, other)])
     next(a2_steps)
     line.tick()
-    sum_copies("gate", weight_grad(clock, (dgate_et, dgate_ot), n2, 2))
-    sum_copies("up", weight_grad(clock, (dup_et, dup_ot), n2, 2))
+    sum_copies("gate", weight_grad(clock, (dgate_et, dgate_ot), n2, [piece], at=1), 1)
+    sum_copies("up", weight_grad(clock, (dup_et, dup_ot), n2, [piece, piece]))
     next(a2_steps)
     line.tick()
     drain(a2_steps)
@@ -858,8 +888,12 @@
     line.tick()
     a1_steps = group.scatter([(part_e, other), out_parts])
     next(a1_steps)
-    sum_copies("qkv", weight_grad(clock, (dqkv_et, dqkv_ot), x_all, 1))
-    sum_copies("o", weight_grad(clock, (context_et, context_ot), dattn, 1))
+    qkv_pieces = weight_grad(clock, (dqkv_et, dqkv_ot), x_all, [cols - rest] + [rest] * (rest > 0))
+    sum_copies("qkv", qkv_pieces[:1])
+    above = qkv_pieces[1] if rest else None
+    context_t = context_et, context_ot
+    sum_copies("o", weight_grad(clock, context_t, dattn, [qcols], above=above, padding=padding))
+    sum_copies("down", down_parts[1:], 1)
     line.tick()
     next(a1_steps)
     line.tick()
@@ -880,31 +914,33 @@
     (layer_out,) = group.finish_rows(output, group.terms[1], [h1], [shape_of(rows, width)])
     def tick_until(name, at):
         while (name, at) not in results:
-            line.tick(4)
+            line.tick(0.1)
 
     tick_until("gate", 1)
-    gate_steps = exchange_back(results["gate", 0], results["gate", 1])
+    gate_steps = exchange_back((results["gate", 0], piece), (results["gate", 1], piece))
     next(gate_steps)
+    tick_until("up", 1)
     next(gate_steps)
-    line.tick(4)
-    down_grad = widen(clock, results["down", 0], results["down", 1])
-    drain(gate_steps)
-    gate_grad, gate_sums = feed_weight_grad(clock, group.exchanged, wg, g2)
-    tick_until("up", 1)
-    up_steps = exchange_back(results["up", 0], results["up", 1])
-    next(up_steps)
+    down_grad = widen(clock, results["down", 0], 0, piece, 0, 2)
+    up_steps = exchange_back((results["up", 0], piece), (results["up", 1], piece))
     next(up_steps)
     tick_until("qkv", 0)
-    qkv_steps = exchange_back(results["qkv", 0])
+    drain(gate_steps)
+    gate_back = group.exchanged
+    next(up_steps)
+    gate_grad, gate_sums = feed_weight_grad(clock, [gate_back], wg, g2)
+    tick_until("o", 0)
+    qkv_steps = exchange_back((results["qkv", 0], cols - rest), *[(results["o", 0], rest)] * (rest > 0))
     next(qkv_steps)
     drain(up_steps)
     up_back = group.exchanged
     next(qkv_steps)
-    up_grad, up_sums = feed_weight_grad(clock, up_back, wu, g2)
-    tick_until("o", 0)
-    o_grad = widen(clock, results["o", 0])
+    o_grad = widen(clock, results["o", 0], rest, qcols)
+    up_grad, up_sums = feed_weight_grad(clock, [up_back], wu, g2)
     drain(qkv_steps)
     q_grad, k_grad, v_grad, qkv_sums = qkv_weight_grad(clock, group.exchanged, wq, wk, wv, g1)
+    tick_until("down", 1)
+    down_grad = widen(clock, results["down", 1], 0, piece, 1, 2, down_grad)
 
     gain1_grad = qkv_sums[:, 0] / g1[:, 0]
     gain2_grad = (gate_sums[:, 0] + up_sums[:, 0]) / g2[:, 0]

time: 692 us -> 687 us (level)
  starting transfers between devices: 113 us -> 97.5 us
  Pallas kernels: 324 us -> 335 us
  waiting for transfers between devices: 190 us -> 183 us
    ppermute x26 -> x24, starting transfers between devices: 64.2 us -> 51 us  [shift(): return lax.ppermute(value, 'rep', pairs)]
    pallas_call x121 -> x123, Pallas kernels: 324 us -> 335 us  [call(): pl.pallas_call(kernel, grid=(steps,), out_shape=(*outs, pltpu.HBM(self.to...]
    unnamed x127 -> x139, local copies, waits for them, and re-layouts: 45.9 us -> 52.2 us
    ppermute x26 -> x24, waiting for transfers between devices: 82.9 us -> 79.1 us  [shift(): return lax.ppermute(value, 'rep', pairs)]
  transfers between devices with their start and end apart: 80 -> 78, of which waited for: 38 -> 33; matrix products, arithmetic and copies ran while one was open for 1% -> 1% of each run, Pallas kernels for 43% -> 44%
where the time goes in v3:
time: 687 us; the launch traced here: 676 us
  Pallas kernels  335 us (49%)
  waiting for transfers between devices  183 us (27%)
  starting transfers between devices  97.5 us (14%)
  local copies, waits for them, and re-layouts  57.8 us (8%)
    pallas_call x123, Pallas kernels, call(): pl.pallas_call(kernel, grid=(steps,), out_shape=(*outs, pltpu.HBM(self.to...  335 us
    ppermute x54, waiting for transfers between devices, swap(): lax.ppermute(value, 'shard', [(i, i ^ bit) for i in range(self.size)])  104 us
    ppermute x24, waiting for transfers between devices, shift(): return lax.ppermute(value, 'rep', pairs)  79.1 us
    unnamed x139, local copies, waits for them, and re-layouts  52.2 us
    ppermute x24, starting transfers between devices, shift(): return lax.ppermute(value, 'rep', pairs)  51 us
    ppermute x54, starting transfers between devices, swap(): lax.ppermute(value, 'shard', [(i, i ^ bit) for i in range(self.size)])  46.5 us
  transfers between devices with their start and end apart: 78, of which 33 were waited for; matrix products, arithmetic and copies ran while one was open for 1% of the time, Pallas kernels for 44%

profile of v3, /device:TPU:0, one launch (start us, length us, event | category | flops | bytes accessed | tf_op | source)
XLA Modules:
  0.0 676.3 jit_solution(5310503725937407704)
XLA Ops:
  0.6 3.0 collective-permute-start.1
  12.0 15.0 %collective-permute-done.1.refs_1_.refs_4_.refs_5_ = bf16[256,2048]{1,0:T(8,128)(2,1)S(1)} collective-permute-done((bf16[256,2048]{1,0:T(8,128)(2,1)}, bf16[256,2048]{1,0:T(8,128)(2,1)S(1)}, u32[]{:S(2)}, u32[]{:S(2)}) %collective-permute-start.1) | collective-permute-done | bytes 1048608 | tf_op jit(solution)/shard_map/ppermute | solution.py:223
  45.2 4.2 shard_map.230
  49.6 3.9 collective-permute-done.5.refs_3_
  53.5 6.9 %collective-permute-done.7.refs_5_ = bf16[2,256,384]{2,1,0:T(8,128)(2,1)} collective-permute-done((bf16[2,256,384]{2,1,0:T(8,128)(2,1)}, bf16[2,256,384]{2,1,0:T(8,128)(2,1)}, u32[]{:S(2)}, u32[]{:S(2)}) %collective-permute-start.7) | collective-permute-done | bytes 393248 | tf_op jit(solution)/shard_map/ppermute | solution.py:223
  69.0 12.0 %shard_map.235 = (bf16[1024,384]{1,0:T(8,128)(2,1)}, f32[1024,128]{1,0:T(8,128)}, bf16[256,1024]{1,0:T(8,128)(2,1)}, bf16[1024,2048]{1,0:T(8,128)(2,1)}, f32[8,128]{1,0:T(8,128)}) custom-call(bf16[1024,2048]{1,0:T(8,128)(2,1)} %collective-permute-done.12.refs_0_.refs_3_, bf16[2048,384]{1,0:T(8,128)(2,1)} %bitcast.21, ...), custom_call_target="tpu_custom_call", output_to_operand_aliasing={{4}: (6, {})} | custom-call | flops 1 | bytes 1 | tf_op jit(solution)/shard_map/pallas_call | solution.py:69
  88.1 5.7 collective-permute-start.18
  93.8 12.0 %shard_map.241 = (bf16[1024,384]{1,0:T(8,128)(2,1)}, f32[1024,128]{1,0:T(8,128)}, bf16[256,1024]{1,0:T(8,128)(2,1)}, bf16[1024,2048]{1,0:T(8,128)(2,1)}, f32[8,128]{1,0:T(8,128)}) custom-call(bf16[1024,2048]{1,0:T(8,128)(2,1)} %get-tuple-element.240.refs_0_.refs_2_, bf16[2048,384]{1,0:T(8,128)(2,1)} %bitcast.22, ...), custom_call_target="tpu_custom_call", output_to_operand_aliasing={{4}: (6, {})} | custom-call | flops 1 | bytes 1 | tf_op jit(solution)/shard_map/pallas_call | solution.py:69
  115.6 7.3 %collective-permute-done.19.refs_1_ = bf16[8,2,64,704]{3,2,1,0:T(8,128)(2,1)} collective-permute-done((bf16[8,2,64,704]{3,2,1,0:T(8,128)(2,1)}, bf16[8,2,64,704]{3,2,1,0:T(8,128)(2,1)}, u32[]{:S(2)}, u32[]{:S(2)}) %collective-permute-start.19) | collective-permute-done | bytes 1441824 | tf_op jit(solution)/shard_map/ppermute | solution.py:106
  126.1 8.3 %collective-permute-done.16.refs_2_ = bf16[256,2048]{1,0:T(8,128)(2,1)S(1)} collective-permute-done((bf16[256,2048]{1,0:T(8,128)(2,1)S(1)}, bf16[256,2048]{1,0:T(8,128)(2,1)S(1)}, u32[]{:S(2)}, u32[]{:S(2)}) %collective-permute-start.16) | collective-permute-done | bytes 1048608 | tf_op jit(solution)/shard_map/ppermute | solution.py:223
  140.2 22.9 %collective-permute-done.23.refs_1_ = bf16[8,2,64,704]{3,2,1,0:T(8,128)(2,1)S(1)} collective-permute-done((bf16[8,2,64,704]{3,2,1,0:T(8,128)(2,1)}, bf16[8,2,64,704]{3,2,1,0:T(8,128)(2,1)S(1)}, u32[]{:S(2)}, u32[]{:S(2)}) %collective-permute-start.23) | collective-permute-done | bytes 1441824 | tf_op jit(solution)/shard_map/ppermute | solution.py:106
  175.8 17.7 %collective-permute-done.25.refs_1_.refs_4_.refs_5_ = bf16[256,2048]{1,0:T(8,128)(2,1)S(1)} collective-permute-done((bf16[256,2048]{1,0:T(8,128)(2,1)S(1)}, bf16[256,2048]{1,0:T(8,128)(2,1)S(1)}, u32[]{:S(2)}, u32[]{:S(2)}) %collective-permute-start.25) | collective-permute-done | bytes 1048608 | tf_op jit(solution)/shard_map/ppermute | solution.py:223
  197.5 4.9 shard_map.258
  208.0 17.4 %shard_map.261 = (bf16[1024,704]{1,0:T(8,128)(2,1)}, bf16[1024,704]{1,0:T(8,128)(2,1)}, bf16[1024,704]{1,0:T(8,128)(2,1)}, bf16[704,1024]{1,0:T(8,128)(2,1)}, bf...) custom-call(bf16[1024,2048]{1,0:T(8,128)(2,1)} %get-tuple-element.286, ...), custom_call_target="tpu_custom_call", output_to_operand_aliasing={{6}: (5, {})} | custom-call | flops 1 | bytes 1 | tf_op jit(solution)/shard_map/pallas_call | solution.py:69
  225.4 17.4 %shard_map.262 = (bf16[1024,704]{1,0:T(8,128)(2,1)}, bf16[1024,704]{1,0:T(8,128)(2,1)}, bf16[1024,704]{1,0:T(8,128)(2,1)}, bf16[704,1024]{1,0:T(8,128)(2,1)}, bf...) custom-call(bf16[1024,2048]{1,0:T(8,128)(2,1)} %collective-permute-do, ...), custom_call_target="tpu_custom_call", output_to_operand_aliasing={{6}: (5, {})} | custom-call | flops 1 | bytes 1 | tf_op jit(solution)/shard_map/pallas_call | solution.py:69
  242.7 10.0 %shard_map.263 = (bf16[352,2048]{1,0:T(8,128)(2,1)}, bf16[352,2048]{1,0:T(8,128)(2,1)}, f32[8,128]{1,0:T(8,128)}) custom-call(bf16[704,1024]{1,0:T(8,128)(2,1)} %get-tuple-element.299.refs_0_, bf16[704,1024]{1,0:T(8,128)(2,1)} %get-tuple-element.300.refs_1_, bf16[1024,2048]{1,0:T(8,128)(2,1)} %get-tuple-element.287.refs_1_.refs_2_, ...), custom_call_target="tpu_custom_call", output_to_operand_aliasing={{2}: (4, {})} | custom-call | flops 1 | bytes 1 | tf_op jit(solution)/shard_map/pallas_call | solution.py:69
  255.2 6.2 collective-permute-start.35
  261.4 7.4 %shard_map.266 = (bf16[352,2048]{1,0:T(8,128)(2,1)}, f32[8,128]{1,0:T(8,128)}) custom-call(bf16[704,1024]{1,0:T(8,128)(2,1)} %get-tuple-element.297.refs_0_, bf16[704,1024]{1,0:T(8,128)(2,1)} %get-tuple-element.298.refs_1_, bf16[1024,2048]{1,0:T(8,128)(2,1)} %get-tuple-element.286.refs_0_.refs_2_, ...), custom_call_target="tpu_custom_call", output_to_operand_aliasing={{1}: (4, {})} | custom-call | flops 1 | bytes 1 | tf_op jit(solution)/shard_map/pallas_call | solution.py:69
  268.8 11.6 %shard_map.267 = (bf16[1024,2048]{1,0:T(8,128)(2,1)}, f32[8,128]{1,0:T(8,128)}) custom-call(bf16[1024,704]{1,0:T(8,128)(2,1)} %get-tuple-element.295.refs_0_, bf16[1024,704]{1,0:T(8,128)(2,1)} %get-tuple-element.296.refs_1_, bf16[2048,704]{1,0:T(8,128)(2,1)} %bitcast.15, bf16[2048,704]{1,0:T(8,128)(2,1)} %bitcast.19, ...), custom_call_target="tpu_custom_call", output_to_operand_aliasing={{1}: (4, {})} | custom-call | flops 1 | bytes 1 | tf_op jit(solution)/shard_map/pallas_call | solution.py:69
  280.6 11.6 %shard_map.269 = (bf16[1024,2048]{1,0:T(8,128)(2,1)}, f32[8,128]{1,0:T(8,128)}) custom-call(bf16[1024,704]{1,0:T(8,128)(2,1)} %get-tuple-element.292.refs_0_, bf16[1024,704]{1,0:T(8,128)(2,1)} %get-tuple-element.293.refs_1_, bf16[2048,704]{1,0:T(8,128)(2,1)} %bitcast.16, bf16[2048,704]{1,0:T(8,128)(2,1)} %bitcast.20, ...), custom_call_target="tpu_custom_call", output_to_operand_aliasing={{1}: (4, {})} | custom-call | flops 1 | bytes 1 | tf_op jit(solution)/shard_map/pallas_call | solution.py:69
  294.4 3.1 shard_map.270
  299.9 3.5 shard_map.272
  307.5 7.3 %shard_map.274 = (bf16[352,2048]{1,0:T(8,128)(2,1)}, f32[8,128]{1,0:T(8,128)}) custom-call(bf16[704,1024]{1,0:T(8,128)(2,1)} %get-tuple-element.297.refs_0_, bf16[704,1024]{1,0:T(8,128)(2,1)} %get-tuple-element.298.refs_1_, bf16[1024,2048]{1,0:T(8,128)(2,1)} %get-tuple-element.286.refs_0_.refs_2_, ...), custom_call_target="tpu_custom_call", output_to_operand_aliasing={{1}: (4, {})} | custom-call | flops 1 | bytes 1 | tf_op jit(solution)/shard_map/pallas_call | solution.py:69
  314.9 10.0 %shard_map.275 = (bf16[352,2048]{1,0:T(8,128)(2,1)}, bf16[352,2048]{1,0:T(8,128)(2,1)}, f32[8,128]{1,0:T(8,128)}) custom-call(bf16[704,1024]{1,0:T(8,128)(2,1)} %get-tuple-element.312.refs_0_, bf16[704,1024]{1,0:T(8,128)(2,1)} %get-tuple-element.313.refs_1_, bf16[1024,2048]{1,0:T(8,128)(2,1)} %get-tuple-element.286.refs_0_.refs_2_, ...), custom_call_target="tpu_custom_call", output_to_operand_aliasing={{2}: (4, {})} | custom-call | flops 1 | bytes 1 | tf_op jit(solution)/shard_map/pallas_call | solution.py:69
  324.9 2.9 copy-done.1
  331.9 5.8 collective-permute-done.39.refs_5_
  337.8 4.7 shard_map.278
  351.6 3.6 shard_map.280
  356.8 7.0 %shard_map.282 = (bf16[1024,2048]{1,0:T(8,128)(2,1)}, f32[8,128]{1,0:T(8,128)}) custom-call(bf16[1024,704]{1,0:T(8,128)(2,1)} %get-tuple-element.291.refs_0_, bf16[704,2048]{1,0:T(8,128)(2,1)} %refs_1_.8, f32[8,128]{1,0:T(8,128)} %shard_map.281.refs_2_), custom_call_target="tpu_custom_call", output_to_operand_aliasing={{1}: (2, {})} | custom-call | flops 1 | bytes 1 | tf_op jit(solution)/shard_map/pallas_call | solution.py:69
  363.8 7.0 %shard_map.283 = (bf16[1024,2048]{1,0:T(8,128)(2,1)}, f32[8,128]{1,0:T(8,128)}) custom-call(bf16[1024,704]{1,0:T(8,128)(2,1)} %get-tuple-element.331.refs_0_, bf16[704,2048]{1,0:T(8,128)(2,1)} %refs_1_.8, f32[8,128]{1,0:T(8,128)} %get-tuple-element.332.refs_2_), custom_call_target="tpu_custom_call", output_to_operand_aliasing={{1}: (2, {})} | custom-call | flops 1 | bytes 1 | tf_op jit(solution)/shard_map/pallas_call | solution.py:69
  370.8 8.5 %collective-permute-done.42.refs_1_.refs_4_.refs_5_ = bf16[256,2048]{1,0:T(8,128)(2,1)S(1)} collective-permute-done((bf16[256,2048]{1,0:T(8,128)(2,1)}, bf16[256,2048]{1,0:T(8,128)(2,1)S(1)}, u32[]{:S(2)}, u32[]{:S(2)}) %collective-permute-start.42) | collective-permute-done | bytes 1048608 | tf_op jit(solution)/shard_map/ppermute | solution.py:223
  383.3 4.5 shard_map.287
  393.2 4.1 shard_map.290
  397.3 14.7 %shard_map.292 = (bf16[384,1024]{1,0:T(8,128)(2,1)}, bf16[1024,2048]{1,0:T(8,128)(2,1)}, f32[8,128]{1,0:T(8,128)}) custom-call(bf16[1024,2048]{1,0:T(8,128)(2,1)} %get-tuple-element.344.refs_0_.refs_2_, bf16[1024,384]{1,0:T(8,128)(2,1)} %get-tuple-element.345.refs_1_, f32[1024,128]{1,0:T(8,128)} %get-tuple-element.346.refs_2_, ...), custom_call_target="tpu_custom_call", output_to_operand_aliasing={{2}: (8, {})} | custom-call | flops 1 | bytes 1 | tf_op jit(solution)/shard_map/pallas_call | solution.py:69
  412.0 14.7 %shard_map.293 = (bf16[384,1024]{1,0:T(8,128)(2,1)}, bf16[1024,2048]{1,0:T(8,128)(2,1)}, f32[8,128]{1,0:T(8,128)}) custom-call(bf16[1024,2048]{1,0:T(8,128)(2,1)} %collective-permute-done.47.refs_0_.refs_3_, bf16[1024,384]{1,0:T(8,128)(2,1)} %get-tuple-element.349.refs_1_, f32[1024,128]{1,0:T(8,128)} %get-tuple-element.350.refs_2_, ...), custom_call_target="tpu_custom_call", output_to_operand_aliasing={{2}: (8, {})} | custom-call | flops 1 | bytes 1 | tf_op jit(solution)/shard_map/pallas_call | solution.py:69
  427.1 4.5 shard_map.295
  440.2 5.5 shard_map.298
  446.6 7.6 %shard_map.300 = (bf16[352,2048]{1,0:T(8,128)(2,1)}, bf16[32,2048]{1,0:T(8,128)(2,1)}, f32[8,128]{1,0:T(8,128)}) custom-call(bf16[384,1024]{1,0:T(8,128)(2,1)} %get-tuple-element.362.refs_0_, bf16[384,1024]{1,0:T(8,128)(2,1)} %get-tuple-element.363.refs_1_, bf16[1024,2048]{1,0:T(8,128)(2,1)} %get-tuple-element.240.refs_0_.refs_2_, ...), custom_call_target="tpu_custom_call", output_to_operand_aliasing={{2}: (4, {})} | custom-call | flops 1 | bytes 1 | tf_op jit(solution)/shard_map/pallas_call | solution.py:69
  454.2 7.0 %shard_map.301 = (bf16[352,2048]{1,0:T(8,128)(2,1)}, f32[8,128]{1,0:T(8,128)}) custom-call(bf16[256,1024]{1,0:T(8,128)(2,1)} %get-tuple-element.367.refs_0_, bf16[256,1024]{1,0:T(8,128)(2,1)} %get-tuple-element.368.refs_1_, bf16[1024,2048]{1,0:T(8,128)(2,1)} %get-tuple-element.344.refs_0_.refs_2_, ...), custom_call_target="tpu_custom_call", output_to_operand_aliasing={{1}: (5, {})} | custom-call | flops 1 | bytes 1 | tf_op jit(solution)/shard_map/pallas_call | solution.py:69
  461.2 4.2 collective-permute-done.53.refs_5_.refs_1_
  466.5 4.5 shard_map.302
  478.2 15.0 %collective-permute-done.51.refs_2_.refs_5_ = bf16[512,2048]{1,0:T(8,128)(2,1)S(1)} collective-permute-done((bf16[512,2048]{1,0:T(8,128)(2,1)}, bf16[512,2048]{1,0:T(8,128)(2,1)S(1)}, u32[]{:S(2)}, u32[]{:S(2)}) %collective-permute-start.51) | collective-permute-done | bytes 2097184 | tf_op jit(solution)/shard_map/ppermute | solution.py:223
  495.4 4.0 shard_map.305
  505.6 4.5 shard_map.307
  511.9 4.9 collective-permute-start.60
  519.5 4.2 collective-permute-done.55.refs_3_
  527.9 4.8 shard_map.310
  532.7 3.4 shard_map.311
  537.7 9.2 %collective-permute-done.60.refs_5_.refs_1_ = bf16[352,2048]{1,0:T(8,128)(2,1)} collective-permute-done((bf16[352,2048]{1,0:T(8,128)(2,1)}, bf16[352,2048]{1,0:T(8,128)(2,1)}, u32[]{:S(2)}, u32[]{:S(2)}) %collective-permute-start.60) | collective-permute-done | bytes 1441824 | tf_op jit(solution)/shard_map/ppermute | solution.py:106
  546.9 4.5 shard_map.314
  554.9 2.8 shard_map.316
  562.9 3.9 shard_map.319
  569.8 12.7 %collective-permute-done.61.refs_4_.refs_1_ = bf16[352,2048]{1,0:T(8,128)(2,1)} collective-permute-done((bf16[352,2048]{1,0:T(8,128)(2,1)}, bf16[352,2048]{1,0:T(8,128)(2,1)}, u32[]{:S(2)}, u32[]{:S(2)}) %collective-permute-start.61) | collective-permute-done | bytes 1441824 | tf_op jit(solution)/shard_map/ppermute | solution.py:106
  582.5 4.1 shard_map.322
  590.0 2.8 shard_map.324
  603.6 6.4 shard_map.328
  610.0 2.8 shard_map.329
  612.8 11.8 %collective-permute-done.64.refs_1_ = bf16[352,2048]{1,0:T(8,128)(2,1)} collective-permute-done((bf16[352,2048]{1,0:T(8,128)(2,1)}, bf16[352,2048]{1,0:T(8,128)(2,1)}, u32[]{:S(2)}, u32[]{:S(2)}) %collective-permute-start.64) | collective-permute-done | bytes 1441824 | tf_op jit(solution)/shard_map/ppermute | solution.py:106
  631.7 3.0 collective-permute-done.72.refs_4_
  642.5 3.6 shard_map.337
  646.2 6.5 shard_map.338
  653.7 5.3 collective-permute-done.75.refs_4_
  662.0 5.0 shard_map.340
  672.1 3.8 shard_map.343
  (364 shorter events, 205.5 us)
Async XLA Ops:
  0.6 26.4 %collective-permute-start.1 = (bf16[256,2048]{1,0:T(8,128)(2,1)}, bf16[256,2048]{1,0:T(8,128)(2,1)S(1)}, u32[]{:S(2)}, u32[]{:S(2)}) collective-permute-start(bf16[256,2048]{1,0:T(8,128)(2,1)} %bitcast.25), channel_id=1, source_target_pairs={{0,16},{4,20},{8,24},{12,28},{16,0},{20,4},{24,8},{28,12},{1,17},{... | collective-permute-start | bytes 3145736 | tf_op jit(solution)/shard_map/ppermute | solution.py:223
  3.7 24.8 %collective-permute-start = (bf16[256,2048]{1,0:T(8,128)(2,1)}, bf16[256,2048]{1,0:T(8,128)(2,1)S(1)}, u32[]{:S(2)}, u32[]{:S(2)}) collective-permute-start(bf16[256,2048]{1,0:T(8,128)(2,1)} %bitcast.26), channel_id=1, source_target_pairs={{0,8},{4,12},{8,0},{12,4},{16,24},{20,28},{24,16},{28,20},{1,9},{5... | collective-permute-start | bytes 3145736 | tf_op jit(solution)/shard_map/ppermute | solution.py:223
  10.8 20.7 %collective-permute-start.4 = (bf16[4,256,384]{2,1,0:T(8,128)(2,1)}, bf16[4,256,384]{2,1,0:T(8,128)(2,1)}, u32[]{:S(2)}, u32[]{:S(2)}) collective-permute-start(bf16[4,256,384]{2,1,0:T(8,128)(2,1)} %get-tuple-element.236), channel_id=1, source_target_pairs={{0,4},{4,0},{8,12},{12,8},{16,20},{20,16},{24,28},{28,24},{1,5},{5... | collective-permute-start | bytes 2359304 | tf_op jit(solution)/shard_map/ppermute | solution.py:223
  34.9 18.6 %collective-permute-start.5 = (bf16[2,256,384]{2,1,0:T(8,128)(2,1)}, bf16[2,256,384]{2,1,0:T(8,128)(2,1)}, u32[]{:S(2)}, u32[]{:S(2)}) collective-permute-start(bf16[2,256,384]{2,1,0:T(8,128)(2,1)} %get-tuple-element.241), channel_id=1, source_target_pairs={{0,8},{4,12},{8,0},{12,4},{16,24},{20,28},{24,16},{28,20},{1,9},{5... | collective-permute-start | bytes 1179656 | tf_op jit(solution)/shard_map/ppermute | solution.py:223
  35.3 18.2 %collective-permute-start.6 = (bf16[2,256,384]{2,1,0:T(8,128)(2,1)}, bf16[2,256,384]{2,1,0:T(8,128)(2,1)}, u32[]{:S(2)}, u32[]{:S(2)}) collective-permute-start(bf16[2,256,384]{2,1,0:T(8,128)(2,1)} %get-tuple-element.242), channel_id=1, source_target_pairs={{0,16},{4,20},{8,24},{12,28},{16,0},{20,4},{24,8},{28,12},{1,17},{... | collective-permute-start | bytes 1179656 | tf_op jit(solution)/shard_map/ppermute | solution.py:223
  36.9 23.4 %collective-permute-start.7 = (bf16[2,256,384]{2,1,0:T(8,128)(2,1)}, bf16[2,256,384]{2,1,0:T(8,128)(2,1)}, u32[]{:S(2)}, u32[]{:S(2)}) collective-permute-start(bf16[2,256,384]{2,1,0:T(8,128)(2,1)} %get-tuple-element.243), channel_id=1, source_target_pairs={{0,24},{4,28},{8,16},{12,20},{16,8},{20,12},{24,0},{28,4},{1,25},{... | collective-permute-start | bytes 1179656 | tf_op jit(solution)/shard_map/ppermute | solution.py:223
  44.8 18.2 %collective-permute-start.8 = (bf16[4,128,704]{1,2,0:T(8,128)(2,1)S(1)}, bf16[4,128,704]{1,2,0:T(8,128)(2,1)}, u32[]{:S(2)}, u32[]{:S(2)}) collective-permute-start(bf16[4,128,704]{1,2,0:T(8,128)(2,1)S(1)} %copy-done.63), channel_id=1, source_target_pairs={{0,4},{4,0},{8,12},{12,8},{16,20},{20,16},{24,28},{28,24},{1,5},{5... | collective-permute-start | bytes 2162696 | tf_op jit(solution)/shard_map/ppermute | solution.py:223
  49.4 19.7 %collective-permute-start.12 = (bf16[1024,2048]{1,0:T(8,128)(2,1)}, bf16[1024,2048]{1,0:T(8,128)(2,1)}, u32[]{:S(2)}, u32[]{:S(2)}) collective-permute-start(bf16[1024,2048]{1,0:T(8,128)(2,1)} %get-tuple-element.240.refs_0_.refs_2_), channel_id=1, source_target_pairs={{0,4},{4,0},{8,12},{12,8},{16,20},{20,16},{24,28},{28,24},{1,5},{5... | collective-permute-start | bytes 12582920 | tf_op jit(solution)/shard_map/ppermute | solution.py:223
  67.0 16.8 %collective-permute-start.10 = (bf16[2,128,704]{2,1,0:T(8,128)(2,1)}, bf16[2,128,704]{2,1,0:T(8,128)(2,1)S(1)}, u32[]{:S(2)}, u32[]{:S(2)}) collective-permute-start(bf16[2,128,704]{2,1,0:T(8,128)(2,1)} %get-tuple-element.250), channel_id=1, source_target_pairs={{0,16},{4,20},{8,24},{12,28},{16,0},{20,4},{24,8},{28,12},{1,17},{... | collective-permute-start | bytes 1081352 | tf_op jit(solution)/shard_map/ppermute | solution.py:223
  67.6 16.2 %collective-permute-start.11 = (bf16[2,128,704]{2,1,0:T(8,128)(2,1)}, bf16[2,128,704]{2,1,0:T(8,128)(2,1)S(1)}, u32[]{:S(2)}, u32[]{:S(2)}) collective-permute-start(bf16[2,128,704]{2,1,0:T(8,128)(2,1)} %get-tuple-element.251), channel_id=1, source_target_pairs={{0,24},{4,28},{8,16},{12,20},{16,8},{20,12},{24,0},{28,4},{1,25},{... | collective-permute-start | bytes 1081352 | tf_op jit(solution)/shard_map/ppermute | solution.py:223
  81.0 27.5 %collective-permute-start.13 = (bf16[1024,2048]{1,0:T(8,128)(2,1)}, bf16[1024,2048]{1,0:T(8,128)(2,1)}, u32[]{:S(2)}, u32[]{:S(2)}) collective-permute-start(bf16[1024,2048]{1,0:T(8,128)(2,1)} %get-tuple-element.257), channel_id=1, source_target_pairs={{0,4},{4,0},{8,12},{12,8},{16,20},{20,16},{24,28},{28,24},{1,5},{5... | collective-permute-start | bytes 12582920 | tf_op jit(solution)/shard_map/ppermute | solution.py:223
  85.1 23.0 %collective-permute-start.15 = (bf16[256,2048]{1,0:T(8,128)(2,1)}, bf16[256,2048]{1,0:T(8,128)(2,1)S(1)}, u32[]{:S(2)}, u32[]{:S(2)}) collective-permute-start(bf16[256,2048]{1,0:T(8,128)(2,1)} %get-tuple-element.258), channel_id=1, source_target_pairs={{0,16},{4,20},{8,24},{12,28},{16,0},{20,4},{24,8},{28,12},{1,17},{... | collective-permute-start | bytes 3145736 | tf_op jit(solution)/shard_map/ppermute | solution.py:223
  85.8 22.7 %collective-permute-start.14 = (bf16[256,2048]{1,0:T(8,128)(2,1)}, bf16[256,2048]{1,0:T(8,128)(2,1)S(1)}, u32[]{:S(2)}, u32[]{:S(2)}) collective-permute-start(bf16[256,2048]{1,0:T(8,128)(2,1)} %get-tuple-element.258), channel_id=1, source_target_pairs={{0,8},{4,12},{8,0},{12,4},{16,24},{20,28},{24,16},{28,20},{1,9},{5... | collective-permute-start | bytes 3145736 | tf_op jit(solution)/shard_map/ppermute | solution.py:223
  86.9 36.0 %collective-permute-start.19 = (bf16[8,2,64,704]{3,2,1,0:T(8,128)(2,1)}, bf16[8,2,64,704]{3,2,1,0:T(8,128)(2,1)}, u32[]{:S(2)}, u32[]{:S(2)}) collective-permute-start(bf16[8,2,64,704]{3,2,1,0:T(8,128)(2,1)} %bitcast.35), channel_id=1, source_target_pairs={{3,2},{2,1},{1,0},{7,6},{6,5},{5,4},{11,10},{10,9},{9,8},{15,14},{... | collective-permute-start | bytes 4325384 | tf_op jit(solution)/shard_map/ppermute | solution.py:106
  88.1 35.9 %collective-permute-start.18 = (bf16[8,2,64,704]{3,2,1,0:T(8,128)(2,1)}, bf16[8,2,64,704]{3,2,1,0:T(8,128)(2,1)}, u32[]{:S(2)}, u32[]{:S(2)}) collective-permute-start(bf16[8,2,64,704]{3,2,1,0:T(8,128)(2,1)} %bitcast.36), channel_id=1, source_target_pairs={{0,1},{1,2},{2,3},{4,5},{5,6},{6,7},{8,9},{9,10},{10,11},{12,13},{... | collective-permute-start | bytes 4325384 | tf_op jit(solution)/shard_map/ppermute | solution.py:106
  112.7 21.7 %collective-permute-start.16 = (bf16[256,2048]{1,0:T(8,128)(2,1)S(1)}, bf16[256,2048]{1,0:T(8,128)(2,1)S(1)}, u32[]{:S(2)}, u32[]{:S(2)}) collective-permute-start(bf16[256,2048]{1,0:T(8,128)(2,1)S(1)} %get-tuple-element.261), channel_id=1, source_target_pairs={{0,16},{4,20},{8,24},{12,28},{16,0},{20,4},{24,8},{28,12},{1,17},{... | collective-permute-start | bytes 3145736 | tf_op jit(solution)/shard_map/ppermute | solution.py:223
  114.1 22.1 %collective-permute-start.17 = (bf16[256,2048]{1,0:T(8,128)(2,1)S(1)}, bf16[256,2048]{1,0:T(8,128)(2,1)S(1)}, u32[]{:S(2)}, u32[]{:S(2)}) collective-permute-start(bf16[256,2048]{1,0:T(8,128)(2,1)S(1)} %get-tuple-element.263), channel_id=1, source_target_pairs={{0,8},{4,12},{8,0},{12,4},{16,24},{20,28},{24,16},{28,20},{1,9},{5... | collective-permute-start | bytes 3145736 | tf_op jit(solution)/shard_map/ppermute | solution.py:223
  124.1 16.2 %collective-permute-start.22 = (bf16[8,2,64,704]{3,2,1,0:T(8,128)(2,1)}, bf16[8,2,64,704]{3,2,1,0:T(8,128)(2,1)S(1)}, u32[]{:S(2)}, u32[]{:S(2)}) collective-permute-start(bf16[8,2,64,704]{3,2,1,0:T(8,128)(2,1)} %get-tuple-element.270.refs_2_), channel_id=1, source_target_pairs={{1,2},{2,3},{5,6},{6,7},{9,10},{10,11},{13,14},{14,15},{17,18},{18... | collective-permute-start | bytes 4325384 | tf_op jit(solution)/shard_map/ppermute | solution.py:106
  124.8 38.3 %collective-permute-start.23 = (bf16[8,2,64,704]{3,2,1,0:T(8,128)(2,1)}, bf16[8,2,64,704]{3,2,1,0:T(8,128)(2,1)S(1)}, u32[]{:S(2)}, u32[]{:S(2)}) collective-permute-start(bf16[8,2,64,704]{3,2,1,0:T(8,128)(2,1)} %get-tuple-element.271.refs_5_), channel_id=1, source_target_pairs={{2,1},{1,0},{6,5},{5,4},{10,9},{9,8},{14,13},{13,12},{18,17},{17,1... | collective-permute-start | bytes 4325384 | tf_op jit(solution)/shard_map/ppermute | solution.py:106
  137.8 27.5 %collective-permute-start.20 = (bf16[256,2048]{1,0:T(8,128)(2,1)S(1)}, bf16[256,2048]{1,0:T(8,128)(2,1)S(1)}, u32[]{:S(2)}, u32[]{:S(2)}) collective-permute-start(bf16[256,2048]{1,0:T(8,128)(2,1)S(1)} %get-tuple-element.268), channel_id=1, source_target_pairs={{0,8},{4,12},{8,0},{12,4},{16,24},{20,28},{24,16},{28,20},{1,9},{5... | collective-permute-start | bytes 3145736 | tf_op jit(solution)/shard_map/ppermute | solution.py:223
  139.6 25.7 %collective-permute-start.21 = (bf16[256,2048]{1,0:T(8,128)(2,1)S(1)}, bf16[256,2048]{1,0:T(8,128)(2,1)S(1)}, u32[]{:S(2)}, u32[]{:S(2)}) collective-permute-start(bf16[256,2048]{1,0:T(8,128)(2,1)S(1)} %get-tuple-element.269), channel_id=1, source_target_pairs={{0,16},{4,20},{8,24},{12,28},{16,0},{20,4},{24,8},{28,12},{1,17},{... | collective-permute-start | bytes 3145736 | tf_op jit(solution)/shard_map/ppermute | solution.py:223
  163.1 33.0 %collective-permute-start.28 = (bf16[8,2,64,704]{3,2,1,0:T(8,128)(2,1)S(1)}, bf16[8,2,64,704]{3,2,1,0:T(8,128)(2,1)S(1)}, u32[]{:S(2)}, u32[]{:S(2)}) collective-permute-start(bf16[8,2,64,704]{3,2,1,0:T(8,128)(2,1)S(1)} %get-tuple-element.279.refs_3_), channel_id=1, source_target_pairs={{2,3},{6,7},{10,11},{14,15},{18,19},{22,23},{26,27},{30,31}} | collective-permute-start | bytes 4325384 | tf_op jit(solution)/shard_map/ppermute | solution.py:106
  163.8 33.6 %collective-permute-start.29 = (bf16[8,2,64,704]{3,2,1,0:T(8,128)(2,1)S(1)}, bf16[8,2,64,704]{3,2,1,0:T(8,128)(2,1)S(1)}, u32[]{:S(2)}, u32[]{:S(2)}) collective-permute-start(bf16[8,2,64,704]{3,2,1,0:T(8,128)(2,1)S(1)} %get-tuple-element.280.refs_6_), channel_id=1, source_target_pairs={{1,0},{5,4},{9,8},{13,12},{17,16},{21,20},{25,24},{29,28}} | collective-permute-start | bytes 4325384 | tf_op jit(solution)/shard_map/ppermute | solution.py:106
  171.1 22.4 %collective-permute-start.25 = (bf16[256,2048]{1,0:T(8,128)(2,1)S(1)}, bf16[256,2048]{1,0:T(8,128)(2,1)S(1)}, u32[]{:S(2)}, u32[]{:S(2)}) collective-permute-start(bf16[256,2048]{1,0:T(8,128)(2,1)S(1)} %get-tuple-element.274.refs_0_.refs_1_), channel_id=1, source_target_pairs={{0,16},{4,20},{8,24},{12,28},{16,0},{20,4},{24,8},{28,12},{1,17},{... | collective-permute-start | bytes 3145736 | tf_op jit(solution)/shard_map/ppermute | solution.py:223
  173.1 22.6 %collective-permute-start.24 = (bf16[256,2048]{1,0:T(8,128)(2,1)S(1)}, bf16[256,2048]{1,0:T(8,128)(2,1)S(1)}, u32[]{:S(2)}, u32[]{:S(2)}) collective-permute-start(bf16[256,2048]{1,0:T(8,128)(2,1)S(1)} %get-tuple-element.274.refs_0_.refs_1_), channel_id=1, source_target_pairs={{0,8},{4,12},{8,0},{12,4},{16,24},{20,28},{24,16},{28,20},{1,9},{5... | collective-permute-start | bytes 3145736 | tf_op jit(solution)/shard_map/ppermute | solution.py:223
  175.8 49.6 %collective-permute-start.31 = (bf16[1024,2048]{1,0:T(8,128)(2,1)}, bf16[1024,2048]{1,0:T(8,128)(2,1)}, u32[]{:S(2)}, u32[]{:S(2)}) collective-permute-start(bf16[1024,2048]{1,0:T(8,128)(2,1)} %get-tuple-element.287.refs_1_.refs_2_), channel_id=1, source_target_pairs={{0,4},{4,0},{8,12},{12,8},{16,20},{20,16},{24,28},{28,24},{1,5},{5... | collective-permute-start | bytes 12582920 | tf_op jit(solution)/shard_map/ppermute | solution.py:223
  208.0 17.4 %collective-permute-start.30 = (bf16[1024,2048]{1,0:T(8,128)(2,1)}, bf16[1024,2048]{1,0:T(8,128)(2,1)}, u32[]{:S(2)}, u32[]{:S(2)}) collective-permute-start(bf16[1024,2048]{1,0:T(8,128)(2,1)} %get-tuple-element.286.refs_0_.refs_2_), channel_id=1, source_target_pairs={{0,4},{4,0},{8,12},{12,8},{16,20},{20,16},{24,28},{28,24},{1,5},{5... | collective-permute-start | bytes 12582920 | tf_op jit(solution)/shard_map/ppermute | solution.py:223
  255.2 44.7 %collective-permute-start.35 = (bf16[352,2048]{1,0:T(8,128)(2,1)}, bf16[352,2048]{1,0:T(8,128)(2,1)}, u32[]{:S(2)}, u32[]{:S(2)}) collective-permute-start(bf16[352,2048]{1,0:T(8,128)(2,1)} %copy-done.27), channel_id=1, source_target_pairs={{0,1},{3,2},{4,5},{7,6},{8,9},{11,10},{12,13},{15,14},{16,17},{19,... | collective-permute-start | bytes 4325384 | tf_op jit(solution)/shard_map/ppermute | solution.py:106
  297.5 27.4 %collective-permute-start.33 = (bf16[256,2048]{1,0:T(8,128)(2,1)}, bf16[256,2048]{1,0:T(8,128)(2,1)S(1)}, u32[]{:S(2)}, u32[]{:S(2)}) collective-permute-start(bf16[256,2048]{1,0:T(8,128)(2,1)} %get-tuple-element.310), channel_id=1, source_target_pairs={{0,16},{4,20},{8,24},{12,28},{16,0},{20,4},{24,8},{28,12},{1,17},{... | collective-permute-start | bytes 3145736 | tf_op jit(solution)/shard_map/ppermute | solution.py:223
  299.3 25.6 %collective-permute-start.34 = (bf16[256,2048]{1,0:T(8,128)(2,1)}, bf16[256,2048]{1,0:T(8,128)(2,1)S(1)}, u32[]{:S(2)}, u32[]{:S(2)}) collective-permute-start(bf16[256,2048]{1,0:T(8,128)(2,1)} %get-tuple-element.311), channel_id=1, source_target_pairs={{0,8},{4,12},{8,0},{12,4},{16,24},{20,28},{24,16},{28,20},{1,9},{5... | collective-permute-start | bytes 3145736 | tf_op jit(solution)/shard_map/ppermute | solution.py:223
  303.4 28.6 %collective-permute-start.38 = (bf16[352,2048]{1,0:T(8,128)(2,1)}, bf16[352,2048]{1,0:T(8,128)(2,1)}, u32[]{:S(2)}, u32[]{:S(2)}) collective-permute-start(bf16[352,2048]{1,0:T(8,128)(2,1)} %get-tuple-element.325.refs_2_), channel_id=1, source_target_pairs={{1,2},{2,1},{5,6},{6,5},{9,10},{10,9},{13,14},{14,13},{17,18},{18,... | collective-permute-start | bytes 4325384 | tf_op jit(solution)/shard_map/ppermute | solution.py:106
  305.1 32.6 %collective-permute-start.39 = (bf16[352,2048]{1,0:T(8,128)(2,1)}, bf16[352,2048]{1,0:T(8,128)(2,1)}, u32[]{:S(2)}, u32[]{:S(2)}) collective-permute-start(bf16[352,2048]{1,0:T(8,128)(2,1)} %get-tuple-element.326.refs_4_), channel_id=1, source_target_pairs={{0,1},{3,2},{4,5},{7,6},{8,9},{11,10},{12,13},{15,14},{16,17},{19,... | collective-permute-start | bytes 4325384 | tf_op jit(solution)/shard_map/ppermute | solution.py:106
  330.3 16.7 %collective-permute-start.36 = (bf16[128,2048]{1,0:T(8,128)(2,1)}, bf16[128,2048]{1,0:T(8,128)(2,1)S(1)}, u32[]{:S(2)}, u32[]{:S(2)}) collective-permute-start(bf16[128,2048]{1,0:T(8,128)(2,1)} %get-tuple-element.320), channel_id=1, source_target_pairs={{0,8},{4,12},{8,0},{12,4},{16,24},{20,28},{24,16},{28,20},{1,9},{5... | collective-permute-start | bytes 1572872 | tf_op jit(solution)/shard_map/ppermute | solution.py:223
  342.5 40.9 %collective-permute-start.45 = (bf16[352,2048]{1,0:T(8,128)(2,1)}, bf16[352,2048]{1,0:T(8,128)(2,1)}, u32[]{:S(2)}, u32[]{:S(2)}) collective-permute-start(bf16[352,2048]{1,0:T(8,128)(2,1)} %get-tuple-element.338.refs_2_), channel_id=1, source_target_pairs={{1,0},{2,3},{0,1},{3,2},{5,4},{6,7},{4,5},{7,6},{9,8},{10,11},{8,9... | collective-permute-start | bytes 4325384 | tf_op jit(solution)/shard_map/ppermute | solution.py:106
  345.0 38.4 %collective-permute-start.46 = (bf16[352,2048]{1,0:T(8,128)(2,1)}, bf16[352,2048]{1,0:T(8,128)(2,1)}, u32[]{:S(2)}, u32[]{:S(2)}) collective-permute-start(bf16[352,2048]{1,0:T(8,128)(2,1)} %get-tuple-element.340.refs_2_), channel_id=1, source_target_pairs={{1,2},{2,1},{5,6},{6,5},{9,10},{10,9},{13,14},{14,13},{17,18},{18,... | collective-permute-start | bytes 4325384 | tf_op jit(solution)/shard_map/ppermute | solution.py:106
  355.2 24.2 %collective-permute-start.42 = (bf16[256,2048]{1,0:T(8,128)(2,1)}, bf16[256,2048]{1,0:T(8,128)(2,1)S(1)}, u32[]{:S(2)}, u32[]{:S(2)}) collective-permute-start(bf16[256,2048]{1,0:T(8,128)(2,1)} %get-tuple-element.334.refs_0_.refs_1_), channel_id=1, source_target_pairs={{0,16},{4,20},{8,24},{12,28},{16,0},{20,4},{24,8},{28,12},{1,17},{... | collective-permute-start | bytes 3145736 | tf_op jit(solution)/shard_map/ppermute | solution.py:223
  355.4 23.9 %collective-permute-start.41 = (bf16[256,2048]{1,0:T(8,128)(2,1)}, bf16[256,2048]{1,0:T(8,128)(2,1)S(1)}, u32[]{:S(2)}, u32[]{:S(2)}) collective-permute-start(bf16[256,2048]{1,0:T(8,128)(2,1)} %get-tuple-element.334.refs_0_.refs_1_), channel_id=1, source_target_pairs={{0,8},{4,12},{8,0},{12,4},{16,24},{20,28},{24,16},{28,20},{1,9},{5... | collective-permute-start | bytes 3145736 | tf_op jit(solution)/shard_map/ppermute | solution.py:223
  370.8 67.1 %collective-permute-start.40 = (bf16[1024,2048]{1,0:T(8,128)(2,1)}, bf16[1024,2048]{1,0:T(8,128)(2,1)}, u32[]{:S(2)}, u32[]{:S(2)}) collective-permute-start(bf16[1024,2048]{1,0:T(8,128)(2,1)} %get-tuple-element.333), channel_id=1, source_target_pairs={{0,4},{4,0},{8,12},{12,8},{16,20},{20,16},{24,28},{28,24},{1,5},{5... | collective-permute-start | bytes 12582920 | tf_op jit(solution)/shard_map/ppermute | solution.py:223
  387.9 39.3 %collective-permute-start.49 = (bf16[352,2048]{1,0:T(8,128)(2,1)}, bf16[352,2048]{1,0:T(8,128)(2,1)}, u32[]{:S(2)}, u32[]{:S(2)}) collective-permute-start(bf16[352,2048]{1,0:T(8,128)(2,1)} %get-tuple-element.353.refs_2_), channel_id=1, source_target_pairs={{1,0},{2,3},{0,1},{3,2},{5,4},{6,7},{4,5},{7,6},{9,8},{10,11},{8,9... | collective-permute-start | bytes 4325384 | tf_op jit(solution)/shard_map/ppermute | solution.py:106
  388.3 38.9 %collective-permute-start.50 = (bf16[352,2048]{1,0:T(8,128)(2,1)}, bf16[352,2048]{1,0:T(8,128)(2,1)}, u32[]{:S(2)}, u32[]{:S(2)}) collective-permute-start(bf16[352,2048]{1,0:T(8,128)(2,1)} %get-tuple-element.355.refs_2_), channel_id=1, source_target_pairs={{1,2},{2,1},{5,6},{6,5},{9,10},{10,9},{13,14},{14,13},{17,18},{18,... | collective-permute-start | bytes 4325384 | tf_op jit(solution)/shard_map/ppermute | solution.py:106
  431.7 33.7 %collective-permute-start.53 = (bf16[352,2048]{1,0:T(8,128)(2,1)}, bf16[352,2048]{1,0:T(8,128)(2,1)S(1)}, u32[]{:S(2)}, u32[]{:S(2)}) collective-permute-start(bf16[352,2048]{1,0:T(8,128)(2,1)} %get-tuple-element.361.refs_2_), channel_id=1, source_target_pairs={{1,0},{2,3},{0,1},{3,2},{5,4},{6,7},{4,5},{7,6},{9,8},{10,11},{8,9... | collective-permute-start | bytes 4325384 | tf_op jit(solution)/shard_map/ppermute | solution.py:106
  433.2 32.2 %collective-permute-start.54 = (bf16[352,2048]{1,0:T(8,128)(2,1)}, bf16[352,2048]{1,0:T(8,128)(2,1)}, u32[]{:S(2)}, u32[]{:S(2)}) collective-permute-start(bf16[352,2048]{1,0:T(8,128)(2,1)} %get-tuple-element.366.refs_2_), channel_id=1, source_target_pairs={{1,2},{2,1},{5,6},{6,5},{9,10},{10,9},{13,14},{14,13},{17,18},{18,... | collective-permute-start | bytes 4325384 | tf_op jit(solution)/shard_map/ppermute | solution.py:106
  445.6 47.5 %collective-permute-start.51 = (bf16[512,2048]{1,0:T(8,128)(2,1)}, bf16[512,2048]{1,0:T(8,128)(2,1)S(1)}, u32[]{:S(2)}, u32[]{:S(2)}) collective-permute-start(bf16[512,2048]{1,0:T(8,128)(2,1)} %get-tuple-element.359), channel_id=1, source_target_pairs={{0,16},{4,20},{8,24},{12,28},{16,0},{20,4},{24,8},{28,12},{1,17},{... | collective-permute-start | bytes 6291464 | tf_op jit(solution)/shard_map/ppermute | solution.py:223
  445.9 47.3 %collective-permute-start.52 = (bf16[512,2048]{1,0:T(8,128)(2,1)}, bf16[512,2048]{1,0:T(8,128)(2,1)}, u32[]{:S(2)}, u32[]{:S(2)}) collective-permute-start(bf16[512,2048]{1,0:T(8,128)(2,1)} %get-tuple-element.360), channel_id=1, source_target_pairs={{0,8},{4,12},{8,0},{12,4},{16,24},{20,28},{24,16},{28,20},{1,9},{5... | collective-permute-start | bytes 6291464 | tf_op jit(solution)/shard_map/ppermute | solution.py:223
  471.0 33.5 %collective-permute-start.57 = (bf16[352,2048]{1,0:T(8,128)(2,1)}, bf16[352,2048]{1,0:T(8,128)(2,1)S(1)}, u32[]{:S(2)}, u32[]{:S(2)}) collective-permute-start(bf16[352,2048]{1,0:T(8,128)(2,1)} %get-tuple-element.377.refs_2_), channel_id=1, source_target_pairs={{1,0},{2,3},{0,1},{3,2},{5,4},{6,7},{4,5},{7,6},{9,8},{10,11},{8,9... | collective-permute-start | bytes 4325384 | tf_op jit(solution)/shard_map/ppermute | solution.py:106
  473.7 30.8 %collective-permute-start.58 = (bf16[352,2048]{1,0:T(8,128)(2,1)}, bf16[352,2048]{1,0:T(8,128)(2,1)}, u32[]{:S(2)}, u32[]{:S(2)}) collective-permute-start(bf16[352,2048]{1,0:T(8,128)(2,1)} %get-tuple-element.379.refs_2_), channel_id=1, source_target_pairs={{1,2},{2,1},{5,6},{6,5},{9,10},{10,9},{13,14},{14,13},{17,18},{18,... | collective-permute-start | bytes 4325384 | tf_op jit(solution)/shard_map/ppermute | solution.py:106
  499.5 24.3 %collective-permute-start.55 = (bf16[256,2048]{1,0:T(8,128)(2,1)}, bf16[256,2048]{1,0:T(8,128)(2,1)}, u32[]{:S(2)}, u32[]{:S(2)}) collective-permute-start(bf16[256,2048]{1,0:T(8,128)(2,1)} %get-tuple-element.374), channel_id=1, source_target_pairs={{0,8},{4,12},{8,0},{12,4},{16,24},{20,28},{24,16},{28,20},{1,9},{5... | collective-permute-start | bytes 3145736 | tf_op jit(solution)/shard_map/ppermute | solution.py:223
  500.1 24.0 %collective-permute-start.56 = (bf16[256,2048]{1,0:T(8,128)(2,1)}, bf16[256,2048]{1,0:T(8,128)(2,1)}, u32[]{:S(2)}, u32[]{:S(2)}) collective-permute-start(bf16[256,2048]{1,0:T(8,128)(2,1)} %get-tuple-element.375), channel_id=1, source_target_pairs={{0,16},{4,20},{8,24},{12,28},{16,0},{20,4},{24,8},{28,12},{1,17},{... | collective-permute-start | bytes 3145736 | tf_op jit(solution)/shard_map/ppermute | solution.py:223
  510.1 27.6 %collective-permute-start.59 = (bf16[352,2048]{1,0:T(8,128)(2,1)}, bf16[352,2048]{1,0:T(8,128)(2,1)}, u32[]{:S(2)}, u32[]{:S(2)}) collective-permute-start(bf16[352,2048]{1,0:T(8,128)(2,1)} %get-tuple-element.387.refs_2_), channel_id=1, source_target_pairs={{1,2},{2,1},{5,6},{6,5},{9,10},{10,9},{13,14},{14,13},{17,18},{18,... | collective-permute-start | bytes 4325384 | tf_op jit(solution)/shard_map/ppermute | solution.py:106
  511.9 35.0 %collective-permute-start.60 = (bf16[352,2048]{1,0:T(8,128)(2,1)}, bf16[352,2048]{1,0:T(8,128)(2,1)}, u32[]{:S(2)}, u32[]{:S(2)}) collective-permute-start(bf16[352,2048]{1,0:T(8,128)(2,1)} %get-tuple-element.388.refs_2_), channel_id=1, source_target_pairs={{1,0},{2,3},{0,1},{3,2},{5,4},{6,7},{4,5},{7,6},{9,8},{10,11},{8,9... | collective-permute-start | bytes 4325384 | tf_op jit(solution)/shard_map/ppermute | solution.py:106
  537.7 19.9 %collective-permute-start.63 = (bf16[4,704,256]{2,1,0:T(8,128)(2,1)}, bf16[4,704,256]{2,1,0:T(8,128)(2,1)S(1)}, u32[]{:S(2)}, u32[]{:S(2)}) collective-permute-start(bf16[4,704,256]{2,1,0:T(8,128)(2,1)} %get-tuple-element.400), channel_id=1, source_target_pairs={{0,4},{4,0},{8,12},{12,8},{16,20},{20,16},{24,28},{28,24},{1,5},{5... | collective-permute-start | bytes 4325384 | tf_op jit(solution)/shard_map/ppermute | solution.py:223
  551.4 31.2 %collective-permute-start.61 = (bf16[352,2048]{1,0:T(8,128)(2,1)}, bf16[352,2048]{1,0:T(8,128)(2,1)}, u32[]{:S(2)}, u32[]{:S(2)}) collective-permute-start(bf16[352,2048]{1,0:T(8,128)(2,1)} %get-tuple-element.393.refs_2_), channel_id=1, source_target_pairs={{1,0},{2,3},{0,1},{3,2},{5,4},{6,7},{4,5},{7,6},{9,8},{10,11},{8,9... | collective-permute-start | bytes 4325384 | tf_op jit(solution)/shard_map/ppermute | solution.py:106
  553.1 29.4 %collective-permute-start.62 = (bf16[352,2048]{1,0:T(8,128)(2,1)}, bf16[352,2048]{1,0:T(8,128)(2,1)}, u32[]{:S(2)}, u32[]{:S(2)}) collective-permute-start(bf16[352,2048]{1,0:T(8,128)(2,1)} %get-tuple-element.394.refs_1_), channel_id=1, source_target_pairs={{1,2},{2,1},{5,6},{6,5},{9,10},{10,9},{13,14},{14,13},{17,18},{18,... | collective-permute-start | bytes 4325384 | tf_op jit(solution)/shard_map/ppermute | solution.py:106
  559.4 29.0 %collective-permute-start.66 = (bf16[2,704,256]{2,1,0:T(8,128)(2,1)}, bf16[2,704,256]{2,1,0:T(8,128)(2,1)S(1)}, u32[]{:S(2)}, u32[]{:S(2)}) collective-permute-start(bf16[2,704,256]{2,1,0:T(8,128)(2,1)} %get-tuple-element.409), channel_id=1, source_target_pairs={{0,8},{4,12},{8,0},{12,4},{16,24},{20,28},{24,16},{28,20},{1,9},{5... | collective-permute-start | bytes 2162696 | tf_op jit(solution)/shard_map/ppermute | solution.py:223
  560.1 32.7 %collective-permute-start.67 = (bf16[2,704,256]{2,1,0:T(8,128)(2,1)}, bf16[2,704,256]{2,1,0:T(8,128)(2,1)}, u32[]{:S(2)}, u32[]{:S(2)}) collective-permute-start(bf16[2,704,256]{2,1,0:T(8,128)(2,1)} %get-tuple-element.410), channel_id=1, source_target_pairs={{0,16},{4,20},{8,24},{12,28},{16,0},{20,4},{24,8},{28,12},{1,17},{... | collective-permute-start | bytes 2162696 | tf_op jit(solution)/shard_map/ppermute | solution.py:223
  560.4 32.4 %collective-permute-start.68 = (bf16[2,704,256]{2,1,0:T(8,128)(2,1)}, bf16[2,704,256]{2,1,0:T(8,128)(2,1)}, u32[]{:S(2)}, u32[]{:S(2)}) collective-permute-start(bf16[2,704,256]{2,1,0:T(8,128)(2,1)} %get-tuple-element.411), channel_id=1, source_target_pairs={{0,24},{4,28},{8,16},{12,20},{16,8},{20,12},{24,0},{28,4},{1,25},{... | collective-permute-start | bytes 2162696 | tf_op jit(solution)/shard_map/ppermute | solution.py:223
  586.6 23.4 %collective-permute-start.65 = (bf16[352,2048]{1,0:T(8,128)(2,1)}, bf16[352,2048]{1,0:T(8,128)(2,1)}, u32[]{:S(2)}, u32[]{:S(2)}) collective-permute-start(bf16[352,2048]{1,0:T(8,128)(2,1)} %get-tuple-element.408.refs_1_), channel_id=1, source_target_pairs={{1,2},{2,1},{5,6},{6,5},{9,10},{10,9},{13,14},{14,13},{17,18},{18,... | collective-permute-start | bytes 4325384 | tf_op jit(solution)/shard_map/ppermute | solution.py:106
  588.4 36.2 %collective-permute-start.64 = (bf16[352,2048]{1,0:T(8,128)(2,1)}, bf16[352,2048]{1,0:T(8,128)(2,1)}, u32[]{:S(2)}, u32[]{:S(2)}) collective-permute-start(bf16[352,2048]{1,0:T(8,128)(2,1)} %get-tuple-element.407.refs_2_), channel_id=1, source_target_pairs={{1,0},{2,3},{5,4},{6,7},{9,8},{10,11},{13,12},{14,15},{17,16},{18,... | collective-permute-start | bytes 4325384 | tf_op jit(solution)/shard_map/ppermute | solution.py:106
  600.1 31.7 %collective-permute-start.71 = (bf16[2,704,256]{2,1,0:T(8,128)(2,1)}, bf16[2,704,256]{2,1,0:T(8,128)(2,1)}, u32[]{:S(2)}, u32[]{:S(2)}) collective-permute-start(bf16[2,704,256]{2,1,0:T(8,128)(2,1)} %get-tuple-element.424), channel_id=1, source_target_pairs={{0,8},{4,12},{8,0},{12,4},{16,24},{20,28},{24,16},{28,20},{1,9},{5... | collective-permute-start | bytes 2162696 | tf_op jit(solution)/shard_map/ppermute | solution.py:223
  600.7 34.0 %collective-permute-start.72 = (bf16[2,704,256]{2,1,0:T(8,128)(2,1)}, bf16[2,704,256]{2,1,0:T(8,128)(2,1)}, u32[]{:S(2)}, u32[]{:S(2)}) collective-permute-start(bf16[2,704,256]{2,1,0:T(8,128)(2,1)} %get-tuple-element.425), channel_id=1, source_target_pairs={{0,16},{4,20},{8,24},{12,28},{16,0},{20,4},{24,8},{28,12},{1,17},{... | collective-permute-start | bytes 2162696 | tf_op jit(solution)/shard_map/ppermute | solution.py:223
  601.0 33.7 %collective-permute-start.73 = (bf16[2,704,256]{2,1,0:T(8,128)(2,1)}, bf16[2,704,256]{2,1,0:T(8,128)(2,1)}, u32[]{:S(2)}, u32[]{:S(2)}) collective-permute-start(bf16[2,704,256]{2,1,0:T(8,128)(2,1)} %get-tuple-element.426), channel_id=1, source_target_pairs={{0,24},{4,28},{8,16},{12,20},{16,8},{20,12},{24,0},{28,4},{1,25},{... | collective-permute-start | bytes 2162696 | tf_op jit(solution)/shard_map/ppermute | solution.py:223
  630.4 38.9 %collective-permute-start.77 = (bf16[352,2048]{1,0:T(8,128)(2,1)}, bf16[352,2048]{1,0:T(8,128)(2,1)}, u32[]{:S(2)}, u32[]{:S(2)}) collective-permute-start(bf16[352,2048]{1,0:T(8,128)(2,1)} %get-tuple-element.447.refs_2_), channel_id=1, source_target_pairs={{1,0},{2,3},{5,4},{6,7},{9,8},{10,11},{13,12},{14,15},{17,16},{18,... | collective-permute-start | bytes 4325384 | tf_op jit(solution)/shard_map/ppermute | solution.py:106
  640.4 18.6 %collective-permute-start.75 = (bf16[2,384,256]{2,1,0:T(8,128)(2,1)S(1)}, bf16[2,384,256]{2,1,0:T(8,128)(2,1)S(1)}, u32[]{:S(2)}, u32[]{:S(2)}) collective-permute-start(bf16[2,384,256]{2,1,0:T(8,128)(2,1)S(1)} %get-tuple-element.430), channel_id=1, source_target_pairs={{0,16},{4,20},{8,24},{12,28},{16,0},{20,4},{24,8},{28,12},{1,17},{... | collective-permute-start | bytes 1179656 | tf_op jit(solution)/shard_map/ppermute | solution.py:223
  640.8 18.2 %collective-permute-start.76 = (bf16[2,384,256]{2,1,0:T(8,128)(2,1)S(1)}, bf16[2,384,256]{2,1,0:T(8,128)(2,1)S(1)}, u32[]{:S(2)}, u32[]{:S(2)}) collective-permute-start(bf16[2,384,256]{2,1,0:T(8,128)(2,1)S(1)} %get-tuple-element.431), channel_id=1, source_target_pairs={{0,24},{4,28},{8,16},{12,20},{16,8},{20,12},{24,0},{28,4},{1,25},{... | collective-permute-start | bytes 1179656 | tf_op jit(solution)/shard_map/ppermute | solution.py:223
  (83 other events, 441.5 us)
